TPU v7x, 256 devices: a whole 4x4x8 slice. The times are simulated.
256 devices in a mesh: tile: 32 (over y, z_hi, core), lev: 8 (over z_lo, x).
Axes of the slice: x: 4, y: 4, z: 8 (z_hi: 4, z_lo: 2; z = z_hi * 2 + z_lo), core: 2. Of those that a mesh axis runs over, the one named last changes fastest.
Arguments:
- state_in: float32 [128, 8192, 128], P('lev', 'tile'), may hold values from -6 to 6
- east_speed: bfloat16 [128, 8192, 128], P('lev', 'tile'), may hold values from -0.19921875 to 0.19921875
- north_speed: bfloat16 [128, 8192, 128], P('lev', 'tile'), may hold values from -0.19921875 to 0.19921875
- w_in: bfloat16 [128, 1024], replicated, may hold values from -0.5 to 0.5
- w_out: bfloat16 [128, 1024], replicated, may hold values from -0.1875 to 0.1875
- cotangent: float32 [128, 8192, 128], P('lev', 'tile'), may hold values from -6 to 6
Outputs:
- state_out: float32 [128, 8192, 128], P('lev', 'tile')
- state_grad: float32 [128, 8192, 128], P('lev', 'tile')
- w_in_grad: float32 [128, 1024], replicated
- w_out_grad: float32 [128, 1024], replicated
All inputs are finite; a program needn't handle non-finite values.
Results may differ from a plain program's by a relative error of at most 0.0053.
Values may be sent and summed in bfloat16 or wider, within the bound.
No kernel may reach another device: no remote copies, remote signals or barrier semaphores. Data moves between devices by JAX's collectives and lax.ppermute only.
A program may use at most 128 MiB of HBM per device.

v0:
```python
import math

import jax
import jax.numpy as jnp
from jax import lax
from jax.sharding import PartitionSpec as P

KAPPA = 0.05
SLOPE_C = 0.7978845608028654
CUBIC = 0.044715


def padded_2(block, sides, width):
    for axis, dim in sides:
        count = lax.axis_size(axis)
        forward = [(i, i + 1) for i in range(count - 1)]
        forward.append((count - 1, 0))
        backward = [(target, source) for source, target in forward]
        low = lax.ppermute(
            lax.slice_in_dim(block, block.shape[dim] - width, None, axis=dim), axis, forward
        )
        high = lax.ppermute(lax.slice_in_dim(block, 0, width, axis=dim), axis, backward)
        block = jnp.concatenate([low, block, high], axis=dim)
    return block


def from_behind(block, axis, distance):
    devices = range(lax.axis_size(axis))
    route = [((i - distance) % len(devices), i) for i in devices]
    return lax.ppermute(block, axis, route)


def gelu_slope(preact):
    tangent = jnp.tanh(SLOPE_C * (preact + CUBIC * preact * preact * preact))
    value = 0.5 * preact * (1.0 + tangent)
    slope = 0.5 * (1.0 + tangent) + 0.5 * preact * (1.0 - tangent * tangent) * SLOPE_C * (
        1.0 + 3.0 * CUBIC * preact * preact
    )
    return (value, slope)


def shift_up(values):
    return jnp.concatenate([values[:, :, 1:], jnp.zeros_like(values[:, :, :1])], 2)


def shift_down(values):
    return jnp.concatenate([jnp.zeros_like(values[:, :, :1]), values[:, :, :-1]], 2)


def widened(quantity):
    padded = padded_2(quantity, (("tile", 1),), 1)
    return (padded[:, 2:, :], padded[:, :-2, :])


def advance_with(quantity, beyond, behind, speeds):
    pos_east, neg_east, pos_west, neg_west, pos_north, neg_north, neg_south = speeds
    east_flux = pos_east * quantity + neg_east * beyond
    west_flux = pos_west * behind + neg_west * quantity
    north_flux = pos_north * quantity + neg_north * shift_up(quantity)
    south_flux = shift_down(north_flux)
    return (
        quantity
        - (east_flux - west_flux)
        - (north_flux - south_flux)
        + KAPPA * (beyond - 2.0 * quantity + behind)
    )


def transpose_with(grad, beyond, behind, speeds):
    pos_east, neg_east, pos_west, neg_west, pos_north, neg_north, neg_south = speeds
    along = pos_east * (beyond - grad) + neg_west * (grad - behind)
    across = pos_north * (shift_up(grad) - grad) + neg_south * (grad - shift_down(grad))
    return grad + along + across + KAPPA * (beyond - 2.0 * grad + behind)


def advance(quantity, speeds):
    beyond, behind = widened(quantity)
    return advance_with(quantity, beyond, behind, speeds)


def transpose_step(grad, speeds):
    beyond, behind = widened(grad)
    return transpose_with(grad, beyond, behind, speeds)


def to_columns(values):
    return lax.all_to_all(values, "lev", split_axis=1, concat_axis=0, tiled=True)


def to_levels(values):
    return lax.all_to_all(values, "lev", split_axis=0, concat_axis=1, tiled=True)


def network_forward(col_in, w_in, w_out):
    pre = jnp.einsum("lxy,lh->xyh", col_in, w_in, preferred_element_type=jnp.float32)
    act, slope = gelu_slope(pre)
    act_b = act.astype(jnp.bfloat16)
    tend = jnp.einsum("xyh,lh->lxy", act_b, w_out, preferred_element_type=jnp.float32).astype(
        jnp.bfloat16
    )
    return (act_b, slope, tend)


def network_backward(col_in, col_grad, act_b, slope, w_in, w_out):
    out_grad = jnp.einsum("lxy,xyh->lh", col_grad, act_b, preferred_element_type=jnp.float32)
    d_act = jnp.einsum("lxy,lh->xyh", col_grad, w_out, preferred_element_type=jnp.float32)
    d_pre = (d_act * slope).astype(jnp.bfloat16)
    in_grad = jnp.einsum("lxy,xyh->lh", col_in, d_pre, preferred_element_type=jnp.float32)
    d_cols = jnp.einsum("xyh,lh->lxy", d_pre, w_in, preferred_element_type=jnp.float32).astype(
        jnp.bfloat16
    )
    return (in_grad, out_grad, d_cols)


def shards(state_in, east_speed, north_speed, w_in, w_out, cotangent):
    edge_speed = from_behind(east_speed[:, -1:, :], "tile", 1)
    east = east_speed.astype(jnp.float32)
    west = jnp.concatenate([edge_speed, east_speed[:, :-1, :]], 1).astype(jnp.float32)
    north = north_speed.astype(jnp.float32)
    width = north.shape[2]
    wall = (jnp.arange(width) < width - 1).astype(jnp.float32)
    pos_north = jnp.maximum(north, 0.0) * wall
    neg_north = jnp.minimum(north, 0.0) * wall
    speeds = (
        jnp.maximum(east, 0.0),
        jnp.minimum(east, 0.0),
        jnp.maximum(west, 0.0),
        jnp.minimum(west, 0.0),
        pos_north,
        neg_north,
        shift_down(neg_north),
    )
    first = advance(state_in, speeds)
    col_in = to_columns(first.astype(jnp.bfloat16))
    act_b, slope, tend = network_forward(col_in, w_in, w_out)
    second = first + to_levels(tend).astype(jnp.float32)
    state_out = advance(second, speeds)
    back_two = transpose_step(cotangent, speeds)
    col_grad = to_columns(back_two.astype(jnp.bfloat16))
    in_grad, out_grad, d_cols = network_backward(col_in, col_grad, act_b, slope, w_in, w_out)
    back_one = back_two + to_levels(d_cols).astype(jnp.float32)
    state_grad = transpose_step(back_one, speeds)
    in_total, out_total = lax.psum((in_grad, out_grad), ("tile", "lev"))
    scale = 1.0 / math.sqrt(lax.axis_size("tile") * state_in.shape[1] * state_in.shape[2])
    return (state_out, state_grad, in_total * scale, out_total * scale)


def solution(mesh):
    in_specs = (
        P("lev", "tile", None),
        P("lev", "tile", None),
        P("lev", "tile", None),
        P(),
        P(),
        P("lev", "tile", None),
    )
    out_specs = (P("lev", "tile", None), P("lev", "tile", None), P(), P())
    return jax.shard_map(shards, mesh=mesh, in_specs=in_specs, out_specs=out_specs, check_vma=False)
```

profile of v0, /device:TPU:2, one launch (start us, length us, event | category | flops | bytes accessed | tf_op | source)
XLA Modules:
  0.0 422.1 jit_solution(6065733611778772545)
XLA Ops:
  7.2 0.0 copy-start
  7.2 0.9 fusion.82
  8.1 8.3 %collective-permute-start.5 = (f32[16,1,128]{2,1,0:T(1,128)S(1)}, f32[16,1,128]{2,1,0:T(1,128)S(1)}, u32[]{:S(2)}, u32[]{:S(2)}) collective-permute-start(f32[16,1,128]{2,1,0:T(1,128)S(1)} %get-tuple-element.14), channel_id=1, source_target_pairs={{8,0},{16,8},{24,16},{32,24},{40,32},{48,40},{56,48},{64,56},{72,6... | collective-permute-start | bytes 24584 | tf_op jit(solution)/shard_map/ppermute | solution.py:22
  16.4 0.8 slice.91
  17.2 0.1 collective-permute-start.1
  17.3 0.0 copy-start.8
  17.3 3.0 fusion.83
  20.3 0.0 copy-start.4
  20.3 0.3 fusion.48
  20.6 1.3 copy-done.4
  21.9 0.6 slice.95
  22.5 2.0 collective-permute-done.1
  24.5 0.0 collective-permute-done.5
  24.6 0.0 copy-done.5
  24.6 4.6 %fusion.76 = (bf16[16,256,128]{2,1,0:T(8,128)(2,1)S(1)}, f32[16,256,128]{2,1,0:T(8,128)}, f32[16,256,128]{2,1,0:T(8,128)}) fusion(f32[16,256,128]{2,1,0:T(8,128)S(1)} %copy-done.5, f32[16,256,127]{2,1,0:T(8,128)S(1)} %get-tuple-element.17, f32[16,256,127]{2,1,0:T(8,128)S(1)} %bitcast.53, f32[16,256,127]{2,1,0:T(8,128)S(1)} %get-tuple-element.16, ...), kind=kLoop, calls=%fused_computation.105 | loop fusion | flops 18350080 | bytes 20922880 | tf_op jit(solution)/shard_map/convert_element_type | solution.py:139
  29.2 1.6 copy.38
  30.8 5.3 %all-to-all-start.2 = ((bf16[16,256,128]{2,0,1:T(8,128)(2,1)}), bf16[16,256,128]{2,0,1:T(8,128)(2,1)}, u32[]{:S(2)}, u32[]{:S(2)}) async-start(bf16[16,256,128]{2,0,1:T(8,128)(2,1)} %copy.38), calls=%async_computation.2 | async-start | bytes 2097152 | tf_op jit(solution)/shard_map/all_to_all | solution.py:87
  36.1 5.5 %collective-permute-start = (f32[16,1,128]{2,1,0:T(1,128)S(1)}, f32[16,1,128]{2,1,0:T(1,128)S(1)}, u32[]{:S(2)}, u32[]{:S(2)}) collective-permute-start(f32[16,1,128]{2,1,0:T(1,128)S(1)} %get-tuple-element.20), channel_id=1, source_target_pairs={{8,0},{16,8},{24,16},{32,24},{40,32},{48,40},{56,48},{64,56},{72,6... | collective-permute-start | bytes 24584 | tf_op jit(solution)/shard_map/ppermute | solution.py:22
  41.6 0.0 collective-permute-start.2
  41.6 1.4 collective-permute-done
  43.0 10.3 %collective-permute-done.2 = f32[16,1,128]{2,1,0:T(1,128)S(1)} collective-permute-done((f32[16,1,128]{2,1,0:T(1,128)S(1)}, f32[16,1,128]{2,1,0:T(1,128)S(1)}, u32[]{:S(2)}, u32[]{:S(2)}) %collective-permute-start.2) | collective-permute-done | bytes 8224 | tf_op jit(solution)/shard_map/ppermute | solution.py:19
  53.2 5.4 %fusion.78 = (bf16[16,256,128]{2,1,0:T(8,128)(2,1)S(1)}, f32[16,256,128]{2,1,0:T(8,128)}) fusion(f32[16,256,128]{2,1,0:T(8,128)S(1)} %copy-done.4, f32[16,256,128]{2,1,0:T(8,128)} %get-tuple-element.24, f32[16,256,127]{2,1,0:T(8,128)} %bitcast.52, f32[16,1,128]{2,1,0:T(1,128)S(1)} %collective-permute-done.2, bf16[16,255,128]{2,1,0:T(8,128)(2,1)S(1)} %bitcast.49, ...), kind=kLoop, calls=%fused_computation.106 | loop fusion | flops 14155776 | bytes 11534336 | tf_op jit(solution)/shard_map/convert_element_type | solution.py:134
  58.7 1.7 copy.32
  60.4 4.8 %all-to-all-start = ((bf16[16,256,128]{2,0,1:T(8,128)(2,1)}), bf16[16,256,128]{2,0,1:T(8,128)(2,1)S(1)}, u32[]{:S(2)}, u32[]{:S(2)}) async-start(bf16[16,256,128]{2,0,1:T(8,128)(2,1)} %copy.32), calls=%async_computation | async-start | bytes 2097152 | tf_op jit(solution)/shard_map/all_to_all | solution.py:87
  65.2 1.5 copy.40
  66.7 8.3 %all-to-all-done = bf16[16,256,128]{2,0,1:T(8,128)(2,1)S(1)} async-done(((bf16[16,256,128]{2,0,1:T(8,128)(2,1)}), bf16[16,256,128]{2,0,1:T(8,128)(2,1)S(1)}, u32[]{:S(2)}, u32[]{:S(2)}) %all-to-all-start) | async-done | bytes 1048608 | tf_op jit(solution)/shard_map/all_to_all | solution.py:87
  75.0 1.0 copy-done.14
  76.0 1.5 copy.34
  77.5 0.0 copy-start.15
  77.5 11.3 %multiply_convert_fusion = (bf16[32,128,1024]{2,1,0:T(8,128)(2,1)}, f32[32,128,1024]{2,1,0:T(8,128)}) fusion(bf16[128,1024]{1,0:T(8,128)(2,1)S(1)} %copy-done, bf16[128,32,128]{2,1,0:T(8,128)(2,1)S(1)} %bitcast.58), kind=kOutput, calls=%fused_computation.9 | convolution fusion | flops 1111490560 | bytes 26476544 | tf_op jit(solution)/shard_map/lxy,lh->xyh/dot_general | solution.py:95
  88.8 13.9 %fusion.6 = bf16[32,128,1024]{2,1,0:T(8,128)(2,1)S(1)} fusion(f32[32,128,1024]{2,1,0:T(8,128)} %get-tuple-element.26, bf16[128,32,128]{2,1,0:T(8,128)(2,1)S(1)} %bitcast.56, bf16[128,1024]{1,0:T(8,128)(2,1)S(1)} %copy-done.15), kind=kOutput, calls=%fused_computation.8 | convolution fusion | flops 1153433600 | bytes 26476544 | tf_op jit(solution)/shard_map/lxy,lh->xyh/dot_general | solution.py:106
  102.7 3.3 copy-done.3
  106.0 3.5 fusion.66
  109.5 2.7 copy.42
  112.1 5.3 %all-to-all-start.3 = ((bf16[128,32,128]{2,1,0:T(8,128)(2,1)}), bf16[128,32,128]{2,1,0:T(8,128)(2,1)}, u32[]{:S(2)}, u32[]{:S(2)}) async-start(bf16[128,32,128]{2,1,0:T(8,128)(2,1)} %copy.42), calls=%async_computation.3 | async-start | bytes 2097152 | tf_op jit(solution)/shard_map/all_to_all | solution.py:91
  117.4 5.7 %convolution_bitcast_fusion.1 = f32[128,1024]{1,0:T(8,128)} fusion(bf16[32,128,1024]{2,1,0:T(8,128)(2,1)} %copy-done.3, bf16[128,32,128]{2,1,0:T(8,128)(2,1)S(1)} %bitcast.59), kind=kOutput, calls=%fused_computation.91 | convolution fusion | flops 1073741824 | bytes 9961472 | tf_op jit(solution)/shard_map/lxy,xyh->lh/dot_general | solution.py:108
  123.1 5.7 %convolution_bitcast_fusion = f32[128,1024]{1,0:T(8,128)} fusion(bf16[32,128,1024]{2,1,0:T(8,128)(2,1)} %get-tuple-element.25, bf16[128,32,128]{2,1,0:T(8,128)(2,1)S(1)} %bitcast.57), kind=kOutput, calls=%fused_computation.90 | convolution fusion | flops 1073741824 | bytes 9961472 | tf_op jit(solution)/shard_map/lxy,xyh->lh/dot_general | solution.py:105
  128.8 0.0 all-reduce.12.cloned.1.call-update
  128.9 5.7 %fusion.65 = bf16[128,32,128]{0,2,1:T(8,128)(2,1)S(1)} fusion(bf16[32,128,1024]{2,1,0:T(8,128)(2,1)} %get-tuple-element.25, bf16[128,1024]{1,0:T(8,128)(2,1)S(1)} %copy-done.16), kind=kOutput, calls=%fused_computation.88 | convolution fusion | flops 1074266112 | bytes 9699328 | tf_op jit(solution)/shard_map/xyh,lh->lxy/dot_general | solution.py:98
  134.6 1.7 copy.36
  136.3 5.7 %all-to-all-start.1 = ((bf16[128,32,128]{2,1,0:T(8,128)(2,1)}), bf16[128,32,128]{2,1,0:T(8,128)(2,1)}, u32[]{:S(2)}, u32[]{:S(2)}) async-start(bf16[128,32,128]{2,1,0:T(8,128)(2,1)} %copy.36), calls=%async_computation.1 | async-start | bytes 2097152 | tf_op jit(solution)/shard_map/all_to_all | solution.py:91
  142.0 242.0 %all-reduce.12.cloned.1.call-done = (f32[128,1024]{1,0:T(8,128)}, f32[128,1024]{1,0:T(8,128)}) async-done(((f32[128,1024]{1,0:T(8,128)}, f32[128,1024]{1,0:T(8,128)}), (f32[128,1024]{1,0:T(8,128)}, f32[128,1024]{1,0:T(8,128)})) %all-reduce.12.cloned.1.call-update) | async-done | bytes 1048592 | tf_op jit(solution)/shard_map/psum | solution.py:143
  384.0 2.3 broadcast_multiply_fusion
  386.3 1.5 convert_bitcast_fusion
  387.8 0.0 copy-start.10
  387.8 0.2 copy.43
  388.0 1.4 copy-done.10
  389.4 0.3 bitcast_add_fusion
  389.7 2.1 collective-permute-start.7
  391.8 0.0 collective-permute-start.8
  391.9 2.8 fusion.80
  394.6 0.0 all-to-all-done.1
  394.6 1.5 convert_bitcast_fusion.1
  396.1 0.0 copy-start.11
  396.2 0.2 copy.37
  396.4 1.4 copy-done.11
  397.7 0.2 bitcast_add_fusion.1
  398.0 0.0 copy-start.9
  398.0 0.6 slice.119
  398.6 6.0 %collective-permute-start.3 = (f32[16,1,128]{2,1,0:T(1,128)S(1)}, f32[16,1,128]{2,1,0:T(1,128)S(1)}, u32[]{:S(2)}, u32[]{:S(2)}) collective-permute-start(f32[16,1,128]{2,1,0:T(1,128)S(1)} %get-tuple-element.18), channel_id=1, source_target_pairs={{8,0},{16,8},{24,16},{32,24},{40,32},{48,40},{56,48},{64,56},{72,6... | collective-permute-start | bytes 24584 | tf_op jit(solution)/shard_map/ppermute | solution.py:22
  404.7 0.0 collective-permute-start.4
  404.7 4.1 fusion.38
  408.8 3.2 collective-permute-done.4
  412.0 3.3 fusion.28
  (33 shorter events, 0.1 us)
Async XLA Ops:
  7.2 70.4 %copy-start = (bf16[128,1024]{1,0:T(8,128)(2,1)S(1)}, bf16[128,1024]{1,0:T(8,128)(2,1)}, u32[]{:S(2)}) copy-start(bf16[128,1024]{1,0:T(8,128)(2,1)} %param.9) | copy-start | bytes 786436
  8.1 16.4 %collective-permute-start.5 = (f32[16,1,128]{2,1,0:T(1,128)S(1)}, f32[16,1,128]{2,1,0:T(1,128)S(1)}, u32[]{:S(2)}, u32[]{:S(2)}) collective-permute-start(f32[16,1,128]{2,1,0:T(1,128)S(1)} %get-tuple-element.14), channel_id=1, source_target_pairs={{8,0},{16,8},{24,16},{32,24},{40,32},{48,40},{56,48},{64,56},{72,6... | collective-permute-start | bytes 24584 | tf_op jit(solution)/shard_map/ppermute | solution.py:22
  16.4 8.2 %collective-permute-start.6 = (f32[16,1,128]{2,1,0:T(1,128)S(1)}, f32[16,1,128]{2,1,0:T(1,128)S(1)}, u32[]{:S(2)}, u32[]{:S(2)}) collective-permute-start(f32[16,1,128]{2,1,0:T(1,128)S(1)} %get-tuple-element.15), channel_id=1, source_target_pairs={{0,8},{8,16},{16,24},{24,32},{32,40},{40,48},{48,56},{56,64},{64,7... | collective-permute-start | bytes 24584 | tf_op jit(solution)/shard_map/ppermute | solution.py:19
  17.2 7.4 %collective-permute-start.1 = (bf16[16,1,128]{2,1,0:T(2,128)(2,1)S(1)}, bf16[16,1,128]{2,1,0:T(2,128)(2,1)S(1)}, u32[]{:S(2)}, u32[]{:S(2)}) collective-permute-start(bf16[16,1,128]{2,1,0:T(2,128)(2,1)S(1)} %slice.91), channel_id=1, source_target_pairs={{248,0},{0,8},{8,16},{16,24},{24,32},{32,40},{40,48},{48,56},{56,6... | collective-permute-start | bytes 12296 | tf_op jit(solution)/shard_map/ppermute | solution.py:30
  17.3 3.1 copy-start.8
  20.3 1.6 copy-start.4
  21.9 2.6 copy-start.6
  21.9 2.6 copy-start.2
  21.9 2.7 copy-start.5
  30.8 29.5 %all-to-all-start.2 = ((bf16[16,256,128]{2,0,1:T(8,128)(2,1)}), bf16[16,256,128]{2,0,1:T(8,128)(2,1)}, u32[]{:S(2)}, u32[]{:S(2)}) async-start(bf16[16,256,128]{2,0,1:T(8,128)(2,1)} %copy.38), calls=%async_computation.2 | async-start | bytes 2097152 | tf_op jit(solution)/shard_map/all_to_all | solution.py:87
  36.1 6.8 %collective-permute-start = (f32[16,1,128]{2,1,0:T(1,128)S(1)}, f32[16,1,128]{2,1,0:T(1,128)S(1)}, u32[]{:S(2)}, u32[]{:S(2)}) collective-permute-start(f32[16,1,128]{2,1,0:T(1,128)S(1)} %get-tuple-element.20), channel_id=1, source_target_pairs={{8,0},{16,8},{24,16},{32,24},{40,32},{48,40},{56,48},{64,56},{72,6... | collective-permute-start | bytes 24584 | tf_op jit(solution)/shard_map/ppermute | solution.py:22
  41.6 11.6 %collective-permute-start.2 = (f32[16,1,128]{2,1,0:T(1,128)S(1)}, f32[16,1,128]{2,1,0:T(1,128)S(1)}, u32[]{:S(2)}, u32[]{:S(2)}) collective-permute-start(f32[16,1,128]{2,1,0:T(1,128)S(1)} %get-tuple-element.21), channel_id=1, source_target_pairs={{0,8},{8,16},{16,24},{24,32},{32,40},{40,48},{48,56},{56,64},{64,7... | collective-permute-start | bytes 24584 | tf_op jit(solution)/shard_map/ppermute | solution.py:19
  60.4 14.7 %all-to-all-start = ((bf16[16,256,128]{2,0,1:T(8,128)(2,1)}), bf16[16,256,128]{2,0,1:T(8,128)(2,1)S(1)}, u32[]{:S(2)}, u32[]{:S(2)}) async-start(bf16[16,256,128]{2,0,1:T(8,128)(2,1)} %copy.32), calls=%async_computation | async-start | bytes 2097152 | tf_op jit(solution)/shard_map/all_to_all | solution.py:87
  75.0 1.0 copy-start.14
  77.5 11.3 %copy-start.15 = (bf16[128,1024]{1,0:T(8,128)(2,1)S(1)}, bf16[128,1024]{1,0:T(8,128)(2,1)}, u32[]{:S(2)}) copy-start(bf16[128,1024]{1,0:T(8,128)(2,1)} %param.10) | copy-start | bytes 786436
  102.7 3.3 copy-start.3
  112.1 24.1 %all-to-all-start.3 = ((bf16[128,32,128]{2,1,0:T(8,128)(2,1)}), bf16[128,32,128]{2,1,0:T(8,128)(2,1)}, u32[]{:S(2)}, u32[]{:S(2)}) async-start(bf16[128,32,128]{2,1,0:T(8,128)(2,1)} %copy.42), calls=%async_computation.3 | async-start | bytes 2097152 | tf_op jit(solution)/shard_map/all_to_all | solution.py:91
  117.4 266.6 %all-reduce.12.cloned.1.call-start = ((), (), s32[]{:S(2)}) async-start(), calls=%async_computation.4 | async-start | bytes 2097152 | tf_op jit(solution)/shard_map/psum | solution.py:143
  123.1 5.7 %copy-start.16 = (bf16[128,1024]{1,0:T(8,128)(2,1)S(1)}, bf16[128,1024]{1,0:T(8,128)(2,1)}, u32[]{:S(2)}) copy-start(bf16[128,1024]{1,0:T(8,128)(2,1)} %param.10) | copy-start | bytes 786436
  136.3 258.4 %all-to-all-start.1 = ((bf16[128,32,128]{2,1,0:T(8,128)(2,1)}), bf16[128,32,128]{2,1,0:T(8,128)(2,1)}, u32[]{:S(2)}, u32[]{:S(2)}) async-start(bf16[128,32,128]{2,1,0:T(8,128)(2,1)} %copy.36), calls=%async_computation.1 | async-start | bytes 2097152 | tf_op jit(solution)/shard_map/all_to_all | solution.py:91
  387.8 1.6 copy-start.10
  389.7 14.9 %collective-permute-start.7 = (f32[16,1,128]{2,1,0:T(1,128)S(1)}, f32[16,1,128]{2,1,0:T(1,128)S(1)}, u32[]{:S(2)}, u32[]{:S(2)}) collective-permute-start(f32[16,1,128]{2,1,0:T(1,128)S(1)} %get-tuple-element.12), channel_id=1, source_target_pairs={{8,0},{16,8},{24,16},{32,24},{40,32},{48,40},{56,48},{64,56},{72,6... | collective-permute-start | bytes 24584 | tf_op jit(solution)/shard_map/ppermute | solution.py:22
  391.8 12.8 %collective-permute-start.8 = (f32[16,1,128]{2,1,0:T(1,128)S(1)}, f32[16,1,128]{2,1,0:T(1,128)S(1)}, u32[]{:S(2)}, u32[]{:S(2)}) collective-permute-start(f32[16,1,128]{2,1,0:T(1,128)S(1)} %get-tuple-element.13), channel_id=1, source_target_pairs={{0,8},{8,16},{16,24},{24,32},{32,40},{40,48},{48,56},{56,64},{64,7... | collective-permute-start | bytes 24584 | tf_op jit(solution)/shard_map/ppermute | solution.py:19
  396.1 1.6 copy-start.11
  397.7 6.9 %copy-start.12 = (f32[16,256,127]{2,1,0:T(8,128)S(1)}, f32[16,256,127]{2,1,0:T(8,128)}, u32[]{:S(2)}) copy-start(f32[16,256,127]{2,1,0:T(8,128)} %get-tuple-element.10) | copy-start | bytes 6242308
  397.7 7.0 %copy-start.13 = (f32[16,256,127]{2,1,0:T(8,128)S(1)}, f32[16,256,127]{2,1,0:T(8,128)}, u32[]{:S(2)}) copy-start(f32[16,256,127]{2,1,0:T(8,128)} %get-tuple-element.11) | copy-start | bytes 6242308
  398.0 6.7 %copy-start.7 = (f32[16,256,128]{2,1,0:T(8,128)S(1)}, f32[16,256,128]{2,1,0:T(8,128)}, u32[]{:S(2)}) copy-start(f32[16,256,128]{2,1,0:T(8,128)} %copy-done.6) | copy-start | bytes 6291460
  398.0 6.7 %copy-start.9 = (bf16[16,256,128]{2,1,0:T(8,128)(2,1)S(1)}, bf16[16,256,128]{2,1,0:T(8,128)(2,1)}, u32[]{:S(2)}) copy-start(bf16[16,256,128]{2,1,0:T(8,128)(2,1)} %param.8) | copy-start | bytes 3145732
  398.6 10.1 %collective-permute-start.3 = (f32[16,1,128]{2,1,0:T(1,128)S(1)}, f32[16,1,128]{2,1,0:T(1,128)S(1)}, u32[]{:S(2)}, u32[]{:S(2)}) collective-permute-start(f32[16,1,128]{2,1,0:T(1,128)S(1)} %get-tuple-element.18), channel_id=1, source_target_pairs={{8,0},{16,8},{24,16},{32,24},{40,32},{48,40},{56,48},{64,56},{72,6... | collective-permute-start | bytes 24584 | tf_op jit(solution)/shard_map/ppermute | solution.py:22
  404.7 7.3 %collective-permute-start.4 = (f32[16,1,128]{2,1,0:T(1,128)S(1)}, f32[16,1,128]{2,1,0:T(1,128)S(1)}, u32[]{:S(2)}, u32[]{:S(2)}) collective-permute-start(f32[16,1,128]{2,1,0:T(1,128)S(1)} %get-tuple-element.19), channel_id=1, source_target_pairs={{0,8},{8,16},{16,24},{24,32},{32,40},{40,48},{48,56},{56,64},{64,7... | collective-permute-start | bytes 24584 | tf_op jit(solution)/shard_map/ppermute | solution.py:19
  412.0 3.3 copy-start.1
Sparse Core Ops, SparseCore 0:
  129.0 254.9 all-reduce.11
where the time goes:
time: 424 us; the launch traced here: 422 us
  waiting for transfers between devices  267 us (63%)
  matrix products  45.8 us (11%)
  starting transfers between devices  43.1 us (10%)
  local copies, waits for them, and re-layouts  28.2 us (7%)
  other arithmetic  23.5 us (6%)
  between operations  14.3 us (3%)
    psum x1, waiting for transfers between devices, shards(): in_total, out_total = lax.psum((in_grad, out_grad), ('tile', 'lev'))  242 us
    ppermute x4, starting transfers between devices, padded_2(): lax.ppermute(lax.slice_in_dim(block, 0, width, axis=dim), axis, backward)  21.9 us
    dot_general x1, matrix products, network_backward(): jnp.einsum('lxy,lh->xyh', col_grad, w_out, preferred_element_type=jnp.flo...  13.9 us
    ppermute x4, waiting for transfers between devices, padded_2(): lax.ppermute(lax.slice_in_dim(block, block.shape[dim] - width, None, axis...  13.5 us
    dot_general x1, matrix products, network_forward(): jnp.einsum('lxy,lh->xyh', col_in, w_in, preferred_element_type=jnp.float32)  11.3 us
    all_to_all x2, starting transfers between devices, to_levels(): lax.all_to_all(values, 'lev', split_axis=0, concat_axis=1, tiled=True)  11 us
    all_to_all x2, starting transfers between devices, to_columns(): lax.all_to_all(values, 'lev', split_axis=1, concat_axis=0, tiled=True)  10.1 us
  transfers between devices with their start and end apart: 14, of which 6 were waited for; matrix products, arithmetic and copies ran while one was open for 11% of the time, Pallas kernels for 0%

commit v1 on v0

v1 whole, which is shorter than its diff:
```python
import functools
import math

import jax
import jax.numpy as jnp
from jax import lax
from jax.experimental import pallas as pl
from jax.experimental.pallas import tpu as pltpu
from jax.sharding import PartitionSpec as P

KAPPA = 0.05
SLOPE_C = 0.7978845608028654
CUBIC = 0.044715
ROWS = 32
F32 = jnp.float32
BF16 = jnp.bfloat16
VMEM_LIMIT = 48 * 1024 * 1024


def rows_at(ref, index, stride):
    return jnp.concatenate(
        [ref[pl.ds(index, 8, stride), :], ref[pl.ds(index + 8 * stride, 8, stride), :]], 0
    )


def put_rows(ref, index, stride, value):
    ref[pl.ds(index, 8, stride), :] = value[:8]
    ref[pl.ds(index + 8 * stride, 8, stride), :] = value[8:]


def up_of(value):
    return pltpu.roll(value, value.shape[1] - 1, 1)


def down_of(value):
    return pltpu.roll(value, 1, 1)


def wall_mask(north):
    lane = lax.broadcasted_iota(jnp.int32, north.shape, 1)
    return jnp.where(lane < north.shape[1] - 1, north, 0.0)


def step_row(q, q_next, g, g_next, east, north, flux, drift):
    north = wall_mask(north)
    pos_east = jnp.maximum(east, 0.0) + KAPPA
    neg_east = jnp.minimum(east, 0.0) - KAPPA
    pos_north = jnp.maximum(north, 0.0)
    neg_north = jnp.minimum(north, 0.0)
    new_flux = pos_east * q + neg_east * q_next
    cross = pos_north * q + neg_north * up_of(q)
    moved = q - (new_flux - flux) - (cross - down_of(cross))
    ahead = g_next - g
    new_drift = neg_east * ahead
    above = up_of(g) - g
    pulled = (
        g + (pos_east * ahead + drift) + (pos_north * above + down_of(neg_north * above))
    )
    return moved, pulled, new_flux, new_drift


def west_terms(q_prev, q, g_prev, g, east_prev):
    pos = jnp.maximum(east_prev, 0.0) + KAPPA
    neg = jnp.minimum(east_prev, 0.0) - KAPPA
    return pos * q_prev + neg * q, neg * (g - g_prev)


def first_kernel(
    start, blocks, state, state_prev, state_next, cot, cot_prev, cot_next, east, east_prev,
    north, low, high, first, back, cols, speeds, east_s, north_s, prev_s,
):
    here = lax.rem(pl.program_id(0) + start, blocks)
    flat = ROWS * 16
    east_s[...] = east[...].astype(F32).reshape(flat, 128)
    north_s[...] = north[...].astype(F32).reshape(flat, 128)
    prev_s[...] = east_prev[...].astype(F32).reshape(256, 128)
    q2 = state.reshape(flat, 128)
    g2 = cot.reshape(flat, 128)
    at_low = here == 0
    at_high = here == blocks - 1
    q_prev = jnp.where(at_low, low[0], rows_at(state_prev.reshape(128, 128), 7, 8))
    g_prev = jnp.where(at_low, low[1], rows_at(cot_prev.reshape(128, 128), 7, 8))
    e_prev = jnp.where(at_low, low[2], rows_at(prev_s, 15, 16))
    q_last = jnp.where(at_high, high[0], rows_at(state_next.reshape(128, 128), 0, 8))
    g_last = jnp.where(at_high, high[1], rows_at(cot_next.reshape(128, 128), 0, 8))
    q = rows_at(q2, 0, ROWS)
    g = rows_at(g2, 0, ROWS)
    flux, drift = west_terms(q_prev, q, g_prev, g, e_prev)

    def one(i, q, g, q_next, g_next, flux, drift):
        e = rows_at(east_s, i, ROWS)
        n = rows_at(north_s, i, ROWS)
        moved, pulled, flux, drift = step_row(q, q_next, g, g_next, e, n, flux, drift)
        first[i] = moved
        back[i] = pulled
        cols[i, 0] = moved.astype(BF16)
        cols[i, 1] = pulled.astype(BF16)
        speeds[i, 0] = e.astype(BF16)
        speeds[i, 1] = n.astype(BF16)
        return flux, drift

    for i in range(ROWS):
        if i < ROWS - 1:
            q_next = rows_at(q2, i + 1, ROWS)
            g_next = rows_at(g2, i + 1, ROWS)
        else:
            q_next, g_next = q_last, g_last
        flux, drift = one(i, q, g, q_next, g_next, flux, drift)
        q, g = q_next, g_next


def first_step(start, count, state, east, north, cot, low, high):
    width = state.shape[1]
    blocks = width // ROWS
    here = lambda s: lax.rem(s + start, blocks)
    before = lambda s, size: lax.rem(here(s) * (ROWS // size) - 1 + width // size, width // size)
    after = lambda s, size: lax.rem((here(s) + 1) * (ROWS // size), width // size)
    main = pl.BlockSpec((16, ROWS, 128), lambda s: (0, here(s), 0))
    prev = pl.BlockSpec((16, 8, 128), lambda s: (0, before(s, 8), 0))
    prev16 = pl.BlockSpec((16, 16, 128), lambda s: (0, before(s, 16), 0))
    post = pl.BlockSpec((16, 8, 128), lambda s: (0, after(s, 8), 0))
    whole = lambda n: pl.BlockSpec((n, 16, 128), lambda s: (0, 0, 0))
    rows = count * ROWS
    field = pl.BlockSpec((ROWS, 16, 128), lambda s: (s, 0, 0))
    pair = pl.BlockSpec((ROWS, 2, 16, 128), lambda s: (s, 0, 0, 0))
    return pl.pallas_call(
        functools.partial(first_kernel, start, blocks),
        grid=(count,),
        in_specs=[main, prev, post, main, prev, post, main, prev16, main, whole(3), whole(2)],
        out_specs=[field, field, pair, pair],
        out_shape=[
            jax.ShapeDtypeStruct((rows, 16, 128), F32),
            jax.ShapeDtypeStruct((rows, 16, 128), F32),
            jax.ShapeDtypeStruct((rows, 2, 16, 128), BF16),
            jax.ShapeDtypeStruct((rows, 2, 16, 128), BF16),
        ],
        scratch_shapes=[
            pltpu.VMEM((ROWS * 16, 128), F32),
            pltpu.VMEM((ROWS * 16, 128), F32),
            pltpu.VMEM((256, 128), F32),
        ],
        compiler_params=pltpu.CompilerParams(vmem_limit_bytes=VMEM_LIMIT),
        cost_estimate=pl.CostEstimate(
            flops=rows * 16 * 128 * 40, bytes_accessed=rows * 16 * 128 * 28, transcendentals=0
        ),
        name="transport_one",
    )(state, state, state, cot, cot, cot, east, east, north, low, high)


CELLS = 4
HTILE = 256


def network_kernel(cols, w_in_t, w_out_t, w_in, w_out, fields, grads, act_s, dpre_s):
    hidden = w_in_t.shape[0]

    @pl.when(pl.program_id(0) == 0)
    def _():
        grads[...] = jnp.zeros_like(grads)

    col = jnp.concatenate([cols[:, i, 0].reshape(128, 128) for i in range(CELLS)], 1)
    gcol = jnp.concatenate([cols[:, i, 1].reshape(128, 128) for i in range(CELLS)], 1)
    nt = (((1,), (1,)), ((), ()))
    for h in range(0, hidden, HTILE):
        part = slice(h, h + HTILE)
        z = jnp.dot(w_in_t[part, :], col, preferred_element_type=F32)
        z2 = z * z
        t = jnp.tanh(z * (z2 * (SLOPE_C * CUBIC) + SLOPE_C))
        half = 0.5 * t + 0.5
        slope = half + (1.0 - t * t) * (z * (z2 * (1.5 * SLOPE_C * CUBIC) + 0.5 * SLOPE_C))
        act = (z * half).astype(BF16)
        act_s[part, :] = act
        d_act = jnp.dot(w_out_t[part, :], gcol, preferred_element_type=F32)
        d_pre = (d_act * slope).astype(BF16)
        dpre_s[part, :] = d_pre
        grads[0, part, :] += lax.dot_general(d_pre, col, nt, preferred_element_type=F32)
        grads[1, part, :] += lax.dot_general(act, gcol, nt, preferred_element_type=F32)
    tend = jnp.dot(w_out[...], act_s[...], preferred_element_type=F32).astype(BF16)
    d_cols = jnp.dot(w_in[...], dpre_s[...], preferred_element_type=F32).astype(BF16)
    for i in range(CELLS):
        fields[:, i, 0] = tend[:, i * 128 : (i + 1) * 128].reshape(8, 16, 128)
        fields[:, i, 1] = d_cols[:, i * 128 : (i + 1) * 128].reshape(8, 16, 128)


def network(cols, w_in_t, w_out_t, w_in, w_out):
    rows = cols.shape[1]
    hidden = w_in.shape[1]
    block = pl.BlockSpec((8, CELLS, 2, 16, 128), lambda s: (0, s, 0, 0, 0))
    tall = pl.BlockSpec((hidden, 128), lambda s: (0, 0))
    wide = pl.BlockSpec((128, hidden), lambda s: (0, 0))
    return pl.pallas_call(
        network_kernel,
        grid=(rows // CELLS,),
        in_specs=[block, tall, tall, wide, wide],
        out_specs=[block, pl.BlockSpec((2, hidden, 128), lambda s: (0, 0, 0))],
        out_shape=[
            jax.ShapeDtypeStruct(cols.shape, BF16),
            jax.ShapeDtypeStruct((2, hidden, 128), F32),
        ],
        scratch_shapes=[
            pltpu.VMEM((hidden, CELLS * 128), BF16),
            pltpu.VMEM((hidden, CELLS * 128), BF16),
        ],
        compiler_params=pltpu.CompilerParams(vmem_limit_bytes=VMEM_LIMIT),
        cost_estimate=pl.CostEstimate(
            flops=rows * 128 * 128 * hidden * 12,
            bytes_accessed=rows * 128 * 128 * 8,
            transcendentals=rows * 128 * hidden,
        ),
        name="column_network",
    )(cols, w_in_t, w_out_t, w_in, w_out)


def last_kernel(
    first_a, back_a, speeds_a, fields_a, first_b, back_b, speeds_b, fields_b, low, high,
    out, grad,
):
    width = out.shape[1]
    half = width // 2
    quarter = width // 4
    out2 = out.reshape(16 * width, 128)
    grad2 = grad.reshape(16 * width, 128)
    inner = (first_a, back_a, speeds_a, fields_a)
    edges = (first_b, back_b, speeds_b, fields_b)

    def load(part, i):
        first, back, _, fields = part
        return (first[i] + fields[i, 0].astype(F32), back[i] + fields[i, 1].astype(F32))

    def segment(part, offset, place, size, q, g, flux, drift, ending):
        def one(i, carry, following):
            q, g, flux, drift = carry
            q_next, g_next = following
            e = part[2][offset + i, 0].astype(F32)
            n = part[2][offset + i, 1].astype(F32)
            moved, pulled, flux, drift = step_row(q, q_next, g, g_next, e, n, flux, drift)
            put_rows(out2, place + i, width, moved)
            put_rows(grad2, place + i, width, pulled)
            return q_next, g_next, flux, drift

        carry = lax.fori_loop(
            0,
            size - 1,
            lambda i, carry: one(i, carry, load(part, offset + i + 1)),
            (q, g, flux, drift),
            unroll=7,
        )
        return one(size - 1, carry, ending())

    q, g = load(edges, quarter)
    flux, drift = west_terms(low[0], q, low[1], g, low[2])
    carry = (q, g, flux, drift)
    carry = segment(edges, quarter, 0, quarter, *carry, lambda: load(inner, 0))
    carry = segment(inner, 0, quarter, half, *carry, lambda: load(edges, 0))
    segment(edges, 0, quarter + half, quarter, *carry, lambda: (high[0], high[1]))


def last_step(parts, low, high, shape):
    spec = pl.BlockSpec(memory_space=pltpu.VMEM)
    return pl.pallas_call(
        last_kernel,
        in_specs=[spec] * 10,
        out_specs=[spec] * 2,
        out_shape=[jax.ShapeDtypeStruct(shape, F32)] * 2,
        compiler_params=pltpu.CompilerParams(vmem_limit_bytes=VMEM_LIMIT),
        cost_estimate=pl.CostEstimate(
            flops=shape[0] * shape[1] * shape[2] * 40,
            bytes_accessed=shape[0] * shape[1] * shape[2] * 24,
            transcendentals=0,
        ),
        name="transport_two",
    )(*parts, low, high)


def shift(block, distance):
    count = lax.axis_size("tile")
    return lax.ppermute(block, "tile", [(i, (i + distance) % count) for i in range(count)])


def exchange(block):
    return lax.all_to_all(block, "lev", split_axis=0, concat_axis=0, tiled=True)


def partner(block, mask):
    return lax.ppermute(block, "tile", [(i, i ^ mask) for i in range(lax.axis_size("tile"))])


def total_of(grads):
    core = lax.rem(lax.axis_index("tile"), 2)
    mine = lax.dynamic_index_in_dim(grads, core, 0, False)
    other = lax.dynamic_index_in_dim(grads, 1 - core, 0, False)
    part = mine + partner(other, 1)
    hidden = part.shape[0]
    part = jnp.sum(exchange(part.reshape(8, hidden // 8, 128)), 0)
    for base in (2, 8):
        one, two, three = (partner(part, base * k) for k in (1, 2, 3))
        part = (part + one) + (two + three)
    part = exchange(jnp.broadcast_to(part[None], (8, hidden // 8, 128))).reshape(hidden, 128)
    other = partner(part, 1)
    return jnp.where(core == 0, part, other), jnp.where(core == 0, other, part)


def shards(state_in, east_speed, north_speed, w_in, w_out, cotangent):
    width = state_in.shape[1]
    blocks = width // ROWS
    low = shift(
        jnp.stack([state_in[:, -1], cotangent[:, -1], east_speed[:, -1].astype(F32)]), 1
    )
    high = shift(jnp.stack([state_in[:, 0], cotangent[:, 0]]), -1)
    w_in_t, w_out_t = w_in.T, w_out.T
    results = []
    grads = 0.0
    none = jnp.zeros((3, 16, 128), F32)
    for start, lo, hi in ((blocks // 4, none, none[:2]), (3 * blocks // 4, low, high)):
        first, back, cols, speeds = first_step(
            start, blocks // 2, state_in, east_speed, north_speed, cotangent, lo, hi
        )
        rows = cols.shape[0] // 8
        got = exchange(cols.reshape(8, rows, 2, 16, 128))
        fields, part = network(got, w_in_t, w_out_t, w_in, w_out)
        grads = grads + part
        fields = exchange(fields).reshape(8 * rows, 2, 16, 128)
        results.append((first, back, speeds, fields))
    first, back, speeds, fields = results[1]
    quarter = width // 4

    def edge(i):
        return first[i] + fields[i, 0].astype(F32), back[i] + fields[i, 1].astype(F32)

    second_low = shift(jnp.stack(edge(quarter - 1)), 1)
    second_high = shift(jnp.stack(edge(quarter)), -1)
    lows = jnp.concatenate([second_low, low[2:]])
    state_out, state_grad = last_step(
        results[0] + results[1], lows, second_high, state_in.shape
    )
    in_total, out_total = total_of(grads)
    scale = 1.0 / math.sqrt(lax.axis_size("tile") * width * state_in.shape[2])
    return state_out, state_grad, in_total.T * scale, out_total.T * scale


def solution(mesh):
    field = P("lev", "tile", None)
    return jax.shard_map(
        shards,
        mesh=mesh,
        in_specs=(field, field, field, P(), P(), field),
        out_specs=(field, field, P(), P()),
        check_vma=False,
    )
```

time: 424 us -> 189 us (0.45)
  waiting for transfers between devices: 267 us -> 27.3 us
  Pallas kernels: 0 us -> 57.8 us
  matrix products: 45.8 us -> 0 us
  blocking collectives: 0 us -> 26.6 us
  other arithmetic: 23.5 us -> 4.19 us
  between operations: 14.3 us -> 0.86 us
    psum x1 -> x0, waiting for transfers between devices: 242 us -> none  [shards(): in_total, out_total = lax.psum((in_grad, out_grad), ('tile', 'lev'))]
    pallas_call x0 -> x5, Pallas kernels: none -> 57.8 us  [the longest x2 22.7 us: network(): pl.pallas_call(network_kernel, grid=(rows // CELLS,), in_specs=[block, ta...]
    dot_general x6 -> x0, matrix products: 45.8 us -> none  [the longest x1 13.9 us: network_backward(): jnp.einsum('lxy,lh->xyh', col_grad, w_out, preferred_element_type=jnp.flo...]
    all_to_all x0 -> x2, blocking collectives: none -> 26.6 us  [exchange(): return lax.all_to_all(block, 'lev', split_axis=0, concat_axis=0, tiled=True)]
    convert_element_type x5 -> x1, other arithmetic: 13 us -> 0.01 us  [shards(): east_speed[:, -1].astype(F32)]
    unnamed x34 -> x50, local copies, waits for them, and re-layouts: 8.42 us -> 21.1 us
    ppermute x9 -> x12, waiting for transfers between devices: 16.8 us -> 27.3 us  [the longest x8 15.5 us: partner(): lax.ppermute(block, 'tile', [(i, i ^ mask) for i in range(lax.axis_size('...]
    all_to_all x4, waiting for transfers between devices: 8.35 us -> 0.01 us  [exchange(): return lax.all_to_all(block, 'lev', split_axis=0, concat_axis=0, tiled=True)]
  transfers between devices with their start and end apart: 14 -> 16, of which waited for: 6 -> 9; matrix products, arithmetic and copies ran while one was open for 11% -> 4% of each run, Pallas kernels for 0% -> 18%
where the time goes in v1:
time: 189 us; the launch traced here: 188 us
  Pallas kernels  57.8 us (31%)
  starting transfers between devices  46.2 us (24%)
  waiting for transfers between devices  27.3 us (14%)
  blocking collectives  26.6 us (14%)
  local copies, waits for them, and re-layouts  25.1 us (13%)
  other arithmetic  4.19 us (2%)
    all_to_all x2, blocking collectives, exchange(): return lax.all_to_all(block, 'lev', split_axis=0, concat_axis=0, tiled=True)  26.6 us
    pallas_call x2, Pallas kernels, network(): pl.pallas_call(network_kernel, grid=(rows // CELLS,), in_specs=[block, ta...  22.7 us
    pallas_call x2, Pallas kernels, first_step(): pl.pallas_call(functools.partial(first_kernel, start, blocks), grid=(coun...  22.1 us
    all_to_all x4, starting transfers between devices, exchange(): return lax.all_to_all(block, 'lev', split_axis=0, concat_axis=0, tiled=True)  22 us
    unnamed x50, local copies, waits for them, and re-layouts  21.1 us
    ppermute x8, waiting for transfers between devices, partner(): lax.ppermute(block, 'tile', [(i, i ^ mask) for i in range(lax.axis_size('...  15.5 us
    pallas_call x1, Pallas kernels, last_step(): pl.pallas_call(last_kernel, in_specs=[spec] * 10, out_specs=[spec] * 2, o...  13 us
    ppermute x4, starting transfers between devices, shift(): lax.ppermute(block, 'tile', [(i, (i + distance) % count) for i in range(c...  12.7 us
  transfers between devices with their start and end apart: 16, of which 9 were waited for; matrix products, arithmetic and copies ran while one was open for 4% of the time, Pallas kernels for 18%

profile of v1, /device:TPU:2, one launch (start us, length us, event | category | flops | bytes accessed | tf_op | source)
XLA Modules:
  0.0 188.0 jit_solution(18145373206165772678)
XLA Ops:
  0.7 0.0 copy-start
  0.7 1.2 copy-done
  1.9 11.4 %transport_one.2 = (f32[128,16,128]{2,1,0:T(8,128)S(1)}, f32[128,16,128]{2,1,0:T(8,128)S(1)}, bf16[128,2,16,128]{3,2,1,0:T(8,128)(2,1)}, bf16[128,2,16,128]{3,2,1,0:T(8,128)(2,1)S(1)}) custom-call(f32[16,256,128]{2,1,0:T(8,128)} %state_next.3, f32[16,256,128]{2,1,0:T(8,128)} %state_next.3, f32[16,256,128]{2,1,0:T(8,128)} %state_next.3, ...), custom_call_target="tpu_custom_call" | custom-call | flops 10485760 | bytes 7340032 | tf_op jit(solution)/shard_map/transport_one/pallas_call | solution.py:126
  13.3 1.0 copy-done.3
  14.2 1.0 copy-done.5
  15.2 1.0 copy-done.7
  16.2 6.5 %all-to-all-start = ((bf16[8,16,2,16,128]{4,3,2,1,0:T(8,128)(2,1)}), bf16[8,16,2,16,128]{4,3,2,1,0:T(8,128)(2,1)}, u32[]{:S(2)}, u32[]{:S(2)}) async-start(bf16[8,16,2,16,128]{4,3,2,1,0:T(8,128)(2,1)} %bitcast), calls=%async_computation | async-start | bytes 2097152 | tf_op jit(solution)/shard_map/all_to_all | solution.py:281
  22.8 0.9 fusion.1
  23.7 0.9 fusion.2
  24.6 0.1 collective-permute-start
  24.7 6.6 %collective-permute-start.1 = (f32[2,16,128]{2,1,0:T(8,128)S(1)}, f32[2,16,128]{2,1,0:T(8,128)S(1)}, u32[]{:S(2)}, u32[]{:S(2)}) collective-permute-start(f32[2,16,128]{2,1,0:T(8,128)S(1)} %pad_maximum_fusion.2), channel_id=1, source_target_pairs={{0,248},{8,0},{16,8},{24,16},{32,24},{40,32},{48,40},{56,48},{64,5... | collective-permute-start | bytes 49160 | tf_op jit(solution)/shard_map/ppermute | solution.py:277
  31.3 1.4 collective-permute-done.1.high
  32.7 8.6 %collective-permute-done.low = f32[3,16,128]{2,1,0:T(8,128)S(1)} collective-permute-done((f32[3,16,128]{2,1,0:T(8,128)S(1)}, f32[3,16,128]{2,1,0:T(8,128)S(1)}, u32[]{:S(2)}, u32[]{:S(2)}) %collective-permute-start) | collective-permute-done | bytes 24608 | tf_op jit(solution)/shard_map/ppermute | solution.py:277
  41.3 10.7 %transport_one.3 = (f32[128,16,128]{2,1,0:T(8,128)S(1)}, f32[128,16,128]{2,1,0:T(8,128)S(1)}, bf16[128,2,16,128]{3,2,1,0:T(8,128)(2,1)S(1)}, bf16[128,2,16,128]{3,2,1,0:T(8,128)(2,1)S(1)}) custom-call(f32[16,256,128]{2,1,0:T(8,128)} %state_next.3, f32[16,256,128]{2,1,0:T(8,128)} %state_next.3, f32[16,256,128]{2,1,0:T(8,128)} %state_next.3, ...), custom_call_target="tpu_custom_call" | custom-call | flops 10485760 | bytes 7340032 | tf_op jit(solution)/shard_map/transport_one/pallas_call | solution.py:126
  52.0 1.0 copy-done.9
  53.0 1.0 copy-done.11
  54.0 4.9 %all-to-all-start.2 = ((bf16[8,16,2,16,128]{4,3,2,1,0:T(8,128)(2,1)}), bf16[8,16,2,16,128]{4,3,2,1,0:T(8,128)(2,1)}, u32[]{:S(2)}, u32[]{:S(2)}) async-start(bf16[8,16,2,16,128]{4,3,2,1,0:T(8,128)(2,1)} %bitcast.56), calls=%async_computation.2 | async-start | bytes 2097152 | tf_op jit(solution)/shard_map/all_to_all | solution.py:281
  58.9 0.8 copy.25
  59.7 0.8 copy.26
  60.6 0.9 copy-done.14
  61.5 0.9 copy-done.16
  62.5 0.9 copy-done.18
  63.4 11.0 %column_network.2 = (bf16[8,16,2,16,128]{4,3,2,1,0:T(8,128)(2,1)S(1)}, f32[2,1024,128]{2,1,0:T(8,128)S(1)}) custom-call(bf16[8,16,2,16,128]{4,3,2,1,0:T(8,128)(2,1)} %all-to-all-done.cols, bf16[1024,128]{1,0:T(8,128)(2,1)S(1)} %bitcast.57, bf16[1024,128]{1,0:T(8,128)(2,1)S(1)} %bitcast.59, bf16[128,1024]{1,0:T(8,128)(2,1)S(1)} %copy-done.12, ...), custom_call_target="tpu_custom_call" | custom-call | flops 3221225472 | bytes 2097152 | tf_op jit(solution)/shard_map/column_network/pallas_call | solution.py:191
  74.4 0.0 copy-start.10
  74.4 1.0 copy-done.10
  75.4 0.9 copy-done.15
  76.4 0.9 copy-done.17
  77.3 0.9 copy-done.19
  78.2 11.7 %column_network.3 = (bf16[8,16,2,16,128]{4,3,2,1,0:T(8,128)(2,1)}, f32[2,1024,128]{2,1,0:T(8,128)S(1)}) custom-call(bf16[8,16,2,16,128]{4,3,2,1,0:T(8,128)(2,1)} %all-to-all-done.2.cols, bf16[1024,128]{1,0:T(8,128)(2,1)S(1)} %bitcast.58, bf16[1024,128]{1,0:T(8,128)(2,1)S(1)} %bitcast.60, bf16[128,1024]{1,0:T(8,128)(2,1)S(1)} %copy-done.12, ...), custom_call_target="tpu_custom_call" | custom-call | flops 3221225472 | bytes 2097152 | tf_op jit(solution)/shard_map/column_network/pallas_call | solution.py:191
  89.9 0.1 add.52
  90.0 1.0 copy-done.21
  91.1 0.1 collective-permute-start.4
  91.2 1.9 %collective-permute-done.4 = f32[1024,128]{1,0:T(8,128)S(1)} collective-permute-done((f32[1024,128]{1,0:T(8,128)S(1)}, f32[1024,128]{1,0:T(8,128)S(1)}, u32[]{:S(2)}, u32[]{:S(2)}) %collective-permute-start.4) | collective-permute-done | bytes 524320 | tf_op jit(solution)/shard_map/ppermute | solution.py:285
  93.0 1.1 bitcast_add_fusion
  94.2 14.1 %all_to_all.30 = f32[8,128,128]{2,1,0:T(8,128)} all-to-all(f32[8,128,128]{2,1,0:T(8,128)S(1)} %bitcast.64), channel_id=1, replica_groups=mesh['tile'=32,'lev'=8] {'lev'}, dimensions={0} | all-to-all | bytes 1048576 | tf_op jit(solution)/shard_map/all_to_all | solution.py:281
  108.3 5.3 %all-to-all-start.3 = ((bf16[8,16,2,16,128]{4,3,2,1,0:T(8,128)(2,1)}), bf16[8,16,2,16,128]{4,3,2,1,0:T(8,128)(2,1)S(1)}, u32[]{:S(2)}, u32[]{:S(2)}) async-start(bf16[8,16,2,16,128]{4,3,2,1,0:T(8,128)(2,1)} %get-tuple-element.27), calls=%async_computation.3 | async-start | bytes 2097152 | tf_op jit(solution)/shard_map/all_to_all | solution.py:281
  113.6 1.1 reduce_sum.9
  114.7 0.2 collective-permute-start.5
  114.8 1.4 collective-permute-start.6
  116.2 5.1 %collective-permute-start.7 = (f32[128,128]{1,0:T(8,128)S(1)}, f32[128,128]{1,0:T(8,128)S(1)}, u32[]{:S(2)}, u32[]{:S(2)}) collective-permute-start(f32[128,128]{1,0:T(8,128)S(1)} %reduce_sum.9), channel_id=1, source_target_pairs={{0,48},{8,56},{16,32},{24,40},{32,16},{40,24},{48,0},{56,8},{64,11... | collective-permute-start | bytes 196616 | tf_op jit(solution)/shard_map/ppermute | solution.py:285
  121.2 7.3 %collective-permute-done.5 = f32[128,128]{1,0:T(8,128)S(1)} collective-permute-done((f32[128,128]{1,0:T(8,128)S(1)}, f32[128,128]{1,0:T(8,128)S(1)}, u32[]{:S(2)}, u32[]{:S(2)}) %collective-permute-start.5) | collective-permute-done | bytes 65568 | tf_op jit(solution)/shard_map/ppermute | solution.py:285
  128.6 2.0 %collective-permute-done.6 = f32[128,128]{1,0:T(8,128)S(1)} collective-permute-done((f32[128,128]{1,0:T(8,128)S(1)}, f32[128,128]{1,0:T(8,128)S(1)}, u32[]{:S(2)}, u32[]{:S(2)}) %collective-permute-start.6) | collective-permute-done | bytes 65568 | tf_op jit(solution)/shard_map/ppermute | solution.py:285
  130.6 3.1 %collective-permute-start.10 = (f32[128,128]{1,0:T(8,128)S(1)}, f32[128,128]{1,0:T(8,128)S(1)}, u32[]{:S(2)}, u32[]{:S(2)}) collective-permute-start(f32[128,128]{1,0:T(8,128)S(1)} %add_add_fusion.1), channel_id=1, source_target_pairs={{0,192},{8,200},{16,208},{24,216},{32,224},{40,232},{48,240},{56,2... | collective-permute-start | bytes 196616 | tf_op jit(solution)/shard_map/ppermute | solution.py:285
  133.7 0.1 collective-permute-start.8
  133.9 1.5 collective-permute-start.9
  135.4 1.3 collective-permute-done.10
  136.7 1.3 collective-permute-done.8
  138.0 1.6 collective-permute-done.9
  139.6 0.1 copy.32
  139.8 12.4 %all_to_all.31 = f32[8,128,128]{1,2,0:T(8,128)} all-to-all(f32[8,128,128]{1,2,0:T(8,128)S(1)} %broadcast_in_dim.10), channel_id=1, replica_groups=mesh['tile'=32,'lev'=8] {'lev'}, dimensions={0} | all-to-all | bytes 1048576 | tf_op jit(solution)/shard_map/all_to_all | solution.py:281
  152.2 5.3 %all-to-all-start.1 = ((bf16[8,16,2,16,128]{4,3,2,1,0:T(8,128)(2,1)}), bf16[8,16,2,16,128]{4,3,2,1,0:T(8,128)(2,1)S(1)}, u32[]{:S(2)}, u32[]{:S(2)}) async-start(bf16[8,16,2,16,128]{4,3,2,1,0:T(8,128)(2,1)} %copy-done.10), calls=%async_computation.1 | async-start | bytes 2097152 | tf_op jit(solution)/shard_map/all_to_all | solution.py:281
  157.5 2.0 %copy.33 = f32[8,128,128]{2,1,0:T(8,128)} copy(f32[8,128,128]{1,2,0:T(8,128)} %all_to_all.31) | data formatting | bytes 1048576 | tf_op jit(solution)/shard_map/all_to_all | solution.py:281
  159.6 0.7 convert_add_fusion.1
  160.3 0.6 collective-permute-start.2
  160.8 5.5 %collective-permute-start.3 = (f32[2,16,128]{2,1,0:T(8,128)S(1)}, f32[2,16,128]{2,1,0:T(8,128)S(1)}, u32[]{:S(2)}, u32[]{:S(2)}) collective-permute-start(f32[2,16,128]{2,1,0:T(8,128)S(1)} %pad_maximum_fusion.4), channel_id=1, source_target_pairs={{0,248},{8,0},{16,8},{24,16},{32,24},{40,32},{48,40},{56,48},{64,5... | collective-permute-start | bytes 49160 | tf_op jit(solution)/shard_map/ppermute | solution.py:277
  166.3 1.8 collective-permute-done.2
  168.1 0.0 copy-start.4
  168.2 1.2 copy-done.4
  169.4 1.2 copy-done.6
  170.6 1.2 copy-done.8
  171.8 13.0 %transport_two.1 = (f32[16,256,128]{2,1,0:T(8,128)}, f32[16,256,128]{2,1,0:T(8,128)}) custom-call(f32[128,16,128]{2,1,0:T(8,128)S(1)} %copy-done.4, f32[128,16,128]{2,1,0:T(8,128)S(1)} %copy-done.6, bf16[128,2,16,128]{3,2,1,0:T(8,128)(2,1)S(1)} %copy-done.8, bf16[128,2,16,128]{3,2,1,0:T(8,128)(2,1)S(1)} %bitcast.55, ...), custom_call_target="tpu_custom_call" | custom-call | flops 20971520 | bytes 12582912 | tf_op jit(solution)/shard_map/transport_two/pallas_call | solution.py:260
  184.9 1.1 multiply_bitcast_fusion
  186.0 1.0 copy.34
  187.0 1.0 copy.35
  (48 shorter events, 0.2 us)
Async XLA Ops:
  0.7 1.2 copy-start
  13.3 1.0 copy-start.3
  14.2 1.0 copy-start.5
  15.2 1.0 copy-start.7
  16.2 6.5 %copy-start.1 = (bf16[16,256,128]{2,1,0:T(8,128)(2,1)S(1)}, bf16[16,256,128]{2,1,0:T(8,128)(2,1)}, u32[]{:S(2)}) copy-start(bf16[16,256,128]{2,1,0:T(8,128)(2,1)} %east_prev.3) | copy-start | bytes 3145732
  16.2 37.7 %all-to-all-start = ((bf16[8,16,2,16,128]{4,3,2,1,0:T(8,128)(2,1)}), bf16[8,16,2,16,128]{4,3,2,1,0:T(8,128)(2,1)}, u32[]{:S(2)}, u32[]{:S(2)}) async-start(bf16[8,16,2,16,128]{4,3,2,1,0:T(8,128)(2,1)} %bitcast), calls=%async_computation | async-start | bytes 2097152 | tf_op jit(solution)/shard_map/all_to_all | solution.py:281
  24.6 16.8 %collective-permute-start = (f32[3,16,128]{2,1,0:T(8,128)S(1)}, f32[3,16,128]{2,1,0:T(8,128)S(1)}, u32[]{:S(2)}, u32[]{:S(2)}) collective-permute-start(f32[3,16,128]{2,1,0:T(8,128)S(1)} %pad_maximum_fusion), channel_id=1, source_target_pairs={{0,8},{8,16},{16,24},{24,32},{32,40},{40,48},{48,56},{56,64},{64,7... | collective-permute-start | bytes 73736 | tf_op jit(solution)/shard_map/ppermute | solution.py:277
  24.7 8.0 %collective-permute-start.1 = (f32[2,16,128]{2,1,0:T(8,128)S(1)}, f32[2,16,128]{2,1,0:T(8,128)S(1)}, u32[]{:S(2)}, u32[]{:S(2)}) collective-permute-start(f32[2,16,128]{2,1,0:T(8,128)S(1)} %pad_maximum_fusion.2), channel_id=1, source_target_pairs={{0,248},{8,0},{16,8},{24,16},{32,24},{40,32},{48,40},{56,48},{64,5... | collective-permute-start | bytes 49160 | tf_op jit(solution)/shard_map/ppermute | solution.py:277
  52.0 1.0 copy-start.9
  53.0 1.0 copy-start.11
  54.0 105.6 %copy-start.2 = (f32[128,16,128]{2,1,0:T(8,128)}, f32[128,16,128]{2,1,0:T(8,128)S(1)}, u32[]{:S(2)}) copy-start(f32[128,16,128]{2,1,0:T(8,128)S(1)} %get-tuple-element.24.back_b) | copy-start | bytes 3145732
  54.0 4.9 %copy-start.12 = (bf16[128,1024]{1,0:T(8,128)(2,1)S(1)}, bf16[128,1024]{1,0:T(8,128)(2,1)}, u32[]{:S(2)}) copy-start(bf16[128,1024]{1,0:T(8,128)(2,1)} %w_in.3) | copy-start | bytes 786436
  54.0 5.8 %copy-start.13 = (bf16[128,1024]{1,0:T(8,128)(2,1)S(1)}, bf16[128,1024]{1,0:T(8,128)(2,1)}, u32[]{:S(2)}) copy-start(bf16[128,1024]{1,0:T(8,128)(2,1)} %w_out.3) | copy-start | bytes 786436
  54.0 21.4 %all-to-all-start.2 = ((bf16[8,16,2,16,128]{4,3,2,1,0:T(8,128)(2,1)}), bf16[8,16,2,16,128]{4,3,2,1,0:T(8,128)(2,1)}, u32[]{:S(2)}, u32[]{:S(2)}) async-start(bf16[8,16,2,16,128]{4,3,2,1,0:T(8,128)(2,1)} %bitcast.56), calls=%async_computation.2 | async-start | bytes 2097152 | tf_op jit(solution)/shard_map/all_to_all | solution.py:281
  60.6 0.9 copy-start.14
  61.5 0.9 copy-start.16
  62.5 0.9 copy-start.18
  74.4 1.0 copy-start.10
  75.4 1.0 copy-start.15
  76.3 0.9 copy-start.17
  77.3 0.9 copy-start.19
  90.0 1.0 copy-start.21
  91.1 2.0 %collective-permute-start.4 = (f32[1024,128]{1,0:T(8,128)S(1)}, f32[1024,128]{1,0:T(8,128)S(1)}, u32[]{:S(2)}, u32[]{:S(2)}) collective-permute-start(f32[1024,128]{1,0:T(8,128)S(1)} %dynamic-slice_bitcast_fusion), channel_id=1, source_target_pairs={{0,8},{8,0},{16,24},{24,16},{32,40},{40,32},{48,56},{56,48},{64,72... | collective-permute-start | bytes 1572872 | tf_op jit(solution)/shard_map/ppermute | solution.py:285
  108.3 31.4 %all-to-all-start.3 = ((bf16[8,16,2,16,128]{4,3,2,1,0:T(8,128)(2,1)}), bf16[8,16,2,16,128]{4,3,2,1,0:T(8,128)(2,1)S(1)}, u32[]{:S(2)}, u32[]{:S(2)}) async-start(bf16[8,16,2,16,128]{4,3,2,1,0:T(8,128)(2,1)} %get-tuple-element.27), calls=%async_computation.3 | async-start | bytes 2097152 | tf_op jit(solution)/shard_map/all_to_all | solution.py:281
  114.7 13.9 %collective-permute-start.5 = (f32[128,128]{1,0:T(8,128)S(1)}, f32[128,128]{1,0:T(8,128)S(1)}, u32[]{:S(2)}, u32[]{:S(2)}) collective-permute-start(f32[128,128]{1,0:T(8,128)S(1)} %reduce_sum.9), channel_id=1, source_target_pairs={{0,16},{8,24},{16,0},{24,8},{32,48},{40,56},{48,32},{56,40},{64,80... | collective-permute-start | bytes 196616 | tf_op jit(solution)/shard_map/ppermute | solution.py:285
  114.8 15.8 %collective-permute-start.6 = (f32[128,128]{1,0:T(8,128)S(1)}, f32[128,128]{1,0:T(8,128)S(1)}, u32[]{:S(2)}, u32[]{:S(2)}) collective-permute-start(f32[128,128]{1,0:T(8,128)S(1)} %reduce_sum.9), channel_id=1, source_target_pairs={{0,32},{8,40},{16,48},{24,56},{32,0},{40,8},{48,16},{56,24},{64,96... | collective-permute-start | bytes 196616 | tf_op jit(solution)/shard_map/ppermute | solution.py:285
  116.2 14.4 %collective-permute-start.7 = (f32[128,128]{1,0:T(8,128)S(1)}, f32[128,128]{1,0:T(8,128)S(1)}, u32[]{:S(2)}, u32[]{:S(2)}) collective-permute-start(f32[128,128]{1,0:T(8,128)S(1)} %reduce_sum.9), channel_id=1, source_target_pairs={{0,48},{8,56},{16,32},{24,40},{32,16},{40,24},{48,0},{56,8},{64,11... | collective-permute-start | bytes 196616 | tf_op jit(solution)/shard_map/ppermute | solution.py:285
  130.6 6.1 %collective-permute-start.10 = (f32[128,128]{1,0:T(8,128)S(1)}, f32[128,128]{1,0:T(8,128)S(1)}, u32[]{:S(2)}, u32[]{:S(2)}) collective-permute-start(f32[128,128]{1,0:T(8,128)S(1)} %add_add_fusion.1), channel_id=1, source_target_pairs={{0,192},{8,200},{16,208},{24,216},{32,224},{40,232},{48,240},{56,2... | collective-permute-start | bytes 196616 | tf_op jit(solution)/shard_map/ppermute | solution.py:285
  133.7 4.3 %collective-permute-start.8 = (f32[128,128]{1,0:T(8,128)S(1)}, f32[128,128]{1,0:T(8,128)S(1)}, u32[]{:S(2)}, u32[]{:S(2)}) collective-permute-start(f32[128,128]{1,0:T(8,128)S(1)} %add_add_fusion.1), channel_id=1, source_target_pairs={{0,64},{8,72},{16,80},{24,88},{32,96},{40,104},{48,112},{56,120},{... | collective-permute-start | bytes 196616 | tf_op jit(solution)/shard_map/ppermute | solution.py:285
  133.9 5.8 %collective-permute-start.9 = (f32[128,128]{1,0:T(8,128)S(1)}, f32[128,128]{1,0:T(8,128)S(1)}, u32[]{:S(2)}, u32[]{:S(2)}) collective-permute-start(f32[128,128]{1,0:T(8,128)S(1)} %add_add_fusion.1), channel_id=1, source_target_pairs={{0,128},{8,136},{16,144},{24,152},{32,160},{40,168},{48,176},{56,1... | collective-permute-start | bytes 196616 | tf_op jit(solution)/shard_map/ppermute | solution.py:285
  139.7 12.5 %copy-start.20 = (bf16[8,16,2,16,128]{4,3,2,1,0:T(8,128)(2,1)}, bf16[8,16,2,16,128]{4,3,2,1,0:T(8,128)(2,1)S(1)}, u32[]{:S(2)}) copy-start(bf16[8,16,2,16,128]{4,3,2,1,0:T(8,128)(2,1)S(1)} %all-to-all-done.3) | copy-start | bytes 3145732
  152.2 15.9 %all-to-all-start.1 = ((bf16[8,16,2,16,128]{4,3,2,1,0:T(8,128)(2,1)}), bf16[8,16,2,16,128]{4,3,2,1,0:T(8,128)(2,1)S(1)}, u32[]{:S(2)}, u32[]{:S(2)}) async-start(bf16[8,16,2,16,128]{4,3,2,1,0:T(8,128)(2,1)} %copy-done.10), calls=%async_computation.1 | async-start | bytes 2097152 | tf_op jit(solution)/shard_map/all_to_all | solution.py:281
  159.5 25.3 %collective-permute-start.11 = (f32[1024,128]{1,0:T(8,128)}, f32[1024,128]{1,0:T(8,128)}, u32[]{:S(2)}, u32[]{:S(2)}) collective-permute-start(f32[1024,128]{1,0:T(8,128)} %bitcast.63), channel_id=1, source_target_pairs={{0,8},{8,0},{16,24},{24,16},{32,40},{40,32},{48,56},{56,48},{64,72... | collective-permute-start | bytes 1572872 | tf_op jit(solution)/shard_map/ppermute | solution.py:285
  160.3 7.9 %collective-permute-start.2 = (f32[2,16,128]{2,1,0:T(8,128)S(1)}, f32[2,16,128]{2,1,0:T(8,128)S(1)}, u32[]{:S(2)}, u32[]{:S(2)}) collective-permute-start(f32[2,16,128]{2,1,0:T(8,128)S(1)} %pad_maximum_fusion.3), channel_id=1, source_target_pairs={{0,8},{8,16},{16,24},{24,32},{32,40},{40,48},{48,56},{56,64},{64,7... | collective-permute-start | bytes 49160 | tf_op jit(solution)/shard_map/ppermute | solution.py:277
  160.8 7.3 %collective-permute-start.3 = (f32[2,16,128]{2,1,0:T(8,128)S(1)}, f32[2,16,128]{2,1,0:T(8,128)S(1)}, u32[]{:S(2)}, u32[]{:S(2)}) collective-permute-start(f32[2,16,128]{2,1,0:T(8,128)S(1)} %pad_maximum_fusion.4), channel_id=1, source_target_pairs={{0,248},{8,0},{16,8},{24,16},{32,24},{40,32},{48,40},{56,48},{64,5... | collective-permute-start | bytes 49160 | tf_op jit(solution)/shard_map/ppermute | solution.py:277
  168.1 1.2 copy-start.4
  169.4 1.2 copy-start.6
  170.6 1.2 copy-start.8
  171.8 13.1 %copy-start.22 = (f32[8,128,128]{2,1,0:T(8,128)S(1)}, f32[8,128,128]{2,1,0:T(8,128)}, u32[]{:S(2)}) copy-start(f32[8,128,128]{2,1,0:T(8,128)} %copy.33) | copy-start | bytes 1572868

commit v2 on v1

v2 whole, which is shorter than its diff:
```python
import functools
import math

import jax
import jax.numpy as jnp
from jax import lax
from jax.experimental import pallas as pl
from jax.experimental.pallas import tpu as pltpu
from jax.sharding import PartitionSpec as P

KAPPA = 0.05
SLOPE_C = 0.7978845608028654
CUBIC = 0.044715
ROWS = 32
UNROLL = 16
F32 = jnp.float32
BF16 = jnp.bfloat16
MIB = 1024 * 1024


def spread(pairs, tile):
    for ref, scratch in pairs:
        size = min(16, ref.shape[1])
        place = pl.multiple_of(tile * 16, size)
        part = ref[:, pl.ds(place, size), :].astype(F32)
        part = jnp.swapaxes(part, 0, 1).reshape(size * 16, 128)
        scratch[pl.ds(pl.multiple_of(tile * 256, 256), size * 16), :] = part


def row(ref, index):
    return ref[pl.ds(pl.multiple_of(index * 16, 16), 16), :]


def put_rows(ref, index, stride, value):
    ref[pl.ds(index, 8, stride), :] = value[:8]
    ref[pl.ds(index + 8 * stride, 8, stride), :] = value[8:]


def up_of(value):
    return pltpu.roll(value, value.shape[1] - 1, 1)


def down_of(value):
    return pltpu.roll(value, 1, 1)


def wall_mask(north):
    lane = lax.broadcasted_iota(jnp.int32, north.shape, 1)
    return jnp.where(lane < north.shape[1] - 1, north, 0.0)


def step_row(q, q_next, g, g_next, east, north, flux, drift):
    north = wall_mask(north)
    pos_east = jnp.maximum(east, 0.0) + KAPPA
    neg_east = jnp.minimum(east, 0.0) - KAPPA
    pos_north = jnp.maximum(north, 0.0)
    neg_north = jnp.minimum(north, 0.0)
    new_flux = pos_east * q + neg_east * q_next
    cross = pos_north * q + neg_north * up_of(q)
    moved = q - (new_flux - flux) - (cross - down_of(cross))
    ahead = g_next - g
    new_drift = neg_east * ahead
    above = up_of(g) - g
    pulled = (
        g + (pos_east * ahead + drift) + (pos_north * above + down_of(neg_north * above))
    )
    return moved, pulled, new_flux, new_drift


def west_terms(q_prev, q, g_prev, g, east_prev):
    pos = jnp.maximum(east_prev, 0.0) + KAPPA
    neg = jnp.minimum(east_prev, 0.0) - KAPPA
    return pos * q_prev + neg * q, neg * (g - g_prev)


def first_kernel(
    start, blocks, state, state_prev, state_next, cot, cot_prev, cot_next, east, east_prev,
    north, low, high, *rest,
):
    first, back, speeds, cols, q_s, g_s, east_s, north_s = rest[-13:-5]
    prev_s, gprev_s, next_s, gnext_s, eprev_s = rest[-5:]
    here = lax.rem(pl.program_id(0) + start, blocks)
    at_low = here == 0
    at_high = here == blocks - 1
    pairs = ((state, q_s), (cot, g_s), (east, east_s), (north, north_s))

    def spread_tile(tile, carry):
        spread(pairs, tile)
        return carry

    lax.fori_loop(0, ROWS // 16, spread_tile, 0)
    spread(((state_prev, prev_s), (cot_prev, gprev_s), (east_prev, eprev_s)), 0)
    spread(((state_next, next_s), (cot_next, gnext_s)), 0)
    q_prev = jnp.where(at_low, low[0], row(prev_s, 7))
    g_prev = jnp.where(at_low, low[1], row(gprev_s, 7))
    e_prev = jnp.where(at_low, low[2], row(eprev_s, 15))
    q_s[ROWS * 16 :, :] = jnp.where(at_high, high[0], row(next_s, 0))
    g_s[ROWS * 16 :, :] = jnp.where(at_high, high[1], row(gnext_s, 0))
    q = row(q_s, 0)
    g = row(g_s, 0)
    flux, drift = west_terms(q_prev, q, g_prev, g, e_prev)

    def one(i, carry):
        q, g, flux, drift = carry
        q_next = row(q_s, i + 1)
        g_next = row(g_s, i + 1)
        e = row(east_s, i)
        n = row(north_s, i)
        moved, pulled, flux, drift = step_row(q, q_next, g, g_next, e, n, flux, drift)
        first[i] = moved
        back[i] = pulled
        cols[i, 0] = moved.astype(BF16)
        cols[i, 1] = pulled.astype(BF16)
        speeds[i, 0] = e.astype(BF16)
        speeds[i, 1] = n.astype(BF16)
        return q_next, g_next, flux, drift

    lax.fori_loop(0, ROWS, one, (q, g, flux, drift), unroll=UNROLL)


def in_hbm(array):
    return pltpu.with_memory_space_constraint(array, pltpu.HBM)


def first_step(start, count, state, east, north, cot, low, high, filled):
    width = state.shape[1]
    blocks = width // ROWS
    here = lambda s: lax.rem(s + start, blocks)
    before = lambda s, size: lax.rem(here(s) * (ROWS // size) - 1 + width // size, width // size)
    after = lambda s, size: lax.rem((here(s) + 1) * (ROWS // size), width // size)
    main = pl.BlockSpec((16, ROWS, 128), lambda s: (0, here(s), 0))
    prev = pl.BlockSpec((16, 8, 128), lambda s: (0, before(s, 8), 0))
    prev16 = pl.BlockSpec((16, 16, 128), lambda s: (0, before(s, 16), 0))
    post = pl.BlockSpec((16, 8, 128), lambda s: (0, after(s, 8), 0))
    whole = lambda n: pl.BlockSpec((n, 16, 128), lambda s: (0, 0, 0))
    rows = count * ROWS
    field = pl.BlockSpec((ROWS, 16, 128), lambda s: (here(s), 0, 0))
    speed = pl.BlockSpec((ROWS, 2, 16, 128), lambda s: (here(s), 0, 0, 0))
    pair = pl.BlockSpec((ROWS, 2, 16, 128), lambda s: (s, 0, 0, 0))
    return pl.pallas_call(
        functools.partial(first_kernel, start, blocks),
        grid=(count,),
        in_specs=[main, prev, post, main, prev, post, main, prev16, main, whole(3), whole(2)]
        + [pl.BlockSpec(memory_space=pl.ANY)] * len(filled),
        out_specs=[field, field, speed, pair],
        out_shape=[
            pltpu.HBM((width, 16, 128), F32),
            pltpu.HBM((width, 16, 128), F32),
            pltpu.HBM((width, 2, 16, 128), BF16),
            pltpu.HBM((rows, 2, 16, 128), BF16),
        ],
        input_output_aliases={11 + k: k for k in range(len(filled))},
        scratch_shapes=[
            pltpu.VMEM(((ROWS + 1) * 16, 128), F32),
            pltpu.VMEM(((ROWS + 1) * 16, 128), F32),
            pltpu.VMEM((ROWS * 16, 128), F32),
            pltpu.VMEM((ROWS * 16, 128), F32),
            pltpu.VMEM((128, 128), F32),
            pltpu.VMEM((128, 128), F32),
            pltpu.VMEM((128, 128), F32),
            pltpu.VMEM((128, 128), F32),
            pltpu.VMEM((256, 128), F32),
        ],
        compiler_params=pltpu.CompilerParams(vmem_limit_bytes=16 * MIB),
        cost_estimate=pl.CostEstimate(
            flops=rows * 16 * 128 * 40, bytes_accessed=rows * 16 * 128 * 28, transcendentals=0
        ),
        name="transport_one",
    )(
        *[in_hbm(x) for x in (state, state, state, cot, cot, cot, east, east, north)],
        low,
        high,
        *filled,
    )


def edge_kernel(state_lo, state_hi, cot_lo, cot_hi, east_hi, low, high):
    low[0] = state_hi[:, 7, :]
    low[1] = cot_hi[:, 7, :]
    low[2] = east_hi[...].astype(F32)[:, 15, :]
    high[0] = state_lo[:, 0, :]
    high[1] = cot_lo[:, 0, :]


def edge_rows(state, east, cot):
    width = state.shape[1]
    head = pl.BlockSpec((16, 8, 128), lambda s: (0, 0, 0))
    tail = pl.BlockSpec((16, 8, 128), lambda s: (0, width // 8 - 1, 0))
    tail16 = pl.BlockSpec((16, 16, 128), lambda s: (0, width // 16 - 1, 0))
    return pl.pallas_call(
        edge_kernel,
        grid=(1,),
        in_specs=[head, tail, head, tail, tail16],
        out_specs=[
            pl.BlockSpec((3, 16, 128), lambda s: (0, 0, 0)),
            pl.BlockSpec((2, 16, 128), lambda s: (0, 0, 0)),
        ],
        out_shape=[
            jax.ShapeDtypeStruct((3, 16, 128), F32),
            jax.ShapeDtypeStruct((2, 16, 128), F32),
        ],
        name="edge_rows",
    )(*[in_hbm(x) for x in (state, state, cot, cot, east)])


CELLS = 8
HTILE = 256


def network_kernel(cols, w_in_t, w_out_t, w_in, w_out, before, fields, grads, act_s, dpre_s):
    hidden = w_in_t.shape[0]

    @pl.when(pl.program_id(0) == 0)
    def _():
        grads[...] = before[...]

    col = jnp.concatenate([cols[:, i, 0].reshape(128, 128) for i in range(CELLS)], 1)
    gcol = jnp.concatenate([cols[:, i, 1].reshape(128, 128) for i in range(CELLS)], 1)
    nt = (((1,), (1,)), ((), ()))
    for h in range(0, hidden, HTILE):
        part = slice(h, h + HTILE)
        z = jnp.dot(w_in_t[part, :], col, preferred_element_type=F32)
        z2 = z * z
        t = jnp.tanh(z * (z2 * (SLOPE_C * CUBIC) + SLOPE_C))
        half = 0.5 * t + 0.5
        slope = half + (1.0 - t * t) * (z * (z2 * (1.5 * SLOPE_C * CUBIC) + 0.5 * SLOPE_C))
        act = (z * half).astype(BF16)
        act_s[part, :] = act
        d_act = jnp.dot(w_out_t[part, :], gcol, preferred_element_type=F32)
        d_pre = (d_act * slope).astype(BF16)
        dpre_s[part, :] = d_pre
        grads[0, part, :] += lax.dot_general(d_pre, col, nt, preferred_element_type=F32)
        grads[1, part, :] += lax.dot_general(act, gcol, nt, preferred_element_type=F32)
    tend = jnp.dot(w_out[...], act_s[...], preferred_element_type=F32).astype(BF16)
    d_cols = jnp.dot(w_in[...], dpre_s[...], preferred_element_type=F32).astype(BF16)
    for i in range(CELLS):
        fields[:, i, 0] = tend[:, i * 128 : (i + 1) * 128].reshape(8, 16, 128)
        fields[:, i, 1] = d_cols[:, i * 128 : (i + 1) * 128].reshape(8, 16, 128)


def network(cols, w_in_t, w_out_t, w_in, w_out, grads):
    rows = cols.shape[1]
    hidden = w_in.shape[1]
    block = pl.BlockSpec((8, CELLS, 2, 16, 128), lambda s: (0, s, 0, 0, 0))
    tall = pl.BlockSpec((hidden, 128), lambda s: (0, 0))
    wide = pl.BlockSpec((128, hidden), lambda s: (0, 0))
    total = pl.BlockSpec((2, hidden, 128), lambda s: (0, 0, 0))
    return pl.pallas_call(
        functools.partial(network_kernel),
        grid=(rows // CELLS,),
        in_specs=[block, tall, tall, wide, wide, total],
        out_specs=[block, total],
        out_shape=[
            pltpu.HBM(cols.shape, BF16),
            jax.ShapeDtypeStruct((2, hidden, 128), F32),
        ],
        scratch_shapes=[
            pltpu.VMEM((hidden, CELLS * 128), BF16),
            pltpu.VMEM((hidden, CELLS * 128), BF16),
        ],
        compiler_params=pltpu.CompilerParams(vmem_limit_bytes=24 * MIB),
        cost_estimate=pl.CostEstimate(
            flops=rows * 128 * 128 * hidden * 12,
            bytes_accessed=rows * 128 * 128 * 8,
            transcendentals=rows * 128 * hidden,
        ),
        name="column_network",
    )(in_hbm(cols), w_in_t, w_out_t, w_in, w_out, grads)


def last_kernel(
    first, first_next, back, back_next, speeds, inner, inner_next, outer, outer_next, low, high,
    out, grad, q_s, g_s, flux_s, drift_s,
):
    here = pl.program_id(0)
    blocks = pl.num_programs(0)
    inside = jnp.logical_and(here >= blocks // 4, here < blocks - blocks // 4)

    def fill(fields):
        def one(i, carry):
            at = pl.ds(pl.multiple_of(i * 16, 16), 16)
            q_s[at, :] = first[i] + fields[i, 0].astype(F32)
            g_s[at, :] = back[i] + fields[i, 1].astype(F32)
            return carry

        lax.fori_loop(0, ROWS, one, 0, unroll=UNROLL)

    pl.when(inside)(lambda: fill(inner))
    pl.when(jnp.logical_not(inside))(lambda: fill(outer))
    last = here == blocks - 1
    next_inside = jnp.logical_and(here + 1 >= blocks // 4, here + 1 < blocks - blocks // 4)
    add = jnp.where(next_inside, inner_next[0].astype(F32), outer_next[0].astype(F32))
    q_s[ROWS * 16 :, :] = jnp.where(last, high[0], first_next[0] + add[0])
    g_s[ROWS * 16 :, :] = jnp.where(last, high[1], back_next[0] + add[1])
    q = row(q_s, 0)
    g = row(g_s, 0)
    flux, drift = west_terms(low[0], q, low[1], g, low[2])
    flux = jnp.where(here == 0, flux, flux_s[...])
    drift = jnp.where(here == 0, drift, drift_s[...])
    out2 = out.reshape(16 * ROWS, 128)
    grad2 = grad.reshape(16 * ROWS, 128)

    def one(i, carry):
        q, g, flux, drift = carry
        q_next = row(q_s, i + 1)
        g_next = row(g_s, i + 1)
        e = speeds[i, 0].astype(F32)
        n = speeds[i, 1].astype(F32)
        moved, pulled, flux, drift = step_row(q, q_next, g, g_next, e, n, flux, drift)
        put_rows(out2, i, ROWS, moved)
        put_rows(grad2, i, ROWS, pulled)
        return q_next, g_next, flux, drift

    carry = lax.fori_loop(0, ROWS, one, (q, g, flux, drift), unroll=UNROLL)
    flux_s[...] = carry[2]
    drift_s[...] = carry[3]


def last_step(first, back, speeds, inner, outer, low, high, shape):
    width = shape[1]
    blocks = width // ROWS
    part = blocks // 4
    quarter = width // 4
    held = lambda s: jnp.clip(s - part, 0, 2 * part - 1)
    kept = lambda s: jnp.where(s < 3 * part, jnp.minimum(s + part, 2 * part - 1), s - 3 * part)
    row_held = lambda r: jnp.clip(r - quarter, 0, 2 * quarter - 1)
    row_kept = lambda r: jnp.where(
        r < quarter, r + quarter, jnp.clip(r - 3 * quarter, 0, 2 * quarter - 1)
    )
    after = lambda s: jnp.minimum((s + 1) * ROWS, width - 1)
    field = pl.BlockSpec((ROWS, 16, 128), lambda s: (s, 0, 0))
    field_next = pl.BlockSpec((1, 16, 128), lambda s: (after(s), 0, 0))
    pair = lambda index: pl.BlockSpec((ROWS, 2, 16, 128), lambda s: (index(s), 0, 0, 0))
    pair_next = lambda index: pl.BlockSpec(
        (1, 2, 16, 128), lambda s: (index((s + 1) * ROWS), 0, 0, 0)
    )
    whole = lambda n: pl.BlockSpec((n, 16, 128), lambda s: (0, 0, 0))
    result = pl.BlockSpec((16, ROWS, 128), lambda s: (0, s, 0))
    return pl.pallas_call(
        last_kernel,
        grid=(blocks,),
        in_specs=[
            field, field_next, field, field_next, pair(lambda s: s),
            pair(held), pair_next(row_held), pair(kept), pair_next(row_kept), whole(3), whole(2),
        ],
        out_specs=[result] * 2,
        out_shape=[pltpu.HBM(shape, F32)] * 2,
        scratch_shapes=[pltpu.VMEM(((ROWS + 1) * 16, 128), F32)] * 2
        + [pltpu.VMEM((16, 128), F32)] * 2,
        compiler_params=pltpu.CompilerParams(vmem_limit_bytes=16 * MIB),
        cost_estimate=pl.CostEstimate(
            flops=shape[0] * shape[1] * shape[2] * 40,
            bytes_accessed=shape[0] * shape[1] * shape[2] * 24,
            transcendentals=0,
        ),
        name="transport_two",
    )(*[in_hbm(x) for x in (first, first, back, back, speeds, inner, inner, outer, outer)], low, high)


def shift(block, distance):
    count = lax.axis_size("tile")
    return lax.ppermute(block, "tile", [(i, (i + distance) % count) for i in range(count)])


def exchange(block):
    return lax.all_to_all(block, "lev", split_axis=0, concat_axis=0, tiled=True)


def partner(block, mask):
    return lax.ppermute(block, "tile", [(i, i ^ mask) for i in range(lax.axis_size("tile"))])


def chip_sum(grads):
    core = lax.rem(lax.axis_index("tile"), 2)
    mine = lax.dynamic_index_in_dim(grads, core, 0, False)
    other = lax.dynamic_index_in_dim(grads, 1 - core, 0, False)
    return mine + partner(other, 1)


def exchange_rows(block):
    lev = lax.axis_size("lev")
    groups = [
        [(y * 8 + rest) * lev + k for y in range(4) for k in range(lev)] for rest in range(8)
    ]
    return lax.all_to_all(
        block, ("tile", "lev"), split_axis=0, concat_axis=0, tiled=True, axis_index_groups=groups
    )


def z_sum(part):
    one, two, three = (partner(part, 2 * k) for k in (1, 2, 3))
    return (part + one) + (two + three)


def shards(state_in, east_speed, north_speed, w_in, w_out, cotangent):
    width = state_in.shape[1]
    blocks = width // ROWS
    hidden = w_in.shape[1]
    barrier = lax.optimization_barrier
    low, high = edge_rows(state_in, east_speed, cotangent)
    low, high, state_in = barrier((low, high, state_in))
    low = shift(low, 1)
    high = shift(high, -1)
    w_in_t, w_out_t = w_in.T, w_out.T
    none = jnp.zeros((3, 16, 128), F32)
    half = blocks // 2
    fields_in = (state_in, east_speed, north_speed, cotangent)
    *held, cols_a = first_step(blocks // 4, half, *fields_in, none, none[:2], ())
    cols_a, low, high = barrier((cols_a, low, high))
    got_a = exchange(cols_a.reshape(8, width // 16, 2, 16, 128))
    first, back, speeds, cols_b = first_step(3 * blocks // 4, half, *fields_in, low, high, held)
    got_b = exchange(cols_b.reshape(8, width // 16, 2, 16, 128))
    zero = jnp.zeros((2, hidden, 128), F32)
    fields_a, grads = network(got_a, w_in_t, w_out_t, w_in, w_out, zero)
    fields_a = exchange(fields_a)
    fields_b, grads = network(got_b, w_in_t, w_out_t, w_in, w_out, grads)
    grads, fields_a = barrier((grads, fields_a))
    part = chip_sum(grads)
    part = jnp.sum(exchange_rows(part.reshape(32, hidden // 32, 128)), 0)
    part, fields_b = barrier((part, fields_b))
    fields_b = exchange(fields_b)
    part = z_sum(part)
    part, fields_b = barrier((part, fields_b))
    inner = fields_a.reshape(width // 2, 2, 16, 128)
    outer = fields_b.reshape(width // 2, 2, 16, 128)
    quarter = width // 4

    def edge(row, i):
        return jnp.stack([first[row], back[row]]) + outer[i].astype(F32)

    second_low = shift(edge(width - 1, quarter - 1), 1)
    second_high = shift(edge(0, quarter), -1)
    lows = jnp.concatenate([second_low, low[2:]])
    part = exchange_rows(jnp.broadcast_to(part[None], (32,) + part.shape)).reshape(hidden, 128)
    state_out, state_grad = last_step(
        first, back, speeds, inner, outer, lows, second_high, state_in.shape
    )
    part, state_out, state_grad = barrier((part, state_out, state_grad))
    other = partner(part, 1)
    core = lax.rem(lax.axis_index("tile"), 2)
    in_total = jnp.where(core == 0, part, other)
    out_total = jnp.where(core == 0, other, part)
    scale = 1.0 / math.sqrt(lax.axis_size("tile") * width * state_in.shape[2])
    return state_out, state_grad, in_total.T * scale, out_total.T * scale


def solution(mesh):
    field = P("lev", "tile", None)
    return jax.shard_map(
        shards,
        mesh=mesh,
        in_specs=(field, field, field, P(), P(), field),
        out_specs=(field, field, P(), P()),
        check_vma=False,
    )
```

time: 189 us -> 145 us (0.77)
  local copies, waits for them, and re-layouts: 25.1 us -> 5.11 us
  Pallas kernels: 57.8 us -> 47.1 us
  waiting for transfers between devices: 27.3 us -> 20.8 us
  blocking collectives: 26.6 us -> 20.5 us
  other arithmetic: 4.19 us -> 0.19 us
  starting transfers between devices: 46.2 us -> 49 us
    unnamed x50 -> x14, local copies, waits for them, and re-layouts: 21.1 us -> 3.31 us
    ppermute x4, waiting for transfers between devices: 11.9 us -> 1.53 us  [shift(): lax.ppermute(block, 'tile', [(i, (i + distance) % count) for i in range(c...]
    pallas_call x2, Pallas kernels: 22.1 us -> 12.8 us  [first_step(): pl.pallas_call(functools.partial(first_kernel, start, blocks), grid=(coun...]
    all_to_all x0 -> x1, starting transfers between devices: none -> 7.64 us  [exchange_rows(): lax.all_to_all(block, ('tile', 'lev'), split_axis=0, concat_axis=0, tiled...]
    all_to_all x4, waiting for transfers between devices: 0.01 us -> 7.45 us  [exchange(): return lax.all_to_all(block, 'lev', split_axis=0, concat_axis=0, tiled=True)]
    all_to_all x2 -> x1, blocking collectives: 26.6 us -> 20.5 us  [exchange_rows(): lax.all_to_all(block, ('tile', 'lev'), split_axis=0, concat_axis=0, tiled...]
    ppermute x8 -> x5, starting transfers between devices: 11.5 us -> 7.45 us  [partner(): lax.ppermute(block, 'tile', [(i, i ^ mask) for i in range(lax.axis_size('...]
    ppermute x8 -> x5, waiting for transfers between devices: 15.5 us -> 11.8 us  [partner(): lax.ppermute(block, 'tile', [(i, i ^ mask) for i in range(lax.axis_size('...]
  transfers between devices with their start and end apart: 16 -> 14, of which waited for: 9 -> 8; matrix products, arithmetic and copies ran while one was open for 4% -> 1% of each run, Pallas kernels for 18% -> 32%
where the time goes in v2:
time: 145 us; the launch traced here: 144 us
  starting transfers between devices  49 us (34%)
  Pallas kernels  47.1 us (32%)
  waiting for transfers between devices  20.8 us (14%)
  blocking collectives  20.5 us (14%)
  local copies, waits for them, and re-layouts  5.11 us (4%)
    pallas_call x2, Pallas kernels, network(): pl.pallas_call(functools.partial(network_kernel), grid=(rows // CELLS,),...  21.3 us
    all_to_all x1, blocking collectives, exchange_rows(): lax.all_to_all(block, ('tile', 'lev'), split_axis=0, concat_axis=0, tiled...  20.5 us
    all_to_all x4, starting transfers between devices, exchange(): return lax.all_to_all(block, 'lev', split_axis=0, concat_axis=0, tiled=True)  19.7 us
    ppermute x4, starting transfers between devices, shift(): lax.ppermute(block, 'tile', [(i, (i + distance) % count) for i in range(c...  14.2 us
    pallas_call x2, Pallas kernels, first_step(): pl.pallas_call(functools.partial(first_kernel, start, blocks), grid=(coun...  12.8 us
    ppermute x5, waiting for transfers between devices, partner(): lax.ppermute(block, 'tile', [(i, i ^ mask) for i in range(lax.axis_size('...  11.8 us
    pallas_call x1, Pallas kernels, last_step(): pl.pallas_call(last_kernel, grid=(blocks,), in_specs=[field, field_next,...  11.4 us
    all_to_all x1, starting transfers between devices, exchange_rows(): lax.all_to_all(block, ('tile', 'lev'), split_axis=0, concat_axis=0, tiled...  7.64 us
  transfers between devices with their start and end apart: 14, of which 8 were waited for; matrix products, arithmetic and copies ran while one was open for 1% of the time, Pallas kernels for 32%

profile of v2, /device:TPU:2, one launch (start us, length us, event | category | flops | bytes accessed | tf_op | source)
XLA Modules:
  0.0 143.5 jit_solution(2667448438560428226)
XLA Ops:
  0.6 1.6 %edge_rows.1 = (f32[3,16,128]{2,1,0:T(8,128)}, f32[2,16,128]{2,1,0:T(8,128)}) custom-call(f32[16,256,128]{2,1,0:T(8,128)} %state_next.1, f32[16,256,128]{2,1,0:T(8,128)} %state_next.1, f32[16,256,128]{2,1,0:T(8,128)} %cot_next.3, f32[16,256,128]{2,1,0:T(8,128)} %cot_next.3, bf16[16,256,128]{2,1,0:T(8,128)(2,1)} %east_prev.3), custom_call_target="tpu_custom_call" | custom-call | tf_op jit(solution)/shard_map/edge_rows/pallas_call | solution.py:190
  2.2 0.0 collective-permute-start
  2.2 8.2 %collective-permute-start.1 = (f32[2,16,128]{2,1,0:T(8,128)}, f32[2,16,128]{2,1,0:T(8,128)S(1)}, u32[]{:S(2)}, u32[]{:S(2)}) collective-permute-start(f32[2,16,128]{2,1,0:T(8,128)} %get-tuple-element.40), channel_id=1, source_target_pairs={{0,248},{8,0},{16,8},{24,16},{32,24},{40,32},{48,40},{56,48},{64,5... | collective-permute-start | bytes 49160 | tf_op jit(solution)/shard_map/ppermute | solution.py:362
  10.4 6.4 %transport_one.2 = (f32[256,16,128]{2,1,0:T(8,128)}, f32[256,16,128]{2,1,0:T(8,128)}, bf16[256,2,16,128]{3,2,1,0:T(8,128)(2,1)}, bf16[128,2,16,128]{3,2,1,0:T(8,128)(2,1)}) custom-call(f32[16,256,128]{2,1,0:T(8,128)} %state_next.1, f32[16,256,128]{2,1,0:T(8,128)} %state_next.1, f32[16,256,128]{2,1,0:T(8,128)} %state_next.1, f32[16,256,128]{2,1,0:T(8,128)} %cot_next.3, ...), custom_call_target="tpu_custom_call" | custom-call | flops 10485760 | bytes 7340032 | tf_op jit(solution)/shard_map/transport_one/pallas_call | solution.py:140
  16.9 0.0 collective-permute-done.1.high
  16.9 0.0 collective-permute-done.low
  16.9 5.3 %all-to-all-start.1 = ((bf16[8,16,2,16,128]{4,3,2,1,0:T(8,128)(2,1)}), bf16[8,16,2,16,128]{4,3,2,1,0:T(8,128)(2,1)S(1)}, u32[]{:S(2)}, u32[]{:S(2)}) async-start(bf16[8,16,2,16,128]{4,3,2,1,0:T(8,128)(2,1)} %bitcast.37), calls=%async_computation.1 | async-start | bytes 2097152 | tf_op jit(solution)/shard_map/all_to_all | solution.py:366
  22.2 6.4 %transport_one.3 = (f32[256,16,128]{2,1,0:T(8,128)}, f32[256,16,128]{2,1,0:T(8,128)}, bf16[256,2,16,128]{3,2,1,0:T(8,128)(2,1)}, bf16[128,2,16,128]{3,2,1,0:T(8,128)(2,1)}) custom-call(f32[16,256,128]{2,1,0:T(8,128)} %state_next.1, f32[16,256,128]{2,1,0:T(8,128)} %state_next.1, ...), custom_call_target="tpu_custom_call", output_to_operand_aliasing={{0}: (11, {}), {1}: (12, {}), {2}: (13, {})} | custom-call | flops 10485760 | bytes 7340032 | tf_op jit(solution)/shard_map/transport_one/pallas_call | solution.py:140
  28.6 0.0 copy-start
  28.6 0.0 copy-start.1
  28.6 3.5 %all-to-all-done.1.cols = bf16[8,16,2,16,128]{4,3,2,1,0:T(8,128)(2,1)S(1)} async-done(((bf16[8,16,2,16,128]{4,3,2,1,0:T(8,128)(2,1)}), bf16[8,16,2,16,128]{4,3,2,1,0:T(8,128)(2,1)S(1)}, u32[]{:S(2)}, u32[]{:S(2)}) %all-to-all-start.1) | async-done | bytes 1048608 | tf_op jit(solution)/shard_map/all_to_all | solution.py:366
  32.1 0.0 copy-start.4
  32.1 1.0 copy-done.4
  33.1 4.8 %all-to-all-start = ((bf16[8,16,2,16,128]{4,3,2,1,0:T(8,128)(2,1)}), bf16[8,16,2,16,128]{4,3,2,1,0:T(8,128)(2,1)S(1)}, u32[]{:S(2)}, u32[]{:S(2)}) async-start(bf16[8,16,2,16,128]{4,3,2,1,0:T(8,128)(2,1)} %bitcast.36), calls=%async_computation | async-start | bytes 2097152 | tf_op jit(solution)/shard_map/all_to_all | solution.py:366
  37.9 0.0 copy-done
  37.9 0.2 copy.15
  38.1 0.0 copy-done.1
  38.1 0.2 copy.16
  38.2 0.1 broadcast_in_dim.13.before
  38.3 10.7 %column_network.2 = (bf16[8,16,2,16,128]{4,3,2,1,0:T(8,128)(2,1)}, f32[2,1024,128]{2,1,0:T(8,128)S(1)}) custom-call(bf16[8,16,2,16,128]{4,3,2,1,0:T(8,128)(2,1)} %copy-done.4, bf16[1024,128]{1,0:T(8,128)(2,1)S(1)} %bitcast.26, bf16[1024,128]{1,0:T(8,128)(2,1)S(1)} %bitcast.28, bf16[128,1024]{1,0:T(8,128)(2,1)S(1)} %copy-done, ...), custom_call_target="tpu_custom_call" | custom-call | flops 3221225472 | bytes 2097152 | tf_op jit(solution)/shard_map/column_network/pallas_call | solution.py:248
  49.0 1.2 all-to-all-done.cols
  50.2 0.0 copy-start.3
  50.2 5.3 %all-to-all-start.2 = ((bf16[8,16,2,16,128]{4,3,2,1,0:T(8,128)(2,1)}), bf16[8,16,2,16,128]{4,3,2,1,0:T(8,128)(2,1)}, u32[]{:S(2)}, u32[]{:S(2)}) async-start(bf16[8,16,2,16,128]{4,3,2,1,0:T(8,128)(2,1)} %get-tuple-element.50), calls=%async_computation.2 | async-start | bytes 2097152 | tf_op jit(solution)/shard_map/all_to_all | solution.py:366
  55.5 0.0 copy-done.3
  55.5 10.6 %column_network.3 = (bf16[8,16,2,16,128]{4,3,2,1,0:T(8,128)(2,1)}, f32[2,1024,128]{2,1,0:T(8,128)S(1)}) custom-call(bf16[8,16,2,16,128]{4,3,2,1,0:T(8,128)(2,1)} %copy-done.3, bf16[1024,128]{1,0:T(8,128)(2,1)S(1)} %bitcast.27, bf16[1024,128]{1,0:T(8,128)(2,1)S(1)} %bitcast.29, bf16[128,1024]{1,0:T(8,128)(2,1)S(1)} %copy-done, ...), custom_call_target="tpu_custom_call" | custom-call | flops 3221225472 | bytes 2097152 | tf_op jit(solution)/shard_map/column_network/pallas_call | solution.py:248
  66.1 2.8 %all-to-all-done.2 = bf16[8,16,2,16,128]{4,3,2,1,0:T(8,128)(2,1)} async-done(((bf16[8,16,2,16,128]{4,3,2,1,0:T(8,128)(2,1)}), bf16[8,16,2,16,128]{4,3,2,1,0:T(8,128)(2,1)}, u32[]{:S(2)}, u32[]{:S(2)}) %all-to-all-start.2) | async-done | bytes 1048608 | tf_op jit(solution)/shard_map/all_to_all | solution.py:366
  68.9 0.1 collective-permute-start.2
  69.0 1.9 %collective-permute-done.2 = f32[1024,128]{1,0:T(8,128)S(1)} collective-permute-done((f32[1024,128]{1,0:T(8,128)S(1)}, f32[1024,128]{1,0:T(8,128)S(1)}, u32[]{:S(2)}, u32[]{:S(2)}) %collective-permute-start.2) | collective-permute-done | bytes 524320 | tf_op jit(solution)/shard_map/ppermute | solution.py:370
  70.9 0.1 bitcast_add_fusion
  71.0 20.5 %all_to_all.30 = f32[32,32,128]{2,1,0:T(8,128)S(1)} all-to-all(f32[32,32,128]{2,1,0:T(8,128)S(1)} %bitcast.35), channel_id=1, replica_groups={{0,1,2,3,4,5,6,7,64,65,66,67,68,69,70,71,128,129,130,131,132,133,134,13..., dimensions={0} | all-to-all | bytes 1048576 | tf_op jit(solution)/shard_map/all_to_all | solution.py:385
  91.5 4.3 %all-to-all-start.4 = ((bf16[8,16,2,16,128]{4,3,2,1,0:T(8,128)(2,1)}), bf16[8,16,2,16,128]{4,3,2,1,0:T(8,128)(2,1)S(1)}, u32[]{:S(2)}, u32[]{:S(2)}) async-start(bf16[8,16,2,16,128]{4,3,2,1,0:T(8,128)(2,1)} %get-tuple-element.54), calls=%async_computation.4 | async-start | bytes 2097152 | tf_op jit(solution)/shard_map/all_to_all | solution.py:366
  95.8 3.7 %collective-permute-start.3 = (f32[32,128]{1,0:T(8,128)S(1)}, f32[32,128]{1,0:T(8,128)S(1)}, u32[]{:S(2)}, u32[]{:S(2)}) collective-permute-start(f32[32,128]{1,0:T(8,128)S(1)} %reduce_sum.9), channel_id=1, source_target_pairs={{0,16},{8,24},{16,0},{24,8},{32,48},{40,56},{48,32},{56,40},{64,80... | collective-permute-start | bytes 49160 | tf_op jit(solution)/shard_map/ppermute | solution.py:370
  99.5 1.3 collective-permute-start.4
  100.8 2.3 %collective-permute-start.5 = (f32[32,128]{1,0:T(8,128)S(1)}, f32[32,128]{1,0:T(8,128)S(1)}, u32[]{:S(2)}, u32[]{:S(2)}) collective-permute-start(f32[32,128]{1,0:T(8,128)S(1)} %reduce_sum.9), channel_id=1, source_target_pairs={{0,48},{8,56},{16,32},{24,40},{32,16},{40,24},{48,0},{56,8},{64,11... | collective-permute-start | bytes 49160 | tf_op jit(solution)/shard_map/ppermute | solution.py:370
  103.1 4.2 %collective-permute-done.3 = f32[32,128]{1,0:T(8,128)S(1)} collective-permute-done((f32[32,128]{1,0:T(8,128)S(1)}, f32[32,128]{1,0:T(8,128)S(1)}, u32[]{:S(2)}, u32[]{:S(2)}) %collective-permute-start.3) | collective-permute-done | bytes 16416 | tf_op jit(solution)/shard_map/ppermute | solution.py:370
  107.3 3.8 %collective-permute-done.4 = f32[32,128]{1,0:T(8,128)S(1)} collective-permute-done((f32[32,128]{1,0:T(8,128)S(1)}, f32[32,128]{1,0:T(8,128)S(1)}, u32[]{:S(2)}, u32[]{:S(2)}) %collective-permute-start.4) | collective-permute-done | bytes 16416 | tf_op jit(solution)/shard_map/ppermute | solution.py:370
  111.1 0.0 collective-permute-done.5
  111.2 0.0 all-to-all-done.4
  111.2 0.0 copy-start.2
  111.2 0.9 broadcast_in_dim.14
  112.1 7.6 %all-to-all-start.5 = ((f32[32,32,128]{2,1,0:T(8,128)}), f32[32,32,128]{2,1,0:T(8,128)S(1)}, u32[]{:S(2)}, u32[]{:S(2)}) async-start(f32[32,32,128]{2,1,0:T(8,128)} %broadcast_in_dim.14), calls=%async_computation.5 | async-start | bytes 1048576 | tf_op jit(solution)/shard_map/all_to_all | solution.py:385
  119.8 0.8 fusion
  120.5 0.1 collective-permute-start.6
  120.6 5.9 %collective-permute-start.7 = (f32[2,16,128]{2,1,0:T(8,128)S(1)}, f32[2,16,128]{2,1,0:T(8,128)S(1)}, u32[]{:S(2)}, u32[]{:S(2)}) collective-permute-start(f32[2,16,128]{2,1,0:T(8,128)S(1)} %get-tuple-element.76), channel_id=1, source_target_pairs={{0,248},{8,0},{16,8},{24,16},{32,24},{40,32},{48,40},{56,48},{64,5... | collective-permute-start | bytes 49160 | tf_op jit(solution)/shard_map/ppermute | solution.py:362
  126.6 1.5 %collective-permute-done.6 = f32[2,16,128]{2,1,0:T(8,128)S(1)} collective-permute-done((f32[2,16,128]{2,1,0:T(8,128)S(1)}, f32[2,16,128]{2,1,0:T(8,128)S(1)}, u32[]{:S(2)}, u32[]{:S(2)}) %collective-permute-start.6) | collective-permute-done | bytes 16416 | tf_op jit(solution)/shard_map/ppermute | solution.py:362
  128.1 0.0 collective-permute-done.7.high
  128.1 0.0 copy-done.2
  128.1 11.4 %transport_two.1 = (f32[16,256,128]{2,1,0:T(8,128)}, f32[16,256,128]{2,1,0:T(8,128)}) custom-call(f32[256,16,128]{2,1,0:T(8,128)} %get-tuple-element.56.first.first_next, f32[256,16,128]{2,1,0:T(8,128)} %get-tuple-element.56.first.first_next, f32[256,16,128]{2,1,0:T(8,128)} %get-tuple-element.57.back.back_next, ...), custom_call_target="tpu_custom_call" | custom-call | flops 20971520 | bytes 12582912 | tf_op jit(solution)/shard_map/transport_two/pallas_call | solution.py:339
  139.5 0.0 all-to-all-done.5
  139.5 0.1 collective-permute-start.8
  139.6 1.9 %collective-permute-done.8 = f32[1024,128]{1,0:T(8,128)S(1)} collective-permute-done((f32[1024,128]{1,0:T(8,128)S(1)}, f32[1024,128]{1,0:T(8,128)S(1)}, u32[]{:S(2)}, u32[]{:S(2)}) %collective-permute-start.8) | collective-permute-done | bytes 524320 | tf_op jit(solution)/shard_map/ppermute | solution.py:370
  141.5 0.1 multiply_bitcast_fusion
  141.5 1.0 copy.17
  142.5 1.0 copy.18
  (8 shorter events, 0.1 us)
Async XLA Ops:
  2.2 14.6 %collective-permute-start = (f32[3,16,128]{2,1,0:T(8,128)}, f32[3,16,128]{2,1,0:T(8,128)S(1)}, u32[]{:S(2)}, u32[]{:S(2)}) collective-permute-start(f32[3,16,128]{2,1,0:T(8,128)} %get-tuple-element.39), channel_id=1, source_target_pairs={{0,8},{8,16},{16,24},{24,32},{32,40},{40,48},{48,56},{56,64},{64,7... | collective-permute-start | bytes 73736 | tf_op jit(solution)/shard_map/ppermute | solution.py:362
  2.2 14.6 %collective-permute-start.1 = (f32[2,16,128]{2,1,0:T(8,128)}, f32[2,16,128]{2,1,0:T(8,128)S(1)}, u32[]{:S(2)}, u32[]{:S(2)}) collective-permute-start(f32[2,16,128]{2,1,0:T(8,128)} %get-tuple-element.40), channel_id=1, source_target_pairs={{0,248},{8,0},{16,8},{24,16},{32,24},{40,32},{48,40},{56,48},{64,5... | collective-permute-start | bytes 49160 | tf_op jit(solution)/shard_map/ppermute | solution.py:362
  16.9 15.2 %all-to-all-start.1 = ((bf16[8,16,2,16,128]{4,3,2,1,0:T(8,128)(2,1)}), bf16[8,16,2,16,128]{4,3,2,1,0:T(8,128)(2,1)S(1)}, u32[]{:S(2)}, u32[]{:S(2)}) async-start(bf16[8,16,2,16,128]{4,3,2,1,0:T(8,128)(2,1)} %bitcast.37), calls=%async_computation.1 | async-start | bytes 2097152 | tf_op jit(solution)/shard_map/all_to_all | solution.py:366
  28.6 9.3 %copy-start = (bf16[128,1024]{1,0:T(8,128)(2,1)S(1)}, bf16[128,1024]{1,0:T(8,128)(2,1)}, u32[]{:S(2)}) copy-start(bf16[128,1024]{1,0:T(8,128)(2,1)} %w_in.3) | copy-start | bytes 786436
  28.6 9.4 %copy-start.1 = (bf16[128,1024]{1,0:T(8,128)(2,1)S(1)}, bf16[128,1024]{1,0:T(8,128)(2,1)}, u32[]{:S(2)}) copy-start(bf16[128,1024]{1,0:T(8,128)(2,1)} %w_out.3) | copy-start | bytes 786436
  32.1 1.0 copy-start.4
  33.1 17.1 %all-to-all-start = ((bf16[8,16,2,16,128]{4,3,2,1,0:T(8,128)(2,1)}), bf16[8,16,2,16,128]{4,3,2,1,0:T(8,128)(2,1)S(1)}, u32[]{:S(2)}, u32[]{:S(2)}) async-start(bf16[8,16,2,16,128]{4,3,2,1,0:T(8,128)(2,1)} %bitcast.36), calls=%async_computation | async-start | bytes 2097152 | tf_op jit(solution)/shard_map/all_to_all | solution.py:366
  50.2 5.3 %copy-start.3 = (bf16[8,16,2,16,128]{4,3,2,1,0:T(8,128)(2,1)}, bf16[8,16,2,16,128]{4,3,2,1,0:T(8,128)(2,1)S(1)}, u32[]{:S(2)}) copy-start(bf16[8,16,2,16,128]{4,3,2,1,0:T(8,128)(2,1)S(1)} %all-to-all-done.cols) | copy-start | bytes 3145732
  50.2 18.7 %all-to-all-start.2 = ((bf16[8,16,2,16,128]{4,3,2,1,0:T(8,128)(2,1)}), bf16[8,16,2,16,128]{4,3,2,1,0:T(8,128)(2,1)}, u32[]{:S(2)}, u32[]{:S(2)}) async-start(bf16[8,16,2,16,128]{4,3,2,1,0:T(8,128)(2,1)} %get-tuple-element.50), calls=%async_computation.2 | async-start | bytes 2097152 | tf_op jit(solution)/shard_map/all_to_all | solution.py:366
  68.9 2.0 %collective-permute-start.2 = (f32[1024,128]{1,0:T(8,128)S(1)}, f32[1024,128]{1,0:T(8,128)S(1)}, u32[]{:S(2)}, u32[]{:S(2)}) collective-permute-start(f32[1024,128]{1,0:T(8,128)S(1)} %dynamic-slice_bitcast_fusion), channel_id=1, source_target_pairs={{0,8},{8,0},{16,24},{24,16},{32,40},{40,32},{48,56},{56,48},{64,72... | collective-permute-start | bytes 1572872 | tf_op jit(solution)/shard_map/ppermute | solution.py:370
  91.5 19.6 %all-to-all-start.4 = ((bf16[8,16,2,16,128]{4,3,2,1,0:T(8,128)(2,1)}), bf16[8,16,2,16,128]{4,3,2,1,0:T(8,128)(2,1)S(1)}, u32[]{:S(2)}, u32[]{:S(2)}) async-start(bf16[8,16,2,16,128]{4,3,2,1,0:T(8,128)(2,1)} %get-tuple-element.54), calls=%async_computation.4 | async-start | bytes 2097152 | tf_op jit(solution)/shard_map/all_to_all | solution.py:366
  95.8 11.5 %collective-permute-start.3 = (f32[32,128]{1,0:T(8,128)S(1)}, f32[32,128]{1,0:T(8,128)S(1)}, u32[]{:S(2)}, u32[]{:S(2)}) collective-permute-start(f32[32,128]{1,0:T(8,128)S(1)} %reduce_sum.9), channel_id=1, source_target_pairs={{0,16},{8,24},{16,0},{24,8},{32,48},{40,56},{48,32},{56,40},{64,80... | collective-permute-start | bytes 49160 | tf_op jit(solution)/shard_map/ppermute | solution.py:370
  99.5 11.6 %collective-permute-start.4 = (f32[32,128]{1,0:T(8,128)S(1)}, f32[32,128]{1,0:T(8,128)S(1)}, u32[]{:S(2)}, u32[]{:S(2)}) collective-permute-start(f32[32,128]{1,0:T(8,128)S(1)} %reduce_sum.9), channel_id=1, source_target_pairs={{0,32},{8,40},{16,48},{24,56},{32,0},{40,8},{48,16},{56,24},{64,96... | collective-permute-start | bytes 49160 | tf_op jit(solution)/shard_map/ppermute | solution.py:370
  100.8 10.4 %collective-permute-start.5 = (f32[32,128]{1,0:T(8,128)S(1)}, f32[32,128]{1,0:T(8,128)S(1)}, u32[]{:S(2)}, u32[]{:S(2)}) collective-permute-start(f32[32,128]{1,0:T(8,128)S(1)} %reduce_sum.9), channel_id=1, source_target_pairs={{0,48},{8,56},{16,32},{24,40},{32,16},{40,24},{48,0},{56,8},{64,11... | collective-permute-start | bytes 49160 | tf_op jit(solution)/shard_map/ppermute | solution.py:370
  111.2 16.9 %copy-start.2 = (bf16[8,16,2,16,128]{4,3,2,1,0:T(8,128)(2,1)}, bf16[8,16,2,16,128]{4,3,2,1,0:T(8,128)(2,1)S(1)}, u32[]{:S(2)}) copy-start(bf16[8,16,2,16,128]{4,3,2,1,0:T(8,128)(2,1)S(1)} %all-to-all-done.4) | copy-start | bytes 3145732
  112.1 27.4 %all-to-all-start.5 = ((f32[32,32,128]{2,1,0:T(8,128)}), f32[32,32,128]{2,1,0:T(8,128)S(1)}, u32[]{:S(2)}, u32[]{:S(2)}) async-start(f32[32,32,128]{2,1,0:T(8,128)} %broadcast_in_dim.14), calls=%async_computation.5 | async-start | bytes 1048576 | tf_op jit(solution)/shard_map/all_to_all | solution.py:385
  120.5 7.6 %collective-permute-start.6 = (f32[2,16,128]{2,1,0:T(8,128)S(1)}, f32[2,16,128]{2,1,0:T(8,128)S(1)}, u32[]{:S(2)}, u32[]{:S(2)}) collective-permute-start(f32[2,16,128]{2,1,0:T(8,128)S(1)} %get-tuple-element.77), channel_id=1, source_target_pairs={{0,8},{8,16},{16,24},{24,32},{32,40},{40,48},{48,56},{56,64},{64,7... | collective-permute-start | bytes 49160 | tf_op jit(solution)/shard_map/ppermute | solution.py:362
  120.6 7.5 %collective-permute-start.7 = (f32[2,16,128]{2,1,0:T(8,128)S(1)}, f32[2,16,128]{2,1,0:T(8,128)S(1)}, u32[]{:S(2)}, u32[]{:S(2)}) collective-permute-start(f32[2,16,128]{2,1,0:T(8,128)S(1)} %get-tuple-element.76), channel_id=1, source_target_pairs={{0,248},{8,0},{16,8},{24,16},{32,24},{40,32},{48,40},{56,48},{64,5... | collective-permute-start | bytes 49160 | tf_op jit(solution)/shard_map/ppermute | solution.py:362
  139.5 2.0 %collective-permute-start.8 = (f32[1024,128]{1,0:T(8,128)S(1)}, f32[1024,128]{1,0:T(8,128)S(1)}, u32[]{:S(2)}, u32[]{:S(2)}) collective-permute-start(f32[1024,128]{1,0:T(8,128)S(1)} %bitcast.33), channel_id=1, source_target_pairs={{0,8},{8,0},{16,24},{24,16},{32,40},{40,32},{48,56},{56,48},{64,72... | collective-permute-start | bytes 1572872 | tf_op jit(solution)/shard_map/ppermute | solution.py:370

commit v3 on v2

--- a/solution.py
+++ b/solution.py
@@ -11,8 +11,11 @@
 KAPPA = 0.05
 SLOPE_C = 0.7978845608028654
 CUBIC = 0.044715
-ROWS = 32
+ROWS = 64
+LAST_ROWS = 32
+SUB = 256
 UNROLL = 16
+SAMPLES = 8192 * 128
 F32 = jnp.float32
 BF16 = jnp.bfloat16
 MIB = 1024 * 1024
@@ -216,21 +219,25 @@
 
     col = jnp.concatenate([cols[:, i, 0].reshape(128, 128) for i in range(CELLS)], 1)
     gcol = jnp.concatenate([cols[:, i, 1].reshape(128, 128) for i in range(CELLS)], 1)
-    nt = (((1,), (1,)), ((), ()))
     for h in range(0, hidden, HTILE):
         part = slice(h, h + HTILE)
-        z = jnp.dot(w_in_t[part, :], col, preferred_element_type=F32)
-        z2 = z * z
-        t = jnp.tanh(z * (z2 * (SLOPE_C * CUBIC) + SLOPE_C))
-        half = 0.5 * t + 0.5
-        slope = half + (1.0 - t * t) * (z * (z2 * (1.5 * SLOPE_C * CUBIC) + 0.5 * SLOPE_C))
-        act = (z * half).astype(BF16)
-        act_s[part, :] = act
-        d_act = jnp.dot(w_out_t[part, :], gcol, preferred_element_type=F32)
-        d_pre = (d_act * slope).astype(BF16)
-        dpre_s[part, :] = d_pre
-        grads[0, part, :] += lax.dot_general(d_pre, col, nt, preferred_element_type=F32)
-        grads[1, part, :] += lax.dot_general(act, gcol, nt, preferred_element_type=F32)
+        for n in range(0, CELLS * 128, SUB):
+            at = slice(n, n + SUB)
+            z = jnp.dot(w_in_t[part, :], col[:, at], preferred_element_type=F32)
+            d_act = jnp.dot(w_out_t[part, :], gcol[:, at], preferred_element_type=F32)
+            z2 = z * z
+            t = jnp.tanh(z * (z2 * (SLOPE_C * CUBIC) + SLOPE_C))
+            part_t = 0.5 * t
+            half = part_t + 0.5
+            act = z * half
+            slope = half + act * (0.5 - part_t) * (
+                z2 * (6.0 * SLOPE_C * CUBIC) + 2.0 * SLOPE_C
+            )
+            act_s[part, at] = act.astype(BF16)
+            dpre_s[part, at] = (d_act * slope).astype(BF16)
+    nt = (((1,), (1,)), ((), ()))
+    grads[0] += lax.dot_general(dpre_s[...], col, nt, preferred_element_type=F32)
+    grads[1] += lax.dot_general(act_s[...], gcol, nt, preferred_element_type=F32)
     tend = jnp.dot(w_out[...], act_s[...], preferred_element_type=F32).astype(BF16)
     d_cols = jnp.dot(w_in[...], dpre_s[...], preferred_element_type=F32).astype(BF16)
     for i in range(CELLS):
@@ -268,37 +275,60 @@
     )(in_hbm(cols), w_in_t, w_out_t, w_in, w_out, grads)
 
 
+def totals_kernel(core, mine, other, in_total, out_total):
+    scale = 1.0 / math.sqrt(SAMPLES)
+    first = core[0] == 0
+    for k in range(0, mine.shape[0], 128):
+        at = slice(k, k + 128)
+        here = mine[at, :].T
+        there = other[at, :].T
+        in_total[:, at] = jnp.where(first, here, there) * scale
+        out_total[:, at] = jnp.where(first, there, here) * scale
+
+
+def totals(core, mine, other):
+    spec = pl.BlockSpec(memory_space=pltpu.VMEM)
+    return pl.pallas_call(
+        totals_kernel,
+        in_specs=[pl.BlockSpec(memory_space=pltpu.SMEM), spec, spec],
+        out_specs=[spec] * 2,
+        out_shape=[jax.ShapeDtypeStruct(mine.shape[::-1], F32)] * 2,
+        name="weight_totals",
+    )(core, mine, other)
+
+
 def last_kernel(
-    first, first_next, back, back_next, speeds, inner, inner_next, outer, outer_next, low, high,
-    out, grad, q_s, g_s, flux_s, drift_s,
+    start, blocks, first, first_next, back, back_next, speeds, inner, inner_next, outer,
+    outer_next, west, low, high, *rest,
 ):
-    here = pl.program_id(0)
-    blocks = pl.num_programs(0)
-    inside = jnp.logical_and(here >= blocks // 4, here < blocks - blocks // 4)
+    out, grad, q_s, g_s, flux_s, drift_s = rest[-6:]
+    here = lax.rem(pl.program_id(0) + start, blocks)
+    quarter = blocks // 4
+
+    def within(block):
+        return jnp.logical_and(block >= quarter, block < blocks - quarter)
 
     def fill(fields):
-        def one(i, carry):
-            at = pl.ds(pl.multiple_of(i * 16, 16), 16)
+        for i in range(LAST_ROWS):
+            at = pl.ds(i * 16, 16)
             q_s[at, :] = first[i] + fields[i, 0].astype(F32)
             g_s[at, :] = back[i] + fields[i, 1].astype(F32)
-            return carry
-
-        lax.fori_loop(0, ROWS, one, 0, unroll=UNROLL)
-
-    pl.when(inside)(lambda: fill(inner))
-    pl.when(jnp.logical_not(inside))(lambda: fill(outer))
+
+    pl.when(within(here))(lambda: fill(inner))
+    pl.when(jnp.logical_not(within(here)))(lambda: fill(outer))
     last = here == blocks - 1
-    next_inside = jnp.logical_and(here + 1 >= blocks // 4, here + 1 < blocks - blocks // 4)
-    add = jnp.where(next_inside, inner_next[0].astype(F32), outer_next[0].astype(F32))
-    q_s[ROWS * 16 :, :] = jnp.where(last, high[0], first_next[0] + add[0])
-    g_s[ROWS * 16 :, :] = jnp.where(last, high[1], back_next[0] + add[1])
+    add = jnp.where(within(here + 1), inner_next[0].astype(F32), outer_next[0].astype(F32))
+    q_s[LAST_ROWS * 16 :, :] = jnp.where(last, high[0], first_next[0] + add[0])
+    g_s[LAST_ROWS * 16 :, :] = jnp.where(last, high[1], back_next[0] + add[1])
     q = row(q_s, 0)
     g = row(g_s, 0)
-    flux, drift = west_terms(low[0], q, low[1], g, low[2])
-    flux = jnp.where(here == 0, flux, flux_s[...])
-    drift = jnp.where(here == 0, drift, drift_s[...])
-    out2 = out.reshape(16 * ROWS, 128)
-    grad2 = grad.reshape(16 * ROWS, 128)
+    edge = jnp.where(here == 0, low[...], west[...])
+    flux, drift = west_terms(edge[0], q, edge[1], g, edge[2])
+    fresh = jnp.logical_or(here == 0, pl.program_id(0) == 0)
+    flux = jnp.where(fresh, flux, flux_s[...])
+    drift = jnp.where(fresh, drift, drift_s[...])
+    out2 = out.reshape(16 * LAST_ROWS, 128)
+    grad2 = grad.reshape(16 * LAST_ROWS, 128)
 
     def one(i, carry):
         q, g, flux, drift = carry
@@ -307,54 +337,69 @@
         e = speeds[i, 0].astype(F32)
         n = speeds[i, 1].astype(F32)
         moved, pulled, flux, drift = step_row(q, q_next, g, g_next, e, n, flux, drift)
-        put_rows(out2, i, ROWS, moved)
-        put_rows(grad2, i, ROWS, pulled)
+        put_rows(out2, i, LAST_ROWS, moved)
+        put_rows(grad2, i, LAST_ROWS, pulled)
         return q_next, g_next, flux, drift
 
-    carry = lax.fori_loop(0, ROWS, one, (q, g, flux, drift), unroll=UNROLL)
+    carry = lax.fori_loop(0, LAST_ROWS, one, (q, g, flux, drift), unroll=UNROLL)
     flux_s[...] = carry[2]
     drift_s[...] = carry[3]
 
 
-def last_step(first, back, speeds, inner, outer, low, high, shape):
+def last_step(start, count, first, back, speeds, inner, outer, west, low, high, shape, filled):
     width = shape[1]
-    blocks = width // ROWS
+    blocks = width // LAST_ROWS
     part = blocks // 4
     quarter = width // 4
-    held = lambda s: jnp.clip(s - part, 0, 2 * part - 1)
-    kept = lambda s: jnp.where(s < 3 * part, jnp.minimum(s + part, 2 * part - 1), s - 3 * part)
-    row_held = lambda r: jnp.clip(r - quarter, 0, 2 * quarter - 1)
-    row_kept = lambda r: jnp.where(
-        r < quarter, r + quarter, jnp.clip(r - 3 * quarter, 0, 2 * quarter - 1)
-    )
-    after = lambda s: jnp.minimum((s + 1) * ROWS, width - 1)
-    field = pl.BlockSpec((ROWS, 16, 128), lambda s: (s, 0, 0))
+    here = lambda s: lax.rem(s + start, blocks)
+
+    def held(s):
+        return jnp.clip(here(s) - part, 0, 2 * part - 1), 0, 0, 0
+
+    def kept(s):
+        b = here(s)
+        return jnp.where(b < 3 * part, jnp.minimum(b + part, 2 * part - 1), b - 3 * part), 0, 0, 0
+
+    after = lambda s: jnp.minimum((here(s) + 1) * LAST_ROWS, width - 1)
+
+    def held_next(s):
+        return jnp.clip(after(s) - quarter, 0, 2 * quarter - 1), 0, 0, 0
+
+    def kept_next(s):
+        r = after(s)
+        far = jnp.clip(r - 3 * quarter, 0, 2 * quarter - 1)
+        return jnp.where(r < quarter, r + quarter, far), 0, 0, 0
+
+    field = pl.BlockSpec((LAST_ROWS, 16, 128), lambda s: (here(s), 0, 0))
     field_next = pl.BlockSpec((1, 16, 128), lambda s: (after(s), 0, 0))
-    pair = lambda index: pl.BlockSpec((ROWS, 2, 16, 128), lambda s: (index(s), 0, 0, 0))
-    pair_next = lambda index: pl.BlockSpec(
-        (1, 2, 16, 128), lambda s: (index((s + 1) * ROWS), 0, 0, 0)
-    )
+    pair = lambda index: pl.BlockSpec((LAST_ROWS, 2, 16, 128), index)
+    pair_next = lambda index: pl.BlockSpec((1, 2, 16, 128), index)
     whole = lambda n: pl.BlockSpec((n, 16, 128), lambda s: (0, 0, 0))
-    result = pl.BlockSpec((16, ROWS, 128), lambda s: (0, s, 0))
+    result = pl.BlockSpec((16, LAST_ROWS, 128), lambda s: (0, here(s), 0))
+    cells = count * LAST_ROWS * shape[0] * shape[2]
     return pl.pallas_call(
-        last_kernel,
-        grid=(blocks,),
+        functools.partial(last_kernel, start, blocks),
+        grid=(count,),
         in_specs=[
-            field, field_next, field, field_next, pair(lambda s: s),
-            pair(held), pair_next(row_held), pair(kept), pair_next(row_kept), whole(3), whole(2),
-        ],
+            field, field_next, field, field_next, pair(lambda s: (here(s), 0, 0, 0)),
+            pair(held), pair_next(held_next), pair(kept), pair_next(kept_next),
+            whole(3), whole(3), whole(2),
+        ]
+        + [pl.BlockSpec(memory_space=pl.ANY)] * len(filled),
         out_specs=[result] * 2,
         out_shape=[pltpu.HBM(shape, F32)] * 2,
-        scratch_shapes=[pltpu.VMEM(((ROWS + 1) * 16, 128), F32)] * 2
+        input_output_aliases={12 + k: k for k in range(len(filled))},
+        scratch_shapes=[pltpu.VMEM(((LAST_ROWS + 1) * 16, 128), F32)] * 2
         + [pltpu.VMEM((16, 128), F32)] * 2,
         compiler_params=pltpu.CompilerParams(vmem_limit_bytes=16 * MIB),
         cost_estimate=pl.CostEstimate(
-            flops=shape[0] * shape[1] * shape[2] * 40,
-            bytes_accessed=shape[0] * shape[1] * shape[2] * 24,
-            transcendentals=0,
+            flops=cells * 40, bytes_accessed=cells * 24, transcendentals=0
         ),
         name="transport_two",
-    )(*[in_hbm(x) for x in (first, first, back, back, speeds, inner, inner, outer, outer)], low, high)
+    )(
+        *[in_hbm(x) for x in (first, first, back, back, speeds, inner, inner, outer, outer)],
+        west, low, high, *filled,
+    )
 
 
 def shift(block, distance):
@@ -405,43 +450,52 @@
     none = jnp.zeros((3, 16, 128), F32)
     half = blocks // 2
     fields_in = (state_in, east_speed, north_speed, cotangent)
-    *held, cols_a = first_step(blocks // 4, half, *fields_in, none, none[:2], ())
-    cols_a, low, high = barrier((cols_a, low, high))
+    first, back, speeds, cols_a = first_step(3 * blocks // 4, half, *fields_in, low, high, ())
     got_a = exchange(cols_a.reshape(8, width // 16, 2, 16, 128))
-    first, back, speeds, cols_b = first_step(3 * blocks // 4, half, *fields_in, low, high, held)
+    held = (first, back, speeds)
+    first, back, speeds, cols_b = first_step(
+        blocks // 4, half, *fields_in, none, none[:2], held
+    )
     got_b = exchange(cols_b.reshape(8, width // 16, 2, 16, 128))
     zero = jnp.zeros((2, hidden, 128), F32)
-    fields_a, grads = network(got_a, w_in_t, w_out_t, w_in, w_out, zero)
-    fields_a = exchange(fields_a)
-    fields_b, grads = network(got_b, w_in_t, w_out_t, w_in, w_out, grads)
-    grads, fields_a = barrier((grads, fields_a))
-    part = chip_sum(grads)
+    outer, grads = network(got_a, w_in_t, w_out_t, w_in, w_out, zero)
+    outer = exchange(outer)
+    inner, grads = network(got_b, w_in_t, w_out_t, w_in, w_out, grads)
+    part, outer = barrier((chip_sum(grads), outer))
+    outer = outer.reshape(width // 2, 2, 16, 128)
+    quarter = width // 4
+
+    def edge(row):
+        fields = outer[(row + quarter) % width]
+        return jnp.stack([first[row], back[row]]) + fields.astype(F32)
+
+    def west(row):
+        return jnp.concatenate([edge(row), speeds[row, 0][None].astype(F32)])
+
+    part, tail, head = barrier((part, edge(width - 1), edge(0)))
     part = jnp.sum(exchange_rows(part.reshape(32, hidden // 32, 128)), 0)
-    part, fields_b = barrier((part, fields_b))
-    fields_b = exchange(fields_b)
+    low_next = jnp.concatenate([shift(tail, 1), low[2:]])
+    high_next = shift(head, -1)
+    part, inner, low_next, high_next = barrier((part, inner, low_next, high_next))
+    inner = exchange(inner).reshape(width // 2, 2, 16, 128)
+    fields_held = (first, back, speeds)
+    shape = state_in.shape
+    ends = shape[1] // LAST_ROWS
+    results = last_step(
+        ends - 1, 2, *fields_held, outer, outer, west(width - 1 - LAST_ROWS), low_next,
+        high_next, shape, (),
+    )
     part = z_sum(part)
-    part, fields_b = barrier((part, fields_b))
-    inner = fields_a.reshape(width // 2, 2, 16, 128)
-    outer = fields_b.reshape(width // 2, 2, 16, 128)
-    quarter = width // 4
-
-    def edge(row, i):
-        return jnp.stack([first[row], back[row]]) + outer[i].astype(F32)
-
-    second_low = shift(edge(width - 1, quarter - 1), 1)
-    second_high = shift(edge(0, quarter), -1)
-    lows = jnp.concatenate([second_low, low[2:]])
+    part, inner, *results = barrier((part, inner, *results))
     part = exchange_rows(jnp.broadcast_to(part[None], (32,) + part.shape)).reshape(hidden, 128)
     state_out, state_grad = last_step(
-        first, back, speeds, inner, outer, lows, second_high, state_in.shape
+        1, ends - 2, *fields_held, inner, outer, west(LAST_ROWS - 1), low_next, high_next,
+        shape, results,
     )
     part, state_out, state_grad = barrier((part, state_out, state_grad))
-    other = partner(part, 1)
     core = lax.rem(lax.axis_index("tile"), 2)
-    in_total = jnp.where(core == 0, part, other)
-    out_total = jnp.where(core == 0, other, part)
-    scale = 1.0 / math.sqrt(lax.axis_size("tile") * width * state_in.shape[2])
-    return state_out, state_grad, in_total.T * scale, out_total.T * scale
+    in_total, out_total = totals(core.reshape(1), part, partner(part, 1))
+    return state_out, state_grad, in_total, out_total
 
 
 def solution(mesh):

time: 145 us -> 141 us (0.972)
  blocking collectives: 20.5 us -> 0 us
  starting transfers between devices: 49 us -> 56 us
  waiting for transfers between devices: 20.8 us -> 26 us
  Pallas kernels: 47.1 us -> 49.4 us
  other arithmetic: 0.19 us -> 2.39 us
    all_to_all x1 -> x0, blocking collectives: 20.5 us -> none  [exchange_rows(): lax.all_to_all(block, ('tile', 'lev'), split_axis=0, concat_axis=0, tiled...]
    all_to_all x1 -> x2, starting transfers between devices: 7.64 us -> 15.3 us  [exchange_rows(): lax.all_to_all(block, ('tile', 'lev'), split_axis=0, concat_axis=0, tiled...]
    ppermute x4, waiting for transfers between devices: 1.53 us -> 6.67 us  [shift(): lax.ppermute(block, 'tile', [(i, (i + distance) % count) for i in range(c...]
    ppermute x5, waiting for transfers between devices: 11.8 us -> 7.28 us  [partner(): lax.ppermute(block, 'tile', [(i, i ^ mask) for i in range(lax.axis_size('...]
    pallas_call x1 -> x3, Pallas kernels: 11.4 us -> 15.6 us  [the longest x2 13.1 us: last_step(): pl.pallas_call(functools.partial(last_kernel, start, blocks), grid=(count...]
    all_to_all x4, waiting for transfers between devices: 7.45 us -> 10.8 us  [exchange(): return lax.all_to_all(block, 'lev', split_axis=0, concat_axis=0, tiled=True)]
    unnamed x14 -> x16, local copies, waits for them, and re-layouts: 3.31 us -> 2.13 us
  transfers between devices with their start and end apart: 14 -> 15, of which waited for: 8 -> 12; matrix products, arithmetic and copies ran while one was open for 1% -> 2% of each run, Pallas kernels for 32% -> 28%
where the time goes in v3:
time: 141 us; the launch traced here: 139 us
  starting transfers between devices  56 us (40%)
  Pallas kernels  49.4 us (35%)
  waiting for transfers between devices  26 us (18%)
  local copies, waits for them, and re-layouts  3.99 us (3%)
  other arithmetic  2.39 us (2%)
    pallas_call x2, Pallas kernels, network(): pl.pallas_call(functools.partial(network_kernel), grid=(rows // CELLS,),...  20.1 us
    all_to_all x4, starting transfers between devices, exchange(): return lax.all_to_all(block, 'lev', split_axis=0, concat_axis=0, tiled=True)  19.7 us
    all_to_all x2, starting transfers between devices, exchange_rows(): lax.all_to_all(block, ('tile', 'lev'), split_axis=0, concat_axis=0, tiled...  15.3 us
    ppermute x4, starting transfers between devices, shift(): lax.ppermute(block, 'tile', [(i, (i + distance) % count) for i in range(c...  14.2 us
    pallas_call x2, Pallas kernels, last_step(): pl.pallas_call(functools.partial(last_kernel, start, blocks), grid=(count...  13.1 us
    pallas_call x2, Pallas kernels, first_step(): pl.pallas_call(functools.partial(first_kernel, start, blocks), grid=(coun...  12 us
    all_to_all x4, waiting for transfers between devices, exchange(): return lax.all_to_all(block, 'lev', split_axis=0, concat_axis=0, tiled=True)  10.8 us
    ppermute x5, waiting for transfers between devices, partner(): lax.ppermute(block, 'tile', [(i, i ^ mask) for i in range(lax.axis_size('...  7.28 us
  transfers between devices with their start and end apart: 15, of which 12 were waited for; matrix products, arithmetic and copies ran while one was open for 2% of the time, Pallas kernels for 28%

profile of v3, /device:TPU:2, one launch (start us, length us, event | category | flops | bytes accessed | tf_op | source)
XLA Modules:
  0.0 138.6 jit_solution(14207209186797599446)
XLA Ops:
  0.6 1.6 %edge_rows.1 = (f32[3,16,128]{2,1,0:T(8,128)}, f32[2,16,128]{2,1,0:T(8,128)}) custom-call(f32[16,256,128]{2,1,0:T(8,128)} %state_next.1, f32[16,256,128]{2,1,0:T(8,128)} %state_next.1, f32[16,256,128]{2,1,0:T(8,128)} %cot_next.3, f32[16,256,128]{2,1,0:T(8,128)} %cot_next.3, bf16[16,256,128]{2,1,0:T(8,128)(2,1)} %east_prev.3), custom_call_target="tpu_custom_call" | custom-call | tf_op jit(solution)/shard_map/edge_rows/pallas_call | solution.py:193
  2.2 0.0 collective-permute-start
  2.2 8.2 %collective-permute-start.1 = (f32[2,16,128]{2,1,0:T(8,128)}, f32[2,16,128]{2,1,0:T(8,128)S(1)}, u32[]{:S(2)}, u32[]{:S(2)}) collective-permute-start(f32[2,16,128]{2,1,0:T(8,128)} %get-tuple-element.47), channel_id=1, source_target_pairs={{0,248},{8,0},{16,8},{24,16},{32,24},{40,32},{48,40},{56,48},{64,5... | collective-permute-start | bytes 49160 | tf_op jit(solution)/shard_map/ppermute | solution.py:407
  10.4 1.7 %collective-permute-done.1.high = f32[2,16,128]{2,1,0:T(8,128)S(1)} collective-permute-done((f32[2,16,128]{2,1,0:T(8,128)}, f32[2,16,128]{2,1,0:T(8,128)S(1)}, u32[]{:S(2)}, u32[]{:S(2)}) %collective-permute-start.1) | collective-permute-done | bytes 16416 | tf_op jit(solution)/shard_map/ppermute | solution.py:407
  12.1 0.1 collective-permute-done.low
  12.2 6.0 %transport_one.2 = (f32[256,16,128]{2,1,0:T(8,128)}, f32[256,16,128]{2,1,0:T(8,128)}, bf16[256,2,16,128]{3,2,1,0:T(8,128)(2,1)}, bf16[128,2,16,128]{3,2,1,0:T(8,128)(2,1)}) custom-call(f32[16,256,128]{2,1,0:T(8,128)} %state_next.1, f32[16,256,128]{2,1,0:T(8,128)} %state_next.1, f32[16,256,128]{2,1,0:T(8,128)} %state_next.1, f32[16,256,128]{2,1,0:T(8,128)} %cot_next.3, ...), custom_call_target="tpu_custom_call" | custom-call | flops 10485760 | bytes 7340032 | tf_op jit(solution)/shard_map/transport_one/pallas_call | solution.py:143
  18.1 5.3 %all-to-all-start.1 = ((bf16[8,16,2,16,128]{4,3,2,1,0:T(8,128)(2,1)}), bf16[8,16,2,16,128]{4,3,2,1,0:T(8,128)(2,1)S(1)}, u32[]{:S(2)}, u32[]{:S(2)}) async-start(bf16[8,16,2,16,128]{4,3,2,1,0:T(8,128)(2,1)} %bitcast.48), calls=%async_computation.1 | async-start | bytes 2097152 | tf_op jit(solution)/shard_map/all_to_all | solution.py:411
  23.4 6.0 %transport_one.3 = (f32[256,16,128]{2,1,0:T(8,128)}, f32[256,16,128]{2,1,0:T(8,128)}, bf16[256,2,16,128]{3,2,1,0:T(8,128)(2,1)}, bf16[128,2,16,128]{3,2,1,0:T(8,128)(2,1)}) custom-call(f32[16,256,128]{2,1,0:T(8,128)} %state_next.1, f32[16,256,128]{2,1,0:T(8,128)} %state_next.1, ...), custom_call_target="tpu_custom_call", output_to_operand_aliasing={{0}: (11, {}), {1}: (12, {}), {2}: (13, {})} | custom-call | flops 10485760 | bytes 7340032 | tf_op jit(solution)/shard_map/transport_one/pallas_call | solution.py:143
  29.5 0.0 copy-start
  29.5 0.0 copy-start.1
  29.5 6.7 %all-to-all-done.1.cols = bf16[8,16,2,16,128]{4,3,2,1,0:T(8,128)(2,1)S(1)} async-done(((bf16[8,16,2,16,128]{4,3,2,1,0:T(8,128)(2,1)}), bf16[8,16,2,16,128]{4,3,2,1,0:T(8,128)(2,1)S(1)}, u32[]{:S(2)}, u32[]{:S(2)}) %all-to-all-start.1) | async-done | bytes 1048608 | tf_op jit(solution)/shard_map/all_to_all | solution.py:411
  36.2 0.0 copy-start.5
  36.2 1.0 copy-done.5
  37.2 4.8 %all-to-all-start = ((bf16[8,16,2,16,128]{4,3,2,1,0:T(8,128)(2,1)}), bf16[8,16,2,16,128]{4,3,2,1,0:T(8,128)(2,1)S(1)}, u32[]{:S(2)}, u32[]{:S(2)}) async-start(bf16[8,16,2,16,128]{4,3,2,1,0:T(8,128)(2,1)} %bitcast.47), calls=%async_computation | async-start | bytes 2097152 | tf_op jit(solution)/shard_map/all_to_all | solution.py:411
  42.0 0.0 copy-done
  42.0 0.2 copy.15
  42.1 0.0 copy-done.1
  42.1 0.2 copy.16
  42.3 0.1 broadcast_in_dim.13.before
  42.4 10.1 %column_network.2 = (bf16[8,16,2,16,128]{4,3,2,1,0:T(8,128)(2,1)}, f32[2,1024,128]{2,1,0:T(8,128)S(1)}) custom-call(bf16[8,16,2,16,128]{4,3,2,1,0:T(8,128)(2,1)} %copy-done.5, bf16[1024,128]{1,0:T(8,128)(2,1)S(1)} %bitcast.39, bf16[1024,128]{1,0:T(8,128)(2,1)S(1)} %bitcast.41, bf16[128,1024]{1,0:T(8,128)(2,1)S(1)} %copy-done, ...), custom_call_target="tpu_custom_call" | custom-call | flops 3221225472 | bytes 2097152 | tf_op jit(solution)/shard_map/column_network/pallas_call | solution.py:255
  52.5 3.3 %all-to-all-done.cols = bf16[8,16,2,16,128]{4,3,2,1,0:T(8,128)(2,1)S(1)} async-done(((bf16[8,16,2,16,128]{4,3,2,1,0:T(8,128)(2,1)}), bf16[8,16,2,16,128]{4,3,2,1,0:T(8,128)(2,1)S(1)}, u32[]{:S(2)}, u32[]{:S(2)}) %all-to-all-start) | async-done | bytes 1048608 | tf_op jit(solution)/shard_map/all_to_all | solution.py:411
  55.8 0.0 copy-start.4
  55.8 5.3 %all-to-all-start.2 = ((bf16[8,16,2,16,128]{4,3,2,1,0:T(8,128)(2,1)}), bf16[8,16,2,16,128]{4,3,2,1,0:T(8,128)(2,1)}, u32[]{:S(2)}, u32[]{:S(2)}) async-start(bf16[8,16,2,16,128]{4,3,2,1,0:T(8,128)(2,1)} %get-tuple-element.55), calls=%async_computation.2 | async-start | bytes 2097152 | tf_op jit(solution)/shard_map/all_to_all | solution.py:411
  61.1 0.0 copy-done.4
  61.1 10.1 %column_network.3 = (bf16[8,16,2,16,128]{4,3,2,1,0:T(8,128)(2,1)}, f32[2,1024,128]{2,1,0:T(8,128)S(1)}) custom-call(bf16[8,16,2,16,128]{4,3,2,1,0:T(8,128)(2,1)} %copy-done.4, bf16[1024,128]{1,0:T(8,128)(2,1)S(1)} %bitcast.40, bf16[1024,128]{1,0:T(8,128)(2,1)S(1)} %bitcast.42, bf16[128,1024]{1,0:T(8,128)(2,1)S(1)} %copy-done, ...), custom_call_target="tpu_custom_call" | custom-call | flops 3221225472 | bytes 2097152 | tf_op jit(solution)/shard_map/column_network/pallas_call | solution.py:255
  71.2 0.3 collective-permute-start.2
  71.5 0.8 fusion
  72.3 1.1 collective-permute-done.2
  73.4 0.8 bitcast_add_fusion
  74.2 0.7 all-to-all-done.2
  74.9 0.8 maximum_add_fusion.3
  75.7 7.7 %all-to-all-start.3 = ((f32[32,32,128]{2,1,0:T(8,128)}), f32[32,32,128]{2,1,0:T(8,128)S(1)}, u32[]{:S(2)}, u32[]{:S(2)}) async-start(f32[32,32,128]{2,1,0:T(8,128)} %bitcast.9), calls=%async_computation.3 | async-start | bytes 1048576 | tf_op jit(solution)/shard_map/all_to_all | solution.py:430
  83.4 0.1 collective-permute-start.3
  83.5 5.9 %collective-permute-start.4 = (f32[2,16,128]{2,1,0:T(8,128)S(1)}, f32[2,16,128]{2,1,0:T(8,128)S(1)}, u32[]{:S(2)}, u32[]{:S(2)}) collective-permute-start(f32[2,16,128]{2,1,0:T(8,128)S(1)} %get-tuple-element.63), channel_id=1, source_target_pairs={{0,248},{8,0},{16,8},{24,16},{32,24},{40,32},{48,40},{56,48},{64,5... | collective-permute-start | bytes 49160 | tf_op jit(solution)/shard_map/ppermute | solution.py:407
  89.4 5.0 %collective-permute-done.3 = f32[2,16,128]{2,1,0:T(8,128)S(1)} collective-permute-done((f32[2,16,128]{2,1,0:T(8,128)S(1)}, f32[2,16,128]{2,1,0:T(8,128)S(1)}, u32[]{:S(2)}, u32[]{:S(2)}) %collective-permute-start.3) | collective-permute-done | bytes 16416 | tf_op jit(solution)/shard_map/ppermute | solution.py:407
  94.4 0.4 all-to-all-done.3
  94.8 0.0 collective-permute-done.4.high
  94.9 4.3 %all-to-all-start.4 = ((bf16[8,16,2,16,128]{4,3,2,1,0:T(8,128)(2,1)}), bf16[8,16,2,16,128]{4,3,2,1,0:T(8,128)(2,1)S(1)}, u32[]{:S(2)}, u32[]{:S(2)}) async-start(bf16[8,16,2,16,128]{4,3,2,1,0:T(8,128)(2,1)} %get-tuple-element.65), calls=%async_computation.4 | async-start | bytes 2097152 | tf_op jit(solution)/shard_map/all_to_all | solution.py:411
  99.2 0.7 bitcast_convert_fusion
  99.9 2.9 %collective-permute-start.7 = (f32[32,128]{1,0:T(8,128)S(1)}, f32[32,128]{1,0:T(8,128)S(1)}, u32[]{:S(2)}, u32[]{:S(2)}) collective-permute-start(f32[32,128]{1,0:T(8,128)S(1)} %reduce_sum.9), channel_id=1, source_target_pairs={{0,48},{8,56},{16,32},{24,40},{32,16},{40,24},{48,0},{56,8},{64,11... | collective-permute-start | bytes 49160 | tf_op jit(solution)/shard_map/ppermute | solution.py:415
  102.8 1.6 %collective-permute-start.6 = (f32[32,128]{1,0:T(8,128)S(1)}, f32[32,128]{1,0:T(8,128)S(1)}, u32[]{:S(2)}, u32[]{:S(2)}) collective-permute-start(f32[32,128]{1,0:T(8,128)S(1)} %reduce_sum.9), channel_id=1, source_target_pairs={{0,32},{8,40},{16,48},{24,56},{32,0},{40,8},{48,16},{56,24},{64,96... | collective-permute-start | bytes 49160 | tf_op jit(solution)/shard_map/ppermute | solution.py:415
  104.4 2.0 %collective-permute-start.5 = (f32[32,128]{1,0:T(8,128)S(1)}, f32[32,128]{1,0:T(8,128)S(1)}, u32[]{:S(2)}, u32[]{:S(2)}) collective-permute-start(f32[32,128]{1,0:T(8,128)S(1)} %reduce_sum.9), channel_id=1, source_target_pairs={{0,16},{8,24},{16,0},{24,8},{32,48},{40,56},{48,32},{56,40},{64,80... | collective-permute-start | bytes 49160 | tf_op jit(solution)/shard_map/ppermute | solution.py:415
  106.4 4.1 %transport_two.2 = (f32[16,256,128]{2,1,0:T(8,128)}, f32[16,256,128]{2,1,0:T(8,128)}) custom-call(f32[256,16,128]{2,1,0:T(8,128)} %get-tuple-element.57.first.first_next, f32[256,16,128]{2,1,0:T(8,128)} %get-tuple-element.57.first.first_next, f32[256,16,128]{2,1,0:T(8,128)} %get-tuple-element.58.back.back_next, ...), custom_call_target="tpu_custom_call" | custom-call | flops 5242880 | bytes 3145728 | tf_op jit(solution)/shard_map/transport_two/pallas_call | solution.py:380
  110.5 3.2 %collective-permute-done.7 = f32[32,128]{1,0:T(8,128)S(1)} collective-permute-done((f32[32,128]{1,0:T(8,128)S(1)}, f32[32,128]{1,0:T(8,128)S(1)}, u32[]{:S(2)}, u32[]{:S(2)}) %collective-permute-start.7) | collective-permute-done | bytes 16416 | tf_op jit(solution)/shard_map/ppermute | solution.py:415
  113.7 1.1 collective-permute-done.6
  114.8 0.0 collective-permute-done.5
  114.8 0.0 all-to-all-done.4
  114.8 0.0 copy-start.2
  114.8 0.9 broadcast_in_dim.14
  115.8 7.7 %all-to-all-start.5 = ((f32[32,32,128]{2,1,0:T(8,128)}), f32[32,32,128]{2,1,0:T(8,128)S(1)}, u32[]{:S(2)}, u32[]{:S(2)}) async-start(f32[32,32,128]{2,1,0:T(8,128)} %broadcast_in_dim.14), calls=%async_computation.5 | async-start | bytes 1048576 | tf_op jit(solution)/shard_map/all_to_all | solution.py:430
  123.4 0.0 copy-done.2
  123.5 9.0 %transport_two.3 = (f32[16,256,128]{2,1,0:T(8,128)}, f32[16,256,128]{2,1,0:T(8,128)}) custom-call(f32[256,16,128]{2,1,0:T(8,128)} %get-tuple-element.57.first.first_next, f32[256,16,128]{2,1,0:T(8,128)} %get-tuple-element.57.first.first_next, f32[256,16,128]{2,1,0:T(8,128)} %get-tuple-element.58.back.back_next, ...), custom_call_target="tpu_custom_call", output_to_operand_aliasing={{0}: (12, {}), {1}: (13, {})} | custom-call | flops 15728640 | bytes 9437184 | tf_op jit(solution)/shard_map/transport_two/pallas_call | solution.py:380
  132.5 0.9 all-to-all-done.5
  133.4 0.0 copy-start.3
  133.4 0.0 collective-permute-start.8
  133.4 1.9 %collective-permute-done.8.other = f32[1024,128]{1,0:T(8,128)S(1)} collective-permute-done((f32[1024,128]{1,0:T(8,128)S(1)}, f32[1024,128]{1,0:T(8,128)S(1)}, u32[]{:S(2)}, u32[]{:S(2)}) %collective-permute-start.8) | collective-permute-done | bytes 524320 | tf_op jit(solution)/shard_map/ppermute | solution.py:415
  135.3 0.0 copy-start.6
  135.3 0.0 copy-done.3
  135.3 0.8 copy-done.6
  136.1 2.5 %weight_totals.1 = (f32[128,1024]{1,0:T(8,128)}, f32[128,1024]{1,0:T(8,128)}) custom-call(s32[1]{0:T(128)} %bitcast.16.core, f32[1024,128]{1,0:T(8,128)} %bitcast.46, f32[1024,128]{1,0:T(8,128)} %copy-done.6), custom_call_target="tpu_custom_call" | custom-call | tf_op jit(solution)/shard_map/weight_totals/pallas_call | solution.py:291
  (9 shorter events, 0.1 us)
Async XLA Ops:
  2.2 9.9 %collective-permute-start = (f32[3,16,128]{2,1,0:T(8,128)}, f32[3,16,128]{2,1,0:T(8,128)S(1)}, u32[]{:S(2)}, u32[]{:S(2)}) collective-permute-start(f32[3,16,128]{2,1,0:T(8,128)} %get-tuple-element.46), channel_id=1, source_target_pairs={{0,8},{8,16},{16,24},{24,32},{32,40},{40,48},{48,56},{56,64},{64,7... | collective-permute-start | bytes 73736 | tf_op jit(solution)/shard_map/ppermute | solution.py:407
  2.2 9.8 %collective-permute-start.1 = (f32[2,16,128]{2,1,0:T(8,128)}, f32[2,16,128]{2,1,0:T(8,128)S(1)}, u32[]{:S(2)}, u32[]{:S(2)}) collective-permute-start(f32[2,16,128]{2,1,0:T(8,128)} %get-tuple-element.47), channel_id=1, source_target_pairs={{0,248},{8,0},{16,8},{24,16},{32,24},{40,32},{48,40},{56,48},{64,5... | collective-permute-start | bytes 49160 | tf_op jit(solution)/shard_map/ppermute | solution.py:407
  18.1 18.0 %all-to-all-start.1 = ((bf16[8,16,2,16,128]{4,3,2,1,0:T(8,128)(2,1)}), bf16[8,16,2,16,128]{4,3,2,1,0:T(8,128)(2,1)S(1)}, u32[]{:S(2)}, u32[]{:S(2)}) async-start(bf16[8,16,2,16,128]{4,3,2,1,0:T(8,128)(2,1)} %bitcast.48), calls=%async_computation.1 | async-start | bytes 2097152 | tf_op jit(solution)/shard_map/all_to_all | solution.py:411
  29.5 12.5 %copy-start = (bf16[128,1024]{1,0:T(8,128)(2,1)S(1)}, bf16[128,1024]{1,0:T(8,128)(2,1)}, u32[]{:S(2)}) copy-start(bf16[128,1024]{1,0:T(8,128)(2,1)} %w_in.3) | copy-start | bytes 786436
  29.5 12.7 %copy-start.1 = (bf16[128,1024]{1,0:T(8,128)(2,1)S(1)}, bf16[128,1024]{1,0:T(8,128)(2,1)}, u32[]{:S(2)}) copy-start(bf16[128,1024]{1,0:T(8,128)(2,1)} %w_out.3) | copy-start | bytes 786436
  36.2 1.0 copy-start.5
  37.2 18.6 %all-to-all-start = ((bf16[8,16,2,16,128]{4,3,2,1,0:T(8,128)(2,1)}), bf16[8,16,2,16,128]{4,3,2,1,0:T(8,128)(2,1)S(1)}, u32[]{:S(2)}, u32[]{:S(2)}) async-start(bf16[8,16,2,16,128]{4,3,2,1,0:T(8,128)(2,1)} %bitcast.47), calls=%async_computation | async-start | bytes 2097152 | tf_op jit(solution)/shard_map/all_to_all | solution.py:411
  55.8 5.3 %copy-start.4 = (bf16[8,16,2,16,128]{4,3,2,1,0:T(8,128)(2,1)}, bf16[8,16,2,16,128]{4,3,2,1,0:T(8,128)(2,1)S(1)}, u32[]{:S(2)}) copy-start(bf16[8,16,2,16,128]{4,3,2,1,0:T(8,128)(2,1)S(1)} %all-to-all-done.cols) | copy-start | bytes 3145732
  55.8 19.2 %all-to-all-start.2 = ((bf16[8,16,2,16,128]{4,3,2,1,0:T(8,128)(2,1)}), bf16[8,16,2,16,128]{4,3,2,1,0:T(8,128)(2,1)}, u32[]{:S(2)}, u32[]{:S(2)}) async-start(bf16[8,16,2,16,128]{4,3,2,1,0:T(8,128)(2,1)} %get-tuple-element.55), calls=%async_computation.2 | async-start | bytes 2097152 | tf_op jit(solution)/shard_map/all_to_all | solution.py:411
  71.2 2.2 %collective-permute-start.2 = (f32[1024,128]{1,0:T(8,128)S(1)}, f32[1024,128]{1,0:T(8,128)S(1)}, u32[]{:S(2)}, u32[]{:S(2)}) collective-permute-start(f32[1024,128]{1,0:T(8,128)S(1)} %dynamic-slice_bitcast_fusion), channel_id=1, source_target_pairs={{0,8},{8,0},{16,24},{24,16},{32,40},{40,32},{48,56},{56,48},{64,72... | collective-permute-start | bytes 1572872 | tf_op jit(solution)/shard_map/ppermute | solution.py:415
  75.7 19.1 %all-to-all-start.3 = ((f32[32,32,128]{2,1,0:T(8,128)}), f32[32,32,128]{2,1,0:T(8,128)S(1)}, u32[]{:S(2)}, u32[]{:S(2)}) async-start(f32[32,32,128]{2,1,0:T(8,128)} %bitcast.9), calls=%async_computation.3 | async-start | bytes 1048576 | tf_op jit(solution)/shard_map/all_to_all | solution.py:430
  83.4 11.0 %collective-permute-start.3 = (f32[2,16,128]{2,1,0:T(8,128)S(1)}, f32[2,16,128]{2,1,0:T(8,128)S(1)}, u32[]{:S(2)}, u32[]{:S(2)}) collective-permute-start(f32[2,16,128]{2,1,0:T(8,128)S(1)} %get-tuple-element.62), channel_id=1, source_target_pairs={{0,8},{8,16},{16,24},{24,32},{32,40},{40,48},{48,56},{56,64},{64,7... | collective-permute-start | bytes 49160 | tf_op jit(solution)/shard_map/ppermute | solution.py:407
  83.5 11.4 %collective-permute-start.4 = (f32[2,16,128]{2,1,0:T(8,128)S(1)}, f32[2,16,128]{2,1,0:T(8,128)S(1)}, u32[]{:S(2)}, u32[]{:S(2)}) collective-permute-start(f32[2,16,128]{2,1,0:T(8,128)S(1)} %get-tuple-element.63), channel_id=1, source_target_pairs={{0,248},{8,0},{16,8},{24,16},{32,24},{40,32},{48,40},{56,48},{64,5... | collective-permute-start | bytes 49160 | tf_op jit(solution)/shard_map/ppermute | solution.py:407
  94.9 20.0 %all-to-all-start.4 = ((bf16[8,16,2,16,128]{4,3,2,1,0:T(8,128)(2,1)}), bf16[8,16,2,16,128]{4,3,2,1,0:T(8,128)(2,1)S(1)}, u32[]{:S(2)}, u32[]{:S(2)}) async-start(bf16[8,16,2,16,128]{4,3,2,1,0:T(8,128)(2,1)} %get-tuple-element.65), calls=%async_computation.4 | async-start | bytes 2097152 | tf_op jit(solution)/shard_map/all_to_all | solution.py:411
  99.9 13.8 %collective-permute-start.7 = (f32[32,128]{1,0:T(8,128)S(1)}, f32[32,128]{1,0:T(8,128)S(1)}, u32[]{:S(2)}, u32[]{:S(2)}) collective-permute-start(f32[32,128]{1,0:T(8,128)S(1)} %reduce_sum.9), channel_id=1, source_target_pairs={{0,48},{8,56},{16,32},{24,40},{32,16},{40,24},{48,0},{56,8},{64,11... | collective-permute-start | bytes 49160 | tf_op jit(solution)/shard_map/ppermute | solution.py:415
  102.8 12.0 %collective-permute-start.6 = (f32[32,128]{1,0:T(8,128)S(1)}, f32[32,128]{1,0:T(8,128)S(1)}, u32[]{:S(2)}, u32[]{:S(2)}) collective-permute-start(f32[32,128]{1,0:T(8,128)S(1)} %reduce_sum.9), channel_id=1, source_target_pairs={{0,32},{8,40},{16,48},{24,56},{32,0},{40,8},{48,16},{56,24},{64,96... | collective-permute-start | bytes 49160 | tf_op jit(solution)/shard_map/ppermute | solution.py:415
  104.4 10.4 %collective-permute-start.5 = (f32[32,128]{1,0:T(8,128)S(1)}, f32[32,128]{1,0:T(8,128)S(1)}, u32[]{:S(2)}, u32[]{:S(2)}) collective-permute-start(f32[32,128]{1,0:T(8,128)S(1)} %reduce_sum.9), channel_id=1, source_target_pairs={{0,16},{8,24},{16,0},{24,8},{32,48},{40,56},{48,32},{56,40},{64,80... | collective-permute-start | bytes 49160 | tf_op jit(solution)/shard_map/ppermute | solution.py:415
  114.8 8.6 %copy-start.2 = (bf16[8,16,2,16,128]{4,3,2,1,0:T(8,128)(2,1)}, bf16[8,16,2,16,128]{4,3,2,1,0:T(8,128)(2,1)S(1)}, u32[]{:S(2)}) copy-start(bf16[8,16,2,16,128]{4,3,2,1,0:T(8,128)(2,1)S(1)} %all-to-all-done.4) | copy-start | bytes 3145732
  115.8 17.6 %all-to-all-start.5 = ((f32[32,32,128]{2,1,0:T(8,128)}), f32[32,32,128]{2,1,0:T(8,128)S(1)}, u32[]{:S(2)}, u32[]{:S(2)}) async-start(f32[32,32,128]{2,1,0:T(8,128)} %broadcast_in_dim.14), calls=%async_computation.5 | async-start | bytes 1048576 | tf_op jit(solution)/shard_map/all_to_all | solution.py:430
  133.4 1.9 %copy-start.3 = (f32[32,32,128]{2,1,0:T(8,128)}, f32[32,32,128]{2,1,0:T(8,128)S(1)}, u32[]{:S(2)}) copy-start(f32[32,32,128]{2,1,0:T(8,128)S(1)} %all-to-all-done.5) | copy-start | bytes 1572868
  133.4 1.9 %collective-permute-start.8 = (f32[1024,128]{1,0:T(8,128)S(1)}, f32[1024,128]{1,0:T(8,128)S(1)}, u32[]{:S(2)}, u32[]{:S(2)}) collective-permute-start(f32[1024,128]{1,0:T(8,128)S(1)} %bitcast.45), channel_id=1, source_target_pairs={{0,8},{8,0},{16,24},{24,16},{32,40},{40,32},{48,56},{56,48},{64,72... | collective-permute-start | bytes 1572872 | tf_op jit(solution)/shard_map/ppermute | solution.py:415
  135.3 0.8 copy-start.6

commit v4 on v3

--- a/solution.py
+++ b/solution.py
@@ -210,12 +210,12 @@
 HTILE = 256
 
 
-def network_kernel(cols, w_in_t, w_out_t, w_in, w_out, before, fields, grads, act_s, dpre_s):
+def network_kernel(cols, w_in_t, w_out_t, w_in, w_out, fields, grads, act_s, dpre_s):
     hidden = w_in_t.shape[0]
 
     @pl.when(pl.program_id(0) == 0)
     def _():
-        grads[...] = before[...]
+        grads[...] = jnp.zeros_like(grads)
 
     col = jnp.concatenate([cols[:, i, 0].reshape(128, 128) for i in range(CELLS)], 1)
     gcol = jnp.concatenate([cols[:, i, 1].reshape(128, 128) for i in range(CELLS)], 1)
@@ -245,7 +245,7 @@
         fields[:, i, 1] = d_cols[:, i * 128 : (i + 1) * 128].reshape(8, 16, 128)
 
 
-def network(cols, w_in_t, w_out_t, w_in, w_out, grads):
+def network(cols, w_in_t, w_out_t, w_in, w_out):
     rows = cols.shape[1]
     hidden = w_in.shape[1]
     block = pl.BlockSpec((8, CELLS, 2, 16, 128), lambda s: (0, s, 0, 0, 0))
@@ -255,7 +255,7 @@
     return pl.pallas_call(
         functools.partial(network_kernel),
         grid=(rows // CELLS,),
-        in_specs=[block, tall, tall, wide, wide, total],
+        in_specs=[block, tall, tall, wide, wide],
         out_specs=[block, total],
         out_shape=[
             pltpu.HBM(cols.shape, BF16),
@@ -272,29 +272,37 @@
             transcendentals=rows * 128 * hidden,
         ),
         name="column_network",
-    )(in_hbm(cols), w_in_t, w_out_t, w_in, w_out, grads)
-
-
-def totals_kernel(core, mine, other, in_total, out_total):
+    )(cols, *[in_hbm(x) for x in (w_in_t, w_out_t, w_in, w_out)])
+
+
+def totals_kernel(core, sums, in_total, out_total):
     scale = 1.0 / math.sqrt(SAMPLES)
     first = core[0] == 0
-    for k in range(0, mine.shape[0], 128):
-        at = slice(k, k + 128)
-        here = mine[at, :].T
-        there = other[at, :].T
+    size = sums.shape[2]
+    for k in range(0, sums.shape[0], 128 // size):
+        pick = range(k, k + 128 // size)
+        at = slice(k * size, k * size + 128)
+        here = jnp.concatenate([sums[i, 0] for i in pick], 0).astype(F32).T
+        there = jnp.concatenate([sums[i, 1] for i in pick], 0).astype(F32).T
         in_total[:, at] = jnp.where(first, here, there) * scale
         out_total[:, at] = jnp.where(first, there, here) * scale
 
 
-def totals(core, mine, other):
-    spec = pl.BlockSpec(memory_space=pltpu.VMEM)
+def totals(core, sums):
+    count, _, size, rows = sums.shape
+    out = pl.BlockSpec((rows, count * size), lambda s: (0, 0))
     return pl.pallas_call(
         totals_kernel,
-        in_specs=[pl.BlockSpec(memory_space=pltpu.SMEM), spec, spec],
-        out_specs=[spec] * 2,
-        out_shape=[jax.ShapeDtypeStruct(mine.shape[::-1], F32)] * 2,
+        grid=(1,),
+        in_specs=[
+            pl.BlockSpec(memory_space=pltpu.SMEM),
+            pl.BlockSpec(sums.shape, lambda s: (0, 0, 0, 0)),
+        ],
+        out_specs=[out] * 2,
+        out_shape=[pltpu.HBM((rows, count * size), F32)] * 2,
+        compiler_params=pltpu.CompilerParams(vmem_limit_bytes=8 * MIB),
         name="weight_totals",
-    )(core, mine, other)
+    )(core, sums)
 
 
 def last_kernel(
@@ -397,8 +405,8 @@
         ),
         name="transport_two",
     )(
-        *[in_hbm(x) for x in (first, first, back, back, speeds, inner, inner, outer, outer)],
-        west, low, high, *filled,
+        *[in_hbm(x) for x in (first, first, back, back, speeds)],
+        inner, inner, outer, outer, west, low, high, *filled,
     )
 
 
@@ -457,11 +465,10 @@
         blocks // 4, half, *fields_in, none, none[:2], held
     )
     got_b = exchange(cols_b.reshape(8, width // 16, 2, 16, 128))
-    zero = jnp.zeros((2, hidden, 128), F32)
-    outer, grads = network(got_a, w_in_t, w_out_t, w_in, w_out, zero)
+    outer, grads_a = network(got_a, w_in_t, w_out_t, w_in, w_out)
     outer = exchange(outer)
-    inner, grads = network(got_b, w_in_t, w_out_t, w_in, w_out, grads)
-    part, outer = barrier((chip_sum(grads), outer))
+    inner, grads_b = network(got_b, w_in_t, w_out_t, w_in, w_out)
+    part, outer = barrier((chip_sum(grads_a + grads_b), outer))
     outer = outer.reshape(width // 2, 2, 16, 128)
     quarter = width // 4
 
@@ -472,10 +479,9 @@
     def west(row):
         return jnp.concatenate([edge(row), speeds[row, 0][None].astype(F32)])
 
-    part, tail, head = barrier((part, edge(width - 1), edge(0)))
     part = jnp.sum(exchange_rows(part.reshape(32, hidden // 32, 128)), 0)
-    low_next = jnp.concatenate([shift(tail, 1), low[2:]])
-    high_next = shift(head, -1)
+    low_next = jnp.concatenate([shift(edge(width - 1), 1), low[2:]])
+    high_next = shift(edge(0), -1)
     part, inner, low_next, high_next = barrier((part, inner, low_next, high_next))
     inner = exchange(inner).reshape(width // 2, 2, 16, 128)
     fields_held = (first, back, speeds)
@@ -485,16 +491,16 @@
         ends - 1, 2, *fields_held, outer, outer, west(width - 1 - LAST_ROWS), low_next,
         high_next, shape, (),
     )
-    part = z_sum(part)
+    part = z_sum(jnp.stack([part, partner(part, 1)])).astype(BF16)
     part, inner, *results = barrier((part, inner, *results))
-    part = exchange_rows(jnp.broadcast_to(part[None], (32,) + part.shape)).reshape(hidden, 128)
+    part = exchange_rows(jnp.broadcast_to(part[None], (32,) + part.shape))
     state_out, state_grad = last_step(
         1, ends - 2, *fields_held, inner, outer, west(LAST_ROWS - 1), low_next, high_next,
         shape, results,
     )
     part, state_out, state_grad = barrier((part, state_out, state_grad))
     core = lax.rem(lax.axis_index("tile"), 2)
-    in_total, out_total = totals(core.reshape(1), part, partner(part, 1))
+    in_total, out_total = totals(core.reshape(1), part)
     return state_out, state_grad, in_total, out_total
 
 

time: 141 us -> 135 us (0.957); the launches traced: 139 us -> 134 us
  Pallas kernels: 49.4 us -> 47.4 us
    all_to_all x4, waiting for transfers between devices: 10.8 us -> 9.22 us  [exchange(): return lax.all_to_all(block, 'lev', split_axis=0, concat_axis=0, tiled=True)]
    all_to_all x2, waiting for transfers between devices: 1.32 us -> 2.8 us  [exchange_rows(): lax.all_to_all(block, ('tile', 'lev'), split_axis=0, concat_axis=0, tiled...]
  transfers between devices with their start and end apart: 15 -> 15, of which waited for: 12 -> 11; matrix products, arithmetic and copies ran while one was open for 2% -> 3% of each run, Pallas kernels for 28% -> 29%
where the time goes in v4:
time: 135 us; the launch traced here: 134 us
  starting transfers between devices  55.2 us (41%)
  Pallas kernels  47.4 us (35%)
  waiting for transfers between devices  25.7 us (19%)
  local copies, waits for them, and re-layouts  3.48 us (3%)
  other arithmetic  1.71 us (1%)
    pallas_call x2, Pallas kernels, network(): pl.pallas_call(functools.partial(network_kernel), grid=(rows // CELLS,),...  20.2 us
    all_to_all x4, starting transfers between devices, exchange(): return lax.all_to_all(block, 'lev', split_axis=0, concat_axis=0, tiled=True)  19.2 us
    all_to_all x2, starting transfers between devices, exchange_rows(): lax.all_to_all(block, ('tile', 'lev'), split_axis=0, concat_axis=0, tiled...  15 us
    ppermute x4, starting transfers between devices, shift(): lax.ppermute(block, 'tile', [(i, (i + distance) % count) for i in range(c...  14.2 us
    pallas_call x2, Pallas kernels, last_step(): pl.pallas_call(functools.partial(last_kernel, start, blocks), grid=(count...  12.3 us
    pallas_call x2, Pallas kernels, first_step(): pl.pallas_call(functools.partial(first_kernel, start, blocks), grid=(coun...  12 us
    all_to_all x4, waiting for transfers between devices, exchange(): return lax.all_to_all(block, 'lev', split_axis=0, concat_axis=0, tiled=True)  9.22 us
    ppermute x5, waiting for transfers between devices, partner(): lax.ppermute(block, 'tile', [(i, i ^ mask) for i in range(lax.axis_size('...  7.87 us
  transfers between devices with their start and end apart: 15, of which 11 were waited for; matrix products, arithmetic and copies ran while one was open for 3% of the time, Pallas kernels for 29%

profile of v4, /device:TPU:2, one launch (start us, length us, event | category | flops | bytes accessed | tf_op | source)
XLA Modules:
  0.0 134.3 jit_solution(8873041347577607322)
XLA Ops:
  0.6 1.6 %edge_rows.1 = (f32[3,16,128]{2,1,0:T(8,128)}, f32[2,16,128]{2,1,0:T(8,128)}) custom-call(f32[16,256,128]{2,1,0:T(8,128)} %state_next.1, f32[16,256,128]{2,1,0:T(8,128)} %state_next.1, f32[16,256,128]{2,1,0:T(8,128)} %cot_next.3, f32[16,256,128]{2,1,0:T(8,128)} %cot_next.3, bf16[16,256,128]{2,1,0:T(8,128)(2,1)} %east_prev.3), custom_call_target="tpu_custom_call" | custom-call | tf_op jit(solution)/shard_map/edge_rows/pallas_call | solution.py:193
  2.2 0.0 collective-permute-start
  2.2 8.2 %collective-permute-start.1 = (f32[2,16,128]{2,1,0:T(8,128)}, f32[2,16,128]{2,1,0:T(8,128)S(1)}, u32[]{:S(2)}, u32[]{:S(2)}) collective-permute-start(f32[2,16,128]{2,1,0:T(8,128)} %get-tuple-element.44), channel_id=1, source_target_pairs={{0,248},{8,0},{16,8},{24,16},{32,24},{40,32},{48,40},{56,48},{64,5... | collective-permute-start | bytes 49160 | tf_op jit(solution)/shard_map/ppermute | solution.py:415
  10.4 1.7 %collective-permute-done.1.high = f32[2,16,128]{2,1,0:T(8,128)S(1)} collective-permute-done((f32[2,16,128]{2,1,0:T(8,128)}, f32[2,16,128]{2,1,0:T(8,128)S(1)}, u32[]{:S(2)}, u32[]{:S(2)}) %collective-permute-start.1) | collective-permute-done | bytes 16416 | tf_op jit(solution)/shard_map/ppermute | solution.py:415
  12.1 0.1 collective-permute-done.low
  12.2 6.0 %transport_one.2 = (f32[256,16,128]{2,1,0:T(8,128)}, f32[256,16,128]{2,1,0:T(8,128)}, bf16[256,2,16,128]{3,2,1,0:T(8,128)(2,1)}, bf16[128,2,16,128]{3,2,1,0:T(8,128)(2,1)}) custom-call(f32[16,256,128]{2,1,0:T(8,128)} %state_next.1, f32[16,256,128]{2,1,0:T(8,128)} %state_next.1, f32[16,256,128]{2,1,0:T(8,128)} %state_next.1, f32[16,256,128]{2,1,0:T(8,128)} %cot_next.3, ...), custom_call_target="tpu_custom_call" | custom-call | flops 10485760 | bytes 7340032 | tf_op jit(solution)/shard_map/transport_one/pallas_call | solution.py:143
  18.1 5.3 %all-to-all-start = ((bf16[8,16,2,16,128]{4,3,2,1,0:T(8,128)(2,1)}), bf16[8,16,2,16,128]{4,3,2,1,0:T(8,128)(2,1)S(1)}, u32[]{:S(2)}, u32[]{:S(2)}) async-start(bf16[8,16,2,16,128]{4,3,2,1,0:T(8,128)(2,1)} %bitcast.50), calls=%async_computation | async-start | bytes 2097152 | tf_op jit(solution)/shard_map/all_to_all | solution.py:419
  23.4 6.0 %transport_one.3 = (f32[256,16,128]{2,1,0:T(8,128)}, f32[256,16,128]{2,1,0:T(8,128)}, bf16[256,2,16,128]{3,2,1,0:T(8,128)(2,1)}, bf16[128,2,16,128]{3,2,1,0:T(8,128)(2,1)}) custom-call(f32[16,256,128]{2,1,0:T(8,128)} %state_next.1, f32[16,256,128]{2,1,0:T(8,128)} %state_next.1, ...), custom_call_target="tpu_custom_call", output_to_operand_aliasing={{0}: (11, {}), {1}: (12, {}), {2}: (13, {})} | custom-call | flops 10485760 | bytes 7340032 | tf_op jit(solution)/shard_map/transport_one/pallas_call | solution.py:143
  29.5 0.0 copy-start
  29.5 0.0 copy-start.1
  29.5 6.7 %all-to-all-done.cols = bf16[8,16,2,16,128]{4,3,2,1,0:T(8,128)(2,1)S(1)} async-done(((bf16[8,16,2,16,128]{4,3,2,1,0:T(8,128)(2,1)}), bf16[8,16,2,16,128]{4,3,2,1,0:T(8,128)(2,1)S(1)}, u32[]{:S(2)}, u32[]{:S(2)}) %all-to-all-start) | async-done | bytes 1048608 | tf_op jit(solution)/shard_map/all_to_all | solution.py:419
  36.2 4.8 %all-to-all-start.1 = ((bf16[8,16,2,16,128]{4,3,2,1,0:T(8,128)(2,1)}), bf16[8,16,2,16,128]{4,3,2,1,0:T(8,128)(2,1)S(1)}, u32[]{:S(2)}, u32[]{:S(2)}) async-start(bf16[8,16,2,16,128]{4,3,2,1,0:T(8,128)(2,1)} %bitcast.49), calls=%async_computation.1 | async-start | bytes 2097152 | tf_op jit(solution)/shard_map/all_to_all | solution.py:419
  41.0 0.0 copy-done
  41.0 0.8 copy.15
  41.8 0.0 copy-done.1
  41.8 0.8 copy.16
  42.7 10.1 %column_network.2 = (bf16[8,16,2,16,128]{4,3,2,1,0:T(8,128)(2,1)}, f32[2,1024,128]{2,1,0:T(8,128)S(1)}) custom-call(bf16[8,16,2,16,128]{4,3,2,1,0:T(8,128)(2,1)S(1)} %all-to-all-done.cols, bf16[1024,128]{1,0:T(8,128)(2,1)} %bitcast.51, bf16[1024,128]{1,0:T(8,128)(2,1)} %bitcast.53, bf16[128,1024]{1,0:T(8,128)(2,1)} %w_in.3, bf16[128,1024]{1,0:T(8,128)(2,1)} %w_out.3), custom_call_target="tpu_custom_call" | custom-call | flops 3221225472 | bytes 2097152 | tf_op jit(solution)/shard_map/column_network/pallas_call | solution.py:255
  52.8 2.0 %all-to-all-done.1.cols = bf16[8,16,2,16,128]{4,3,2,1,0:T(8,128)(2,1)S(1)} async-done(((bf16[8,16,2,16,128]{4,3,2,1,0:T(8,128)(2,1)}), bf16[8,16,2,16,128]{4,3,2,1,0:T(8,128)(2,1)S(1)}, u32[]{:S(2)}, u32[]{:S(2)}) %all-to-all-start.1) | async-done | bytes 1048608 | tf_op jit(solution)/shard_map/all_to_all | solution.py:419
  54.8 4.8 %all-to-all-start.2 = ((bf16[8,16,2,16,128]{4,3,2,1,0:T(8,128)(2,1)}), bf16[8,16,2,16,128]{4,3,2,1,0:T(8,128)(2,1)S(1)}, u32[]{:S(2)}, u32[]{:S(2)}) async-start(bf16[8,16,2,16,128]{4,3,2,1,0:T(8,128)(2,1)} %get-tuple-element.52), calls=%async_computation.2 | async-start | bytes 2097152 | tf_op jit(solution)/shard_map/all_to_all | solution.py:419
  59.6 10.1 %column_network.3 = (bf16[8,16,2,16,128]{4,3,2,1,0:T(8,128)(2,1)}, f32[2,1024,128]{2,1,0:T(8,128)S(1)}) custom-call(bf16[8,16,2,16,128]{4,3,2,1,0:T(8,128)(2,1)S(1)} %all-to-all-done.1.cols, bf16[1024,128]{1,0:T(8,128)(2,1)} %bitcast.52, bf16[1024,128]{1,0:T(8,128)(2,1)} %bitcast.54, bf16[128,1024]{1,0:T(8,128)(2,1)} %w_in.3, bf16[128,1024]{1,0:T(8,128)(2,1)} %w_out.3), custom_call_target="tpu_custom_call" | custom-call | flops 3221225472 | bytes 2097152 | tf_op jit(solution)/shard_map/column_network/pallas_call | solution.py:255
  69.7 0.1 add.35
  69.9 0.3 collective-permute-start.2
  70.2 1.9 %collective-permute-done.2 = f32[1024,128]{1,0:T(8,128)S(1)} collective-permute-done((f32[1024,128]{1,0:T(8,128)S(1)}, f32[1024,128]{1,0:T(8,128)S(1)}, u32[]{:S(2)}, u32[]{:S(2)}) %collective-permute-start.2) | collective-permute-done | bytes 524320 | tf_op jit(solution)/shard_map/ppermute | solution.py:423
  72.1 0.8 bitcast_add_fusion
  72.9 0.5 all-to-all-done.2
  73.4 7.8 %all-to-all-start.3 = ((f32[32,32,128]{2,1,0:T(8,128)}), f32[32,32,128]{2,1,0:T(8,128)S(1)}, u32[]{:S(2)}, u32[]{:S(2)}) async-start(f32[32,32,128]{2,1,0:T(8,128)} %bitcast.6), calls=%async_computation.3 | async-start | bytes 1048576 | tf_op jit(solution)/shard_map/all_to_all | solution.py:438
  81.3 0.8 fusion
  82.1 0.1 collective-permute-start.3
  82.2 5.9 %collective-permute-start.4 = (f32[2,16,128]{2,1,0:T(8,128)S(1)}, f32[2,16,128]{2,1,0:T(8,128)S(1)}, u32[]{:S(2)}, u32[]{:S(2)}) collective-permute-start(f32[2,16,128]{2,1,0:T(8,128)S(1)} %get-tuple-element.88), channel_id=1, source_target_pairs={{0,248},{8,0},{16,8},{24,16},{32,24},{40,32},{48,40},{56,48},{64,5... | collective-permute-start | bytes 49160 | tf_op jit(solution)/shard_map/ppermute | solution.py:415
  88.1 4.1 %collective-permute-done.3 = f32[2,16,128]{2,1,0:T(8,128)S(1)} collective-permute-done((f32[2,16,128]{2,1,0:T(8,128)S(1)}, f32[2,16,128]{2,1,0:T(8,128)S(1)}, u32[]{:S(2)}, u32[]{:S(2)}) %collective-permute-start.3) | collective-permute-done | bytes 16416 | tf_op jit(solution)/shard_map/ppermute | solution.py:415
  92.3 0.4 all-to-all-done.3
  92.7 0.0 collective-permute-done.4.high
  92.7 4.3 %all-to-all-start.4 = ((bf16[8,16,2,16,128]{4,3,2,1,0:T(8,128)(2,1)}), bf16[8,16,2,16,128]{4,3,2,1,0:T(8,128)(2,1)S(1)}, u32[]{:S(2)}, u32[]{:S(2)}) async-start(bf16[8,16,2,16,128]{4,3,2,1,0:T(8,128)(2,1)} %get-tuple-element.59), calls=%async_computation.4 | async-start | bytes 2097152 | tf_op jit(solution)/shard_map/all_to_all | solution.py:419
  97.1 0.0 collective-permute-start.5
  97.1 0.7 bitcast_convert_fusion
  97.8 0.5 collective-permute-done.5
  98.3 4.2 %collective-permute-start.7 = (f32[2,32,128]{2,1,0:T(8,128)S(1)}, f32[2,32,128]{2,1,0:T(8,128)S(1)}, u32[]{:S(2)}, u32[]{:S(2)}) collective-permute-start(f32[2,32,128]{2,1,0:T(8,128)S(1)} %pad_maximum_fusion), channel_id=1, source_target_pairs={{0,32},{8,40},{16,48},{24,56},{32,0},{40,8},{48,16},{56,24},{64,96... | collective-permute-start | bytes 98312 | tf_op jit(solution)/shard_map/ppermute | solution.py:423
  102.5 0.3 collective-permute-start.8
  102.7 2.0 %collective-permute-start.6 = (f32[2,32,128]{2,1,0:T(8,128)S(1)}, f32[2,32,128]{2,1,0:T(8,128)S(1)}, u32[]{:S(2)}, u32[]{:S(2)}) collective-permute-start(f32[2,32,128]{2,1,0:T(8,128)S(1)} %pad_maximum_fusion), channel_id=1, source_target_pairs={{0,16},{8,24},{16,0},{24,8},{32,48},{40,56},{48,32},{56,40},{64,80... | collective-permute-start | bytes 98312 | tf_op jit(solution)/shard_map/ppermute | solution.py:423
  104.8 3.8 %transport_two.2 = (f32[16,256,128]{2,1,0:T(8,128)}, f32[16,256,128]{2,1,0:T(8,128)}) custom-call(f32[256,16,128]{2,1,0:T(8,128)} %get-tuple-element.55.first.first_next, f32[256,16,128]{2,1,0:T(8,128)} %get-tuple-element.55.first.first_next, f32[256,16,128]{2,1,0:T(8,128)} %get-tuple-element.56.back.back_next, ...), custom_call_target="tpu_custom_call" | custom-call | flops 5242880 | bytes 3145728 | tf_op jit(solution)/shard_map/transport_two/pallas_call | solution.py:388
  108.6 5.5 %collective-permute-done.7 = f32[2,32,128]{2,1,0:T(8,128)S(1)} collective-permute-done((f32[2,32,128]{2,1,0:T(8,128)S(1)}, f32[2,32,128]{2,1,0:T(8,128)S(1)}, u32[]{:S(2)}, u32[]{:S(2)}) %collective-permute-start.7) | collective-permute-done | bytes 32800 | tf_op jit(solution)/shard_map/ppermute | solution.py:423
  114.1 0.0 collective-permute-done.8
  114.1 0.0 collective-permute-done.6
  114.1 0.0 all-to-all-done.4
  114.1 0.9 broadcast_in_dim.10
  115.0 7.2 %all-to-all-start.5 = ((bf16[32,2,32,128]{3,2,1,0:T(8,128)(2,1)}), bf16[32,2,32,128]{3,2,1,0:T(8,128)(2,1)S(1)}, u32[]{:S(2)}, u32[]{:S(2)}) async-start(bf16[32,2,32,128]{3,2,1,0:T(8,128)(2,1)} %broadcast_in_dim.10), calls=%async_computation.5 | async-start | bytes 1048576 | tf_op jit(solution)/shard_map/all_to_all | solution.py:438
  122.2 8.5 %transport_two.3 = (f32[16,256,128]{2,1,0:T(8,128)}, f32[16,256,128]{2,1,0:T(8,128)}) custom-call(f32[256,16,128]{2,1,0:T(8,128)} %get-tuple-element.55.first.first_next, f32[256,16,128]{2,1,0:T(8,128)} %get-tuple-element.55.first.first_next, f32[256,16,128]{2,1,0:T(8,128)} %get-tuple-element.56.back.back_next, ...), custom_call_target="tpu_custom_call", output_to_operand_aliasing={{0}: (12, {}), {1}: (13, {})} | custom-call | flops 15728640 | bytes 9437184 | tf_op jit(solution)/shard_map/transport_two/pallas_call | solution.py:388
  130.7 2.4 %all-to-all-done.5.sums = bf16[32,2,32,128]{3,2,1,0:T(8,128)(2,1)S(1)} async-done(((bf16[32,2,32,128]{3,2,1,0:T(8,128)(2,1)}), bf16[32,2,32,128]{3,2,1,0:T(8,128)(2,1)S(1)}, u32[]{:S(2)}, u32[]{:S(2)}) %all-to-all-start.5) | async-done | bytes 524320 | tf_op jit(solution)/shard_map/all_to_all | solution.py:438
  133.1 1.2 weight_totals.1
  (11 shorter events, 0.1 us)
Async XLA Ops:
  2.2 9.9 %collective-permute-start = (f32[3,16,128]{2,1,0:T(8,128)}, f32[3,16,128]{2,1,0:T(8,128)S(1)}, u32[]{:S(2)}, u32[]{:S(2)}) collective-permute-start(f32[3,16,128]{2,1,0:T(8,128)} %get-tuple-element.43), channel_id=1, source_target_pairs={{0,8},{8,16},{16,24},{24,32},{32,40},{40,48},{48,56},{56,64},{64,7... | collective-permute-start | bytes 73736 | tf_op jit(solution)/shard_map/ppermute | solution.py:415
  2.2 9.8 %collective-permute-start.1 = (f32[2,16,128]{2,1,0:T(8,128)}, f32[2,16,128]{2,1,0:T(8,128)S(1)}, u32[]{:S(2)}, u32[]{:S(2)}) collective-permute-start(f32[2,16,128]{2,1,0:T(8,128)} %get-tuple-element.44), channel_id=1, source_target_pairs={{0,248},{8,0},{16,8},{24,16},{32,24},{40,32},{48,40},{56,48},{64,5... | collective-permute-start | bytes 49160 | tf_op jit(solution)/shard_map/ppermute | solution.py:415
  18.1 18.0 %all-to-all-start = ((bf16[8,16,2,16,128]{4,3,2,1,0:T(8,128)(2,1)}), bf16[8,16,2,16,128]{4,3,2,1,0:T(8,128)(2,1)S(1)}, u32[]{:S(2)}, u32[]{:S(2)}) async-start(bf16[8,16,2,16,128]{4,3,2,1,0:T(8,128)(2,1)} %bitcast.50), calls=%async_computation | async-start | bytes 2097152 | tf_op jit(solution)/shard_map/all_to_all | solution.py:419
  29.5 11.5 %copy-start = (bf16[128,1024]{1,0:T(8,128)(2,1)S(1)}, bf16[128,1024]{1,0:T(8,128)(2,1)}, u32[]{:S(2)}) copy-start(bf16[128,1024]{1,0:T(8,128)(2,1)} %w_in.3) | copy-start | bytes 786436
  29.5 12.4 %copy-start.1 = (bf16[128,1024]{1,0:T(8,128)(2,1)S(1)}, bf16[128,1024]{1,0:T(8,128)(2,1)}, u32[]{:S(2)}) copy-start(bf16[128,1024]{1,0:T(8,128)(2,1)} %w_out.3) | copy-start | bytes 786436
  36.2 18.6 %all-to-all-start.1 = ((bf16[8,16,2,16,128]{4,3,2,1,0:T(8,128)(2,1)}), bf16[8,16,2,16,128]{4,3,2,1,0:T(8,128)(2,1)S(1)}, u32[]{:S(2)}, u32[]{:S(2)}) async-start(bf16[8,16,2,16,128]{4,3,2,1,0:T(8,128)(2,1)} %bitcast.49), calls=%async_computation.1 | async-start | bytes 2097152 | tf_op jit(solution)/shard_map/all_to_all | solution.py:419
  54.8 18.6 %all-to-all-start.2 = ((bf16[8,16,2,16,128]{4,3,2,1,0:T(8,128)(2,1)}), bf16[8,16,2,16,128]{4,3,2,1,0:T(8,128)(2,1)S(1)}, u32[]{:S(2)}, u32[]{:S(2)}) async-start(bf16[8,16,2,16,128]{4,3,2,1,0:T(8,128)(2,1)} %get-tuple-element.52), calls=%async_computation.2 | async-start | bytes 2097152 | tf_op jit(solution)/shard_map/all_to_all | solution.py:419
  69.9 2.2 %collective-permute-start.2 = (f32[1024,128]{1,0:T(8,128)S(1)}, f32[1024,128]{1,0:T(8,128)S(1)}, u32[]{:S(2)}, u32[]{:S(2)}) collective-permute-start(f32[1024,128]{1,0:T(8,128)S(1)} %dynamic-slice_bitcast_fusion), channel_id=1, source_target_pairs={{0,8},{8,0},{16,24},{24,16},{32,40},{40,32},{48,56},{56,48},{64,72... | collective-permute-start | bytes 1572872 | tf_op jit(solution)/shard_map/ppermute | solution.py:423
  73.4 19.3 %all-to-all-start.3 = ((f32[32,32,128]{2,1,0:T(8,128)}), f32[32,32,128]{2,1,0:T(8,128)S(1)}, u32[]{:S(2)}, u32[]{:S(2)}) async-start(f32[32,32,128]{2,1,0:T(8,128)} %bitcast.6), calls=%async_computation.3 | async-start | bytes 1048576 | tf_op jit(solution)/shard_map/all_to_all | solution.py:438
  82.1 10.2 %collective-permute-start.3 = (f32[2,16,128]{2,1,0:T(8,128)S(1)}, f32[2,16,128]{2,1,0:T(8,128)S(1)}, u32[]{:S(2)}, u32[]{:S(2)}) collective-permute-start(f32[2,16,128]{2,1,0:T(8,128)S(1)} %get-tuple-element.89), channel_id=1, source_target_pairs={{0,8},{8,16},{16,24},{24,32},{32,40},{40,48},{48,56},{56,64},{64,7... | collective-permute-start | bytes 49160 | tf_op jit(solution)/shard_map/ppermute | solution.py:415
  82.2 10.5 %collective-permute-start.4 = (f32[2,16,128]{2,1,0:T(8,128)S(1)}, f32[2,16,128]{2,1,0:T(8,128)S(1)}, u32[]{:S(2)}, u32[]{:S(2)}) collective-permute-start(f32[2,16,128]{2,1,0:T(8,128)S(1)} %get-tuple-element.88), channel_id=1, source_target_pairs={{0,248},{8,0},{16,8},{24,16},{32,24},{40,32},{48,40},{56,48},{64,5... | collective-permute-start | bytes 49160 | tf_op jit(solution)/shard_map/ppermute | solution.py:415
  92.7 21.4 %all-to-all-start.4 = ((bf16[8,16,2,16,128]{4,3,2,1,0:T(8,128)(2,1)}), bf16[8,16,2,16,128]{4,3,2,1,0:T(8,128)(2,1)S(1)}, u32[]{:S(2)}, u32[]{:S(2)}) async-start(bf16[8,16,2,16,128]{4,3,2,1,0:T(8,128)(2,1)} %get-tuple-element.59), calls=%async_computation.4 | async-start | bytes 2097152 | tf_op jit(solution)/shard_map/all_to_all | solution.py:419
  97.1 1.2 collective-permute-start.5
  98.3 15.8 %collective-permute-start.7 = (f32[2,32,128]{2,1,0:T(8,128)S(1)}, f32[2,32,128]{2,1,0:T(8,128)S(1)}, u32[]{:S(2)}, u32[]{:S(2)}) collective-permute-start(f32[2,32,128]{2,1,0:T(8,128)S(1)} %pad_maximum_fusion), channel_id=1, source_target_pairs={{0,32},{8,40},{16,48},{24,56},{32,0},{40,8},{48,16},{56,24},{64,96... | collective-permute-start | bytes 98312 | tf_op jit(solution)/shard_map/ppermute | solution.py:423
  102.5 11.6 %collective-permute-start.8 = (f32[2,32,128]{2,1,0:T(8,128)S(1)}, f32[2,32,128]{2,1,0:T(8,128)S(1)}, u32[]{:S(2)}, u32[]{:S(2)}) collective-permute-start(f32[2,32,128]{2,1,0:T(8,128)S(1)} %pad_maximum_fusion), channel_id=1, source_target_pairs={{0,48},{8,56},{16,32},{24,40},{32,16},{40,24},{48,0},{56,8},{64,11... | collective-permute-start | bytes 98312 | tf_op jit(solution)/shard_map/ppermute | solution.py:423
  102.7 11.4 %collective-permute-start.6 = (f32[2,32,128]{2,1,0:T(8,128)S(1)}, f32[2,32,128]{2,1,0:T(8,128)S(1)}, u32[]{:S(2)}, u32[]{:S(2)}) collective-permute-start(f32[2,32,128]{2,1,0:T(8,128)S(1)} %pad_maximum_fusion), channel_id=1, source_target_pairs={{0,16},{8,24},{16,0},{24,8},{32,48},{40,56},{48,32},{56,40},{64,80... | collective-permute-start | bytes 98312 | tf_op jit(solution)/shard_map/ppermute | solution.py:423
  115.0 18.1 %all-to-all-start.5 = ((bf16[32,2,32,128]{3,2,1,0:T(8,128)(2,1)}), bf16[32,2,32,128]{3,2,1,0:T(8,128)(2,1)S(1)}, u32[]{:S(2)}, u32[]{:S(2)}) async-start(bf16[32,2,32,128]{3,2,1,0:T(8,128)(2,1)} %broadcast_in_dim.10), calls=%async_computation.5 | async-start | bytes 1048576 | tf_op jit(solution)/shard_map/all_to_all | solution.py:438

commit v5 on v4

--- a/solution.py
+++ b/solution.py
@@ -12,7 +12,7 @@
 SLOPE_C = 0.7978845608028654
 CUBIC = 0.044715
 ROWS = 64
-LAST_ROWS = 32
+LAST_ROWS = 64
 SUB = 256
 UNROLL = 16
 SAMPLES = 8192 * 128
@@ -34,9 +34,13 @@
     return ref[pl.ds(pl.multiple_of(index * 16, 16), 16), :]
 
 
-def put_rows(ref, index, stride, value):
-    ref[pl.ds(index, 8, stride), :] = value[:8]
-    ref[pl.ds(index + 8 * stride, 8, stride), :] = value[8:]
+def gather(scratch, ref, rows):
+    def one(tile, carry):
+        part = scratch[pl.ds(pl.multiple_of(tile * 256, 256), 256), :].reshape(16, 16, 128)
+        ref[:, pl.ds(pl.multiple_of(tile * 16, 16), 16), :] = jnp.swapaxes(part, 0, 1)
+        return carry
+
+    lax.fori_loop(0, rows // 16, one, 0)
 
 
 def up_of(value):
@@ -143,7 +147,7 @@
     return pl.pallas_call(
         functools.partial(first_kernel, start, blocks),
         grid=(count,),
-        in_specs=[main, prev, post, main, prev, post, main, prev16, main, whole(3), whole(2)]
+        in_specs=[main, prev, post, main, prev, post, main, prev16, main, whole(3), whole(3)]
         + [pl.BlockSpec(memory_space=pl.ANY)] * len(filled),
         out_specs=[field, field, speed, pair],
         out_shape=[
@@ -183,6 +187,7 @@
     low[2] = east_hi[...].astype(F32)[:, 15, :]
     high[0] = state_lo[:, 0, :]
     high[1] = cot_lo[:, 0, :]
+    high[2] = cot_lo[:, 0, :]
 
 
 def edge_rows(state, east, cot):
@@ -196,11 +201,11 @@
         in_specs=[head, tail, head, tail, tail16],
         out_specs=[
             pl.BlockSpec((3, 16, 128), lambda s: (0, 0, 0)),
-            pl.BlockSpec((2, 16, 128), lambda s: (0, 0, 0)),
+            pl.BlockSpec((3, 16, 128), lambda s: (0, 0, 0)),
         ],
         out_shape=[
             jax.ShapeDtypeStruct((3, 16, 128), F32),
-            jax.ShapeDtypeStruct((2, 16, 128), F32),
+            jax.ShapeDtypeStruct((3, 16, 128), F32),
         ],
         name="edge_rows",
     )(*[in_hbm(x) for x in (state, state, cot, cot, east)])
@@ -309,7 +314,7 @@
     start, blocks, first, first_next, back, back_next, speeds, inner, inner_next, outer,
     outer_next, west, low, high, *rest,
 ):
-    out, grad, q_s, g_s, flux_s, drift_s = rest[-6:]
+    out, grad, q_s, g_s, out_s, grad_s, flux_s, drift_s = rest[-8:]
     here = lax.rem(pl.program_id(0) + start, blocks)
     quarter = blocks // 4
 
@@ -335,9 +340,6 @@
     fresh = jnp.logical_or(here == 0, pl.program_id(0) == 0)
     flux = jnp.where(fresh, flux, flux_s[...])
     drift = jnp.where(fresh, drift, drift_s[...])
-    out2 = out.reshape(16 * LAST_ROWS, 128)
-    grad2 = grad.reshape(16 * LAST_ROWS, 128)
-
     def one(i, carry):
         q, g, flux, drift = carry
         q_next = row(q_s, i + 1)
@@ -345,13 +347,16 @@
         e = speeds[i, 0].astype(F32)
         n = speeds[i, 1].astype(F32)
         moved, pulled, flux, drift = step_row(q, q_next, g, g_next, e, n, flux, drift)
-        put_rows(out2, i, LAST_ROWS, moved)
-        put_rows(grad2, i, LAST_ROWS, pulled)
+        at = pl.ds(pl.multiple_of(i * 16, 16), 16)
+        out_s[at, :] = moved
+        grad_s[at, :] = pulled
         return q_next, g_next, flux, drift
 
     carry = lax.fori_loop(0, LAST_ROWS, one, (q, g, flux, drift), unroll=UNROLL)
     flux_s[...] = carry[2]
     drift_s[...] = carry[3]
+    gather(out_s, out, LAST_ROWS)
+    gather(grad_s, grad, LAST_ROWS)
 
 
 def last_step(start, count, first, back, speeds, inner, outer, west, low, high, shape, filled):
@@ -398,6 +403,7 @@
         out_shape=[pltpu.HBM(shape, F32)] * 2,
         input_output_aliases={12 + k: k for k in range(len(filled))},
         scratch_shapes=[pltpu.VMEM(((LAST_ROWS + 1) * 16, 128), F32)] * 2
+        + [pltpu.VMEM((LAST_ROWS * 16, 128), F32)] * 2
         + [pltpu.VMEM((16, 128), F32)] * 2,
         compiler_params=pltpu.CompilerParams(vmem_limit_bytes=16 * MIB),
         cost_estimate=pl.CostEstimate(
@@ -410,9 +416,18 @@
     )
 
 
-def shift(block, distance):
+def across(block):
     count = lax.axis_size("tile")
-    return lax.ppermute(block, "tile", [(i, (i + distance) % count) for i in range(count)])
+    return lax.ppermute(
+        block, "tile", [(i, (i + 1 if i % 2 else i - 1) % count) for i in range(count)]
+    )
+
+
+def halo(core, last, first):
+    even = core == 0
+    by_link = across(jnp.where(even, first, last))
+    by_chip = partner(jnp.where(even, last, first), 1)
+    return jnp.where(even, by_link, by_chip), jnp.where(even, by_chip, by_link)
 
 
 def exchange(block):
@@ -452,8 +467,8 @@
     barrier = lax.optimization_barrier
     low, high = edge_rows(state_in, east_speed, cotangent)
     low, high, state_in = barrier((low, high, state_in))
-    low = shift(low, 1)
-    high = shift(high, -1)
+    core = lax.rem(lax.axis_index("tile"), 2)
+    low, high = halo(core, low, high)
     w_in_t, w_out_t = w_in.T, w_out.T
     none = jnp.zeros((3, 16, 128), F32)
     half = blocks // 2
@@ -462,7 +477,7 @@
     got_a = exchange(cols_a.reshape(8, width // 16, 2, 16, 128))
     held = (first, back, speeds)
     first, back, speeds, cols_b = first_step(
-        blocks // 4, half, *fields_in, none, none[:2], held
+        blocks // 4, half, *fields_in, none, none, held
     )
     got_b = exchange(cols_b.reshape(8, width // 16, 2, 16, 128))
     outer, grads_a = network(got_a, w_in_t, w_out_t, w_in, w_out)
@@ -480,23 +495,16 @@
         return jnp.concatenate([edge(row), speeds[row, 0][None].astype(F32)])
 
     part = jnp.sum(exchange_rows(part.reshape(32, hidden // 32, 128)), 0)
-    low_next = jnp.concatenate([shift(edge(width - 1), 1), low[2:]])
-    high_next = shift(edge(0), -1)
+    part, inner, tail, head = barrier((part, inner, edge(width - 1), edge(0)))
+    inner = exchange(inner).reshape(width // 2, 2, 16, 128)
+    part = z_sum(jnp.stack([part, partner(part, 1)])).astype(BF16)
+    low_next, high_next = halo(core, tail, head)
+    low_next = jnp.concatenate([low_next, low[2:]])
     part, inner, low_next, high_next = barrier((part, inner, low_next, high_next))
-    inner = exchange(inner).reshape(width // 2, 2, 16, 128)
-    fields_held = (first, back, speeds)
-    shape = state_in.shape
-    ends = shape[1] // LAST_ROWS
-    results = last_step(
-        ends - 1, 2, *fields_held, outer, outer, west(width - 1 - LAST_ROWS), low_next,
-        high_next, shape, (),
-    )
-    part = z_sum(jnp.stack([part, partner(part, 1)])).astype(BF16)
-    part, inner, *results = barrier((part, inner, *results))
     part = exchange_rows(jnp.broadcast_to(part[None], (32,) + part.shape))
     state_out, state_grad = last_step(
-        1, ends - 2, *fields_held, inner, outer, west(LAST_ROWS - 1), low_next, high_next,
-        shape, results,
+        0, width // LAST_ROWS, first, back, speeds, inner, outer, low_next, low_next, high_next,
+        state_in.shape, (),
     )
     part, state_out, state_grad = barrier((part, state_out, state_grad))
     core = lax.rem(lax.axis_index("tile"), 2)

time: 135 us -> 134 us (level)
  waiting for transfers between devices: 25.7 us -> 31.5 us
  starting transfers between devices: 55.2 us -> 51.2 us
  Pallas kernels: 47.4 us -> 43.6 us
    all_to_all x2, waiting for transfers between devices: 2.8 us -> 11.2 us  [exchange_rows(): lax.all_to_all(block, ('tile', 'lev'), split_axis=0, concat_axis=0, tiled...]
    pallas_call x2 -> x1, Pallas kernels: 12.3 us -> 8.61 us  [last_step(): pl.pallas_call(functools.partial(last_kernel, start, blocks), grid=(count...]
    ppermute x5 -> x7, waiting for transfers between devices: 7.87 us -> 4.56 us  [partner(): lax.ppermute(block, 'tile', [(i, i ^ mask) for i in range(lax.axis_size('...]
    all_to_all x2, starting transfers between devices: 15 us -> 11.8 us  [exchange_rows(): lax.all_to_all(block, ('tile', 'lev'), split_axis=0, concat_axis=0, tiled...]
    ppermute x4 -> x2, starting transfers between devices: 14.2 us -> 13.5 us  [across(): lax.ppermute(block, 'tile', [(i, (i + 1 if i % 2 else i - 1) % count) for...]
    ppermute x4 -> x2, waiting for transfers between devices: 5.84 us -> 5.54 us  [across(): lax.ppermute(block, 'tile', [(i, (i + 1 if i % 2 else i - 1) % count) for...]
    ppermute x5 -> x7, starting transfers between devices: 6.77 us -> 6.68 us  [partner(): lax.ppermute(block, 'tile', [(i, i ^ mask) for i in range(lax.axis_size('...]
  transfers between devices with their start and end apart: 15 -> 15, of which waited for: 11 -> 10; matrix products, arithmetic and copies ran while one was open for 3% -> 3% of each run, Pallas kernels for 29% -> 26%
where the time goes in v5:
time: 134 us; the launch traced here: 132 us
  starting transfers between devices  51.2 us (38%)
  Pallas kernels  43.6 us (33%)
  waiting for transfers between devices  31.5 us (24%)
  local copies, waits for them, and re-layouts  3.4 us (3%)
  other arithmetic  1.83 us (1%)
    pallas_call x2, Pallas kernels, network(): pl.pallas_call(functools.partial(network_kernel), grid=(rows // CELLS,),...  20.2 us
    all_to_all x4, starting transfers between devices, exchange(): return lax.all_to_all(block, 'lev', split_axis=0, concat_axis=0, tiled=True)  19.2 us
    ppermute x2, starting transfers between devices, across(): lax.ppermute(block, 'tile', [(i, (i + 1 if i % 2 else i - 1) % count) for...  13.5 us
    pallas_call x2, Pallas kernels, first_step(): pl.pallas_call(functools.partial(first_kernel, start, blocks), grid=(coun...  12 us
    all_to_all x2, starting transfers between devices, exchange_rows(): lax.all_to_all(block, ('tile', 'lev'), split_axis=0, concat_axis=0, tiled...  11.8 us
    all_to_all x2, waiting for transfers between devices, exchange_rows(): lax.all_to_all(block, ('tile', 'lev'), split_axis=0, concat_axis=0, tiled...  11.2 us
    all_to_all x4, waiting for transfers between devices, exchange(): return lax.all_to_all(block, 'lev', split_axis=0, concat_axis=0, tiled=True)  10.3 us
    pallas_call x1, Pallas kernels, last_step(): pl.pallas_call(functools.partial(last_kernel, start, blocks), grid=(count...  8.61 us
  transfers between devices with their start and end apart: 15, of which 10 were waited for; matrix products, arithmetic and copies ran while one was open for 3% of the time, Pallas kernels for 26%

profile of v5, /device:TPU:2, one launch (start us, length us, event | category | flops | bytes accessed | tf_op | source)
XLA Modules:
  0.0 132.4 jit_solution(11210783462941202789)
XLA Ops:
  0.6 1.6 %edge_rows.1 = (f32[3,16,128]{2,1,0:T(8,128)}, f32[3,16,128]{2,1,0:T(8,128)}) custom-call(f32[16,256,128]{2,1,0:T(8,128)} %state_next.1, f32[16,256,128]{2,1,0:T(8,128)} %state_next.1, f32[16,256,128]{2,1,0:T(8,128)} %cot_next.3, f32[16,256,128]{2,1,0:T(8,128)} %cot_next.3, bf16[16,256,128]{2,1,0:T(8,128)(2,1)} %east_prev.3), custom_call_target="tpu_custom_call" | custom-call | tf_op jit(solution)/shard_map/edge_rows/pallas_call | solution.py:198
  2.3 0.8 broadcast_select_fusion.2
  3.0 8.2 %collective-permute-start = (f32[3,16,128]{2,1,0:T(8,128)S(1)}, f32[3,16,128]{2,1,0:T(8,128)S(1)}, u32[]{:S(2)}, u32[]{:S(2)}) collective-permute-start(f32[3,16,128]{2,1,0:T(8,128)S(1)} %get-tuple-element.81), channel_id=1, source_target_pairs={{0,248},{8,16},{16,8},{24,32},{32,24},{40,48},{48,40},{56,64},{64,... | collective-permute-start | bytes 73736 | tf_op jit(solution)/shard_map/ppermute | solution.py:421
  11.2 0.0 collective-permute-start.1
  11.2 1.5 %collective-permute-done = f32[3,16,128]{2,1,0:T(8,128)S(1)} collective-permute-done((f32[3,16,128]{2,1,0:T(8,128)S(1)}, f32[3,16,128]{2,1,0:T(8,128)S(1)}, u32[]{:S(2)}, u32[]{:S(2)}) %collective-permute-start) | collective-permute-done | bytes 24608 | tf_op jit(solution)/shard_map/ppermute | solution.py:421
  12.7 0.0 collective-permute-done.1
  12.7 6.0 %transport_one.2 = (f32[256,16,128]{2,1,0:T(8,128)}, f32[256,16,128]{2,1,0:T(8,128)}, bf16[256,2,16,128]{3,2,1,0:T(8,128)(2,1)}, bf16[128,2,16,128]{3,2,1,0:T(8,128)(2,1)}) custom-call(f32[16,256,128]{2,1,0:T(8,128)} %state_next.1, f32[16,256,128]{2,1,0:T(8,128)} %state_next.1, f32[16,256,128]{2,1,0:T(8,128)} %state_next.1, f32[16,256,128]{2,1,0:T(8,128)} %cot_next.3, ...), custom_call_target="tpu_custom_call" | custom-call | flops 10485760 | bytes 7340032 | tf_op jit(solution)/shard_map/transport_one/pallas_call | solution.py:147
  18.8 5.3 %all-to-all-start = ((bf16[8,16,2,16,128]{4,3,2,1,0:T(8,128)(2,1)}), bf16[8,16,2,16,128]{4,3,2,1,0:T(8,128)(2,1)S(1)}, u32[]{:S(2)}, u32[]{:S(2)}) async-start(bf16[8,16,2,16,128]{4,3,2,1,0:T(8,128)(2,1)} %bitcast.30), calls=%async_computation | async-start | bytes 2097152 | tf_op jit(solution)/shard_map/all_to_all | solution.py:434
  24.1 6.0 %transport_one.3 = (f32[256,16,128]{2,1,0:T(8,128)}, f32[256,16,128]{2,1,0:T(8,128)}, bf16[256,2,16,128]{3,2,1,0:T(8,128)(2,1)}, bf16[128,2,16,128]{3,2,1,0:T(8,128)(2,1)}) custom-call(f32[16,256,128]{2,1,0:T(8,128)} %state_next.1, f32[16,256,128]{2,1,0:T(8,128)} %state_next.1, ...), custom_call_target="tpu_custom_call", output_to_operand_aliasing={{0}: (11, {}), {1}: (12, {}), {2}: (13, {})} | custom-call | flops 10485760 | bytes 7340032 | tf_op jit(solution)/shard_map/transport_one/pallas_call | solution.py:147
  30.0 0.0 copy-start
  30.0 0.0 copy-start.1
  30.1 7.6 %all-to-all-done.cols = bf16[8,16,2,16,128]{4,3,2,1,0:T(8,128)(2,1)S(1)} async-done(((bf16[8,16,2,16,128]{4,3,2,1,0:T(8,128)(2,1)}), bf16[8,16,2,16,128]{4,3,2,1,0:T(8,128)(2,1)S(1)}, u32[]{:S(2)}, u32[]{:S(2)}) %all-to-all-start) | async-done | bytes 1048608 | tf_op jit(solution)/shard_map/all_to_all | solution.py:434
  37.7 4.8 %all-to-all-start.1 = ((bf16[8,16,2,16,128]{4,3,2,1,0:T(8,128)(2,1)}), bf16[8,16,2,16,128]{4,3,2,1,0:T(8,128)(2,1)S(1)}, u32[]{:S(2)}, u32[]{:S(2)}) async-start(bf16[8,16,2,16,128]{4,3,2,1,0:T(8,128)(2,1)} %bitcast.29), calls=%async_computation.1 | async-start | bytes 2097152 | tf_op jit(solution)/shard_map/all_to_all | solution.py:434
  42.5 0.0 copy-done
  42.5 0.8 copy.13
  43.3 0.0 copy-done.1
  43.3 0.8 copy.14
  44.1 10.1 %column_network.2 = (bf16[8,16,2,16,128]{4,3,2,1,0:T(8,128)(2,1)}, f32[2,1024,128]{2,1,0:T(8,128)S(1)}) custom-call(bf16[8,16,2,16,128]{4,3,2,1,0:T(8,128)(2,1)S(1)} %all-to-all-done.cols, bf16[1024,128]{1,0:T(8,128)(2,1)} %bitcast.31, bf16[1024,128]{1,0:T(8,128)(2,1)} %bitcast.33, bf16[128,1024]{1,0:T(8,128)(2,1)} %w_in.3, bf16[128,1024]{1,0:T(8,128)(2,1)} %w_out.3), custom_call_target="tpu_custom_call" | custom-call | flops 3221225472 | bytes 2097152 | tf_op jit(solution)/shard_map/column_network/pallas_call | solution.py:260
  54.3 2.0 %all-to-all-done.1.cols = bf16[8,16,2,16,128]{4,3,2,1,0:T(8,128)(2,1)S(1)} async-done(((bf16[8,16,2,16,128]{4,3,2,1,0:T(8,128)(2,1)}), bf16[8,16,2,16,128]{4,3,2,1,0:T(8,128)(2,1)S(1)}, u32[]{:S(2)}, u32[]{:S(2)}) %all-to-all-start.1) | async-done | bytes 1048608 | tf_op jit(solution)/shard_map/all_to_all | solution.py:434
  56.3 4.8 %all-to-all-start.2 = ((bf16[8,16,2,16,128]{4,3,2,1,0:T(8,128)(2,1)}), bf16[8,16,2,16,128]{4,3,2,1,0:T(8,128)(2,1)S(1)}, u32[]{:S(2)}, u32[]{:S(2)}) async-start(bf16[8,16,2,16,128]{4,3,2,1,0:T(8,128)(2,1)} %get-tuple-element.50), calls=%async_computation.2 | async-start | bytes 2097152 | tf_op jit(solution)/shard_map/all_to_all | solution.py:434
  61.1 10.1 %column_network.3 = (bf16[8,16,2,16,128]{4,3,2,1,0:T(8,128)(2,1)}, f32[2,1024,128]{2,1,0:T(8,128)S(1)}) custom-call(bf16[8,16,2,16,128]{4,3,2,1,0:T(8,128)(2,1)S(1)} %all-to-all-done.1.cols, bf16[1024,128]{1,0:T(8,128)(2,1)} %bitcast.32, bf16[1024,128]{1,0:T(8,128)(2,1)} %bitcast.34, bf16[128,1024]{1,0:T(8,128)(2,1)} %w_in.3, bf16[128,1024]{1,0:T(8,128)(2,1)} %w_out.3), custom_call_target="tpu_custom_call" | custom-call | flops 3221225472 | bytes 2097152 | tf_op jit(solution)/shard_map/column_network/pallas_call | solution.py:260
  71.2 0.1 add.29
  71.4 0.1 collective-permute-start.2
  71.5 1.9 %collective-permute-done.2 = f32[1024,128]{1,0:T(8,128)S(1)} collective-permute-done((f32[1024,128]{1,0:T(8,128)S(1)}, f32[1024,128]{1,0:T(8,128)S(1)}, u32[]{:S(2)}, u32[]{:S(2)}) %collective-permute-start.2) | collective-permute-done | bytes 524320 | tf_op jit(solution)/shard_map/ppermute | solution.py:438
  73.4 0.8 bitcast_add_fusion
  74.2 0.7 all-to-all-done.2
  74.9 5.5 %all-to-all-start.3 = ((f32[32,32,128]{2,1,0:T(8,128)}), f32[32,32,128]{2,1,0:T(8,128)S(1)}, u32[]{:S(2)}, u32[]{:S(2)}) async-start(f32[32,32,128]{2,1,0:T(8,128)} %bitcast.6), calls=%async_computation.3 | async-start | bytes 1048576 | tf_op jit(solution)/shard_map/all_to_all | solution.py:453
  80.4 0.8 fusion
  81.2 10.3 %all-to-all-done.3 = f32[32,32,128]{2,1,0:T(8,128)S(1)} async-done(((f32[32,32,128]{2,1,0:T(8,128)}), f32[32,32,128]{2,1,0:T(8,128)S(1)}, u32[]{:S(2)}, u32[]{:S(2)}) %all-to-all-start.3) | async-done | bytes 524320 | tf_op jit(solution)/shard_map/all_to_all | solution.py:453
  91.6 4.3 %all-to-all-start.4 = ((bf16[8,16,2,16,128]{4,3,2,1,0:T(8,128)(2,1)}), bf16[8,16,2,16,128]{4,3,2,1,0:T(8,128)(2,1)S(1)}, u32[]{:S(2)}, u32[]{:S(2)}) async-start(bf16[8,16,2,16,128]{4,3,2,1,0:T(8,128)(2,1)} %get-tuple-element.57), calls=%async_computation.4 | async-start | bytes 2097152 | tf_op jit(solution)/shard_map/all_to_all | solution.py:434
  95.9 0.0 collective-permute-start.3
  95.9 5.3 %collective-permute-start.7 = (f32[2,16,128]{2,1,0:T(8,128)S(1)}, f32[2,16,128]{2,1,0:T(8,128)S(1)}, u32[]{:S(2)}, u32[]{:S(2)}) collective-permute-start(f32[2,16,128]{2,1,0:T(8,128)S(1)} %get-tuple-element.85), channel_id=1, source_target_pairs={{0,248},{8,16},{16,8},{24,32},{32,24},{40,48},{48,40},{56,64},{64,... | collective-permute-start | bytes 49160 | tf_op jit(solution)/shard_map/ppermute | solution.py:421
  101.3 0.0 collective-permute-start.8
  101.3 0.0 collective-permute-done.3
  101.3 0.1 collective-permute-start.4
  101.4 2.7 %collective-permute-start.5 = (f32[2,32,128]{2,1,0:T(8,128)S(1)}, f32[2,32,128]{2,1,0:T(8,128)S(1)}, u32[]{:S(2)}, u32[]{:S(2)}) collective-permute-start(f32[2,32,128]{2,1,0:T(8,128)S(1)} %pad_maximum_fusion), channel_id=1, source_target_pairs={{0,32},{8,40},{16,48},{24,56},{32,0},{40,8},{48,16},{56,24},{64,96... | collective-permute-start | bytes 98312 | tf_op jit(solution)/shard_map/ppermute | solution.py:438
  104.1 3.7 %collective-permute-start.6 = (f32[2,32,128]{2,1,0:T(8,128)S(1)}, f32[2,32,128]{2,1,0:T(8,128)S(1)}, u32[]{:S(2)}, u32[]{:S(2)}) collective-permute-start(f32[2,32,128]{2,1,0:T(8,128)S(1)} %pad_maximum_fusion), channel_id=1, source_target_pairs={{0,48},{8,56},{16,32},{24,40},{32,16},{40,24},{48,0},{56,8},{64,11... | collective-permute-start | bytes 98312 | tf_op jit(solution)/shard_map/ppermute | solution.py:438
  107.9 4.0 %collective-permute-done.7 = f32[2,16,128]{2,1,0:T(8,128)S(1)} collective-permute-done((f32[2,16,128]{2,1,0:T(8,128)S(1)}, f32[2,16,128]{2,1,0:T(8,128)S(1)}, u32[]{:S(2)}, u32[]{:S(2)}) %collective-permute-start.7) | collective-permute-done | bytes 16416 | tf_op jit(solution)/shard_map/ppermute | solution.py:421
  111.9 0.0 collective-permute-done.8
  111.9 0.0 collective-permute-done.4
  111.9 1.8 %collective-permute-done.5 = f32[2,32,128]{2,1,0:T(8,128)S(1)} collective-permute-done((f32[2,32,128]{2,1,0:T(8,128)S(1)}, f32[2,32,128]{2,1,0:T(8,128)S(1)}, u32[]{:S(2)}, u32[]{:S(2)}) %collective-permute-start.5) | collective-permute-done | bytes 32800 | tf_op jit(solution)/shard_map/ppermute | solution.py:438
  113.8 0.8 collective-permute-done.6
  114.6 0.0 all-to-all-done.4
  114.6 0.9 broadcast_in_dim.10
  115.5 6.2 %all-to-all-start.5 = ((bf16[32,2,32,128]{3,2,1,0:T(8,128)(2,1)}), bf16[32,2,32,128]{3,2,1,0:T(8,128)(2,1)S(1)}, u32[]{:S(2)}, u32[]{:S(2)}) async-start(bf16[32,2,32,128]{3,2,1,0:T(8,128)(2,1)} %broadcast_in_dim.10), calls=%async_computation.5 | async-start | bytes 1048576 | tf_op jit(solution)/shard_map/all_to_all | solution.py:453
  121.8 8.6 %transport_two.1 = (f32[16,256,128]{2,1,0:T(8,128)}, f32[16,256,128]{2,1,0:T(8,128)}) custom-call(f32[256,16,128]{2,1,0:T(8,128)} %get-tuple-element.53.first.first_next, f32[256,16,128]{2,1,0:T(8,128)} %get-tuple-element.53.first.first_next, f32[256,16,128]{2,1,0:T(8,128)} %get-tuple-element.54.back.back_next, ...), custom_call_target="tpu_custom_call" | custom-call | flops 20971520 | bytes 12582912 | tf_op jit(solution)/shard_map/transport_two/pallas_call | solution.py:393
  130.4 0.8 all-to-all-done.5.sums
  131.2 1.2 weight_totals.1
  (11 shorter events, 0.1 us)
Async XLA Ops:
  3.0 9.7 %collective-permute-start = (f32[3,16,128]{2,1,0:T(8,128)S(1)}, f32[3,16,128]{2,1,0:T(8,128)S(1)}, u32[]{:S(2)}, u32[]{:S(2)}) collective-permute-start(f32[3,16,128]{2,1,0:T(8,128)S(1)} %get-tuple-element.81), channel_id=1, source_target_pairs={{0,248},{8,16},{16,8},{24,32},{32,24},{40,48},{48,40},{56,64},{64,... | collective-permute-start | bytes 73736 | tf_op jit(solution)/shard_map/ppermute | solution.py:421
  11.2 1.5 %collective-permute-start.1 = (f32[3,16,128]{2,1,0:T(8,128)S(1)}, f32[3,16,128]{2,1,0:T(8,128)S(1)}, u32[]{:S(2)}, u32[]{:S(2)}) collective-permute-start(f32[3,16,128]{2,1,0:T(8,128)S(1)} %get-tuple-element.80), channel_id=1, source_target_pairs={{0,8},{8,0},{16,24},{24,16},{32,40},{40,32},{48,56},{56,48},{64,72... | collective-permute-start | bytes 73736 | tf_op jit(solution)/shard_map/ppermute | solution.py:438
  18.8 18.9 %all-to-all-start = ((bf16[8,16,2,16,128]{4,3,2,1,0:T(8,128)(2,1)}), bf16[8,16,2,16,128]{4,3,2,1,0:T(8,128)(2,1)S(1)}, u32[]{:S(2)}, u32[]{:S(2)}) async-start(bf16[8,16,2,16,128]{4,3,2,1,0:T(8,128)(2,1)} %bitcast.30), calls=%async_computation | async-start | bytes 2097152 | tf_op jit(solution)/shard_map/all_to_all | solution.py:434
  30.0 12.4 %copy-start = (bf16[128,1024]{1,0:T(8,128)(2,1)S(1)}, bf16[128,1024]{1,0:T(8,128)(2,1)}, u32[]{:S(2)}) copy-start(bf16[128,1024]{1,0:T(8,128)(2,1)} %w_in.3) | copy-start | bytes 786436
  30.0 13.3 %copy-start.1 = (bf16[128,1024]{1,0:T(8,128)(2,1)S(1)}, bf16[128,1024]{1,0:T(8,128)(2,1)}, u32[]{:S(2)}) copy-start(bf16[128,1024]{1,0:T(8,128)(2,1)} %w_out.3) | copy-start | bytes 786436
  37.7 18.6 %all-to-all-start.1 = ((bf16[8,16,2,16,128]{4,3,2,1,0:T(8,128)(2,1)}), bf16[8,16,2,16,128]{4,3,2,1,0:T(8,128)(2,1)S(1)}, u32[]{:S(2)}, u32[]{:S(2)}) async-start(bf16[8,16,2,16,128]{4,3,2,1,0:T(8,128)(2,1)} %bitcast.29), calls=%async_computation.1 | async-start | bytes 2097152 | tf_op jit(solution)/shard_map/all_to_all | solution.py:434
  56.3 18.6 %all-to-all-start.2 = ((bf16[8,16,2,16,128]{4,3,2,1,0:T(8,128)(2,1)}), bf16[8,16,2,16,128]{4,3,2,1,0:T(8,128)(2,1)S(1)}, u32[]{:S(2)}, u32[]{:S(2)}) async-start(bf16[8,16,2,16,128]{4,3,2,1,0:T(8,128)(2,1)} %get-tuple-element.50), calls=%async_computation.2 | async-start | bytes 2097152 | tf_op jit(solution)/shard_map/all_to_all | solution.py:434
  71.4 2.0 %collective-permute-start.2 = (f32[1024,128]{1,0:T(8,128)S(1)}, f32[1024,128]{1,0:T(8,128)S(1)}, u32[]{:S(2)}, u32[]{:S(2)}) collective-permute-start(f32[1024,128]{1,0:T(8,128)S(1)} %dynamic-slice_bitcast_fusion), channel_id=1, source_target_pairs={{0,8},{8,0},{16,24},{24,16},{32,40},{40,32},{48,56},{56,48},{64,72... | collective-permute-start | bytes 1572872 | tf_op jit(solution)/shard_map/ppermute | solution.py:438
  74.9 16.7 %all-to-all-start.3 = ((f32[32,32,128]{2,1,0:T(8,128)}), f32[32,32,128]{2,1,0:T(8,128)S(1)}, u32[]{:S(2)}, u32[]{:S(2)}) async-start(f32[32,32,128]{2,1,0:T(8,128)} %bitcast.6), calls=%async_computation.3 | async-start | bytes 1048576 | tf_op jit(solution)/shard_map/all_to_all | solution.py:453
  91.6 23.0 %all-to-all-start.4 = ((bf16[8,16,2,16,128]{4,3,2,1,0:T(8,128)(2,1)}), bf16[8,16,2,16,128]{4,3,2,1,0:T(8,128)(2,1)S(1)}, u32[]{:S(2)}, u32[]{:S(2)}) async-start(bf16[8,16,2,16,128]{4,3,2,1,0:T(8,128)(2,1)} %get-tuple-element.57), calls=%async_computation.4 | async-start | bytes 2097152 | tf_op jit(solution)/shard_map/all_to_all | solution.py:434
  95.9 5.4 %collective-permute-start.3 = (f32[32,128]{1,0:T(8,128)S(1)}, f32[32,128]{1,0:T(8,128)S(1)}, u32[]{:S(2)}, u32[]{:S(2)}) collective-permute-start(f32[32,128]{1,0:T(8,128)S(1)} %reduce_sum.9), channel_id=1, source_target_pairs={{0,8},{8,0},{16,24},{24,16},{32,40},{40,32},{48,56},{56,48},{64,72... | collective-permute-start | bytes 49160 | tf_op jit(solution)/shard_map/ppermute | solution.py:438
  95.9 16.0 %collective-permute-start.7 = (f32[2,16,128]{2,1,0:T(8,128)S(1)}, f32[2,16,128]{2,1,0:T(8,128)S(1)}, u32[]{:S(2)}, u32[]{:S(2)}) collective-permute-start(f32[2,16,128]{2,1,0:T(8,128)S(1)} %get-tuple-element.85), channel_id=1, source_target_pairs={{0,248},{8,16},{16,8},{24,32},{32,24},{40,48},{48,40},{56,64},{64,... | collective-permute-start | bytes 49160 | tf_op jit(solution)/shard_map/ppermute | solution.py:421
  101.3 10.6 %collective-permute-start.8 = (f32[2,16,128]{2,1,0:T(8,128)S(1)}, f32[2,16,128]{2,1,0:T(8,128)S(1)}, u32[]{:S(2)}, u32[]{:S(2)}) collective-permute-start(f32[2,16,128]{2,1,0:T(8,128)S(1)} %get-tuple-element.84), channel_id=1, source_target_pairs={{0,8},{8,0},{16,24},{24,16},{32,40},{40,32},{48,56},{56,48},{64,72... | collective-permute-start | bytes 49160 | tf_op jit(solution)/shard_map/ppermute | solution.py:438
  101.3 10.6 %collective-permute-start.4 = (f32[2,32,128]{2,1,0:T(8,128)S(1)}, f32[2,32,128]{2,1,0:T(8,128)S(1)}, u32[]{:S(2)}, u32[]{:S(2)}) collective-permute-start(f32[2,32,128]{2,1,0:T(8,128)S(1)} %pad_maximum_fusion), channel_id=1, source_target_pairs={{0,16},{8,24},{16,0},{24,8},{32,48},{40,56},{48,32},{56,40},{64,80... | collective-permute-start | bytes 98312 | tf_op jit(solution)/shard_map/ppermute | solution.py:438
  101.4 12.4 %collective-permute-start.5 = (f32[2,32,128]{2,1,0:T(8,128)S(1)}, f32[2,32,128]{2,1,0:T(8,128)S(1)}, u32[]{:S(2)}, u32[]{:S(2)}) collective-permute-start(f32[2,32,128]{2,1,0:T(8,128)S(1)} %pad_maximum_fusion), channel_id=1, source_target_pairs={{0,32},{8,40},{16,48},{24,56},{32,0},{40,8},{48,16},{56,24},{64,96... | collective-permute-start | bytes 98312 | tf_op jit(solution)/shard_map/ppermute | solution.py:438
  104.1 10.5 %collective-permute-start.6 = (f32[2,32,128]{2,1,0:T(8,128)S(1)}, f32[2,32,128]{2,1,0:T(8,128)S(1)}, u32[]{:S(2)}, u32[]{:S(2)}) collective-permute-start(f32[2,32,128]{2,1,0:T(8,128)S(1)} %pad_maximum_fusion), channel_id=1, source_target_pairs={{0,48},{8,56},{16,32},{24,40},{32,16},{40,24},{48,0},{56,8},{64,11... | collective-permute-start | bytes 98312 | tf_op jit(solution)/shard_map/ppermute | solution.py:438
  115.5 15.6 %all-to-all-start.5 = ((bf16[32,2,32,128]{3,2,1,0:T(8,128)(2,1)}), bf16[32,2,32,128]{3,2,1,0:T(8,128)(2,1)S(1)}, u32[]{:S(2)}, u32[]{:S(2)}) async-start(bf16[32,2,32,128]{3,2,1,0:T(8,128)(2,1)} %broadcast_in_dim.10), calls=%async_computation.5 | async-start | bytes 1048576 | tf_op jit(solution)/shard_map/all_to_all | solution.py:453

commit v6 on v5

--- a/solution.py
+++ b/solution.py
@@ -181,16 +181,16 @@
     )
 
 
-def edge_kernel(state_lo, state_hi, cot_lo, cot_hi, east_hi, low, high):
-    low[0] = state_hi[:, 7, :]
-    low[1] = cot_hi[:, 7, :]
-    low[2] = east_hi[...].astype(F32)[:, 15, :]
-    high[0] = state_lo[:, 0, :]
-    high[1] = cot_lo[:, 0, :]
-    high[2] = cot_lo[:, 0, :]
-
-
-def edge_rows(state, east, cot):
+def edge_kernel(core, state_lo, state_hi, cot_lo, cot_hi, east_hi, by_chip, by_link):
+    even = core[0] == 0
+    last = (state_hi[:, 7, :], cot_hi[:, 7, :], east_hi[...].astype(F32)[:, 15, :])
+    first = (state_lo[:, 0, :], cot_lo[:, 0, :], cot_lo[:, 0, :])
+    for k in range(3):
+        by_chip[k] = jnp.where(even, last[k], first[k])
+        by_link[k] = jnp.where(even, first[k], last[k])
+
+
+def edge_rows(core, state, east, cot):
     width = state.shape[1]
     head = pl.BlockSpec((16, 8, 128), lambda s: (0, 0, 0))
     tail = pl.BlockSpec((16, 8, 128), lambda s: (0, width // 8 - 1, 0))
@@ -198,7 +198,7 @@
     return pl.pallas_call(
         edge_kernel,
         grid=(1,),
-        in_specs=[head, tail, head, tail, tail16],
+        in_specs=[pl.BlockSpec(memory_space=pltpu.SMEM), head, tail, head, tail, tail16],
         out_specs=[
             pl.BlockSpec((3, 16, 128), lambda s: (0, 0, 0)),
             pl.BlockSpec((3, 16, 128), lambda s: (0, 0, 0)),
@@ -208,7 +208,7 @@
             jax.ShapeDtypeStruct((3, 16, 128), F32),
         ],
         name="edge_rows",
-    )(*[in_hbm(x) for x in (state, state, cot, cot, east)])
+    )(core, *[in_hbm(x) for x in (state, state, cot, cot, east)])
 
 
 CELLS = 8
@@ -423,10 +423,10 @@
     )
 
 
-def halo(core, last, first):
+def halo(core, to_chip, to_link):
     even = core == 0
-    by_link = across(jnp.where(even, first, last))
-    by_chip = partner(jnp.where(even, last, first), 1)
+    by_link = across(to_link)
+    by_chip = partner(to_chip, 1)
     return jnp.where(even, by_link, by_chip), jnp.where(even, by_chip, by_link)
 
 
@@ -465,10 +465,10 @@
     blocks = width // ROWS
     hidden = w_in.shape[1]
     barrier = lax.optimization_barrier
-    low, high = edge_rows(state_in, east_speed, cotangent)
-    low, high, state_in = barrier((low, high, state_in))
     core = lax.rem(lax.axis_index("tile"), 2)
-    low, high = halo(core, low, high)
+    to_chip, to_link = edge_rows(core.reshape(1), state_in, east_speed, cotangent)
+    to_chip, to_link, state_in = barrier((to_chip, to_link, state_in))
+    low, high = halo(core, to_chip, to_link)
     w_in_t, w_out_t = w_in.T, w_out.T
     none = jnp.zeros((3, 16, 128), F32)
     half = blocks // 2
@@ -498,7 +498,9 @@
     part, inner, tail, head = barrier((part, inner, edge(width - 1), edge(0)))
     inner = exchange(inner).reshape(width // 2, 2, 16, 128)
     part = z_sum(jnp.stack([part, partner(part, 1)])).astype(BF16)
-    low_next, high_next = halo(core, tail, head)
+    low_next, high_next = halo(
+        core, jnp.where(core == 0, tail, head), jnp.where(core == 0, head, tail)
+    )
     low_next = jnp.concatenate([low_next, low[2:]])
     part, inner, low_next, high_next = barrier((part, inner, low_next, high_next))
     part = exchange_rows(jnp.broadcast_to(part[None], (32,) + part.shape))

time: 134 us -> 133 us (level)
  transfers between devices with their start and end apart: 15 -> 15, of which waited for: 10 -> 10; matrix products, arithmetic and copies ran while one was open for 3% -> 3% of each run, Pallas kernels for 26% -> 27%
where the time goes in v6:
time: 133 us; the launch traced here: 132 us
  starting transfers between devices  51.2 us (38%)
  Pallas kernels  43.7 us (33%)
  waiting for transfers between devices  31.7 us (24%)
  local copies, waits for them, and re-layouts  3.4 us (3%)
    pallas_call x2, Pallas kernels, network(): pl.pallas_call(functools.partial(network_kernel), grid=(rows // CELLS,),...  20.3 us
    all_to_all x4, starting transfers between devices, exchange(): return lax.all_to_all(block, 'lev', split_axis=0, concat_axis=0, tiled=True)  19.2 us
    ppermute x2, starting transfers between devices, across(): lax.ppermute(block, 'tile', [(i, (i + 1 if i % 2 else i - 1) % count) for...  13.5 us
    pallas_call x2, Pallas kernels, first_step(): pl.pallas_call(functools.partial(first_kernel, start, blocks), grid=(coun...  12 us
    all_to_all x2, starting transfers between devices, exchange_rows(): lax.all_to_all(block, ('tile', 'lev'), split_axis=0, concat_axis=0, tiled...  11.8 us
    all_to_all x2, waiting for transfers between devices, exchange_rows(): lax.all_to_all(block, ('tile', 'lev'), split_axis=0, concat_axis=0, tiled...  11.1 us
    all_to_all x4, waiting for transfers between devices, exchange(): return lax.all_to_all(block, 'lev', split_axis=0, concat_axis=0, tiled=True)  10.2 us
    pallas_call x1, Pallas kernels, last_step(): pl.pallas_call(functools.partial(last_kernel, start, blocks), grid=(count...  8.65 us
  transfers between devices with their start and end apart: 15, of which 10 were waited for; matrix products, arithmetic and copies ran while one was open for 3% of the time, Pallas kernels for 27%

profile of v6, /device:TPU:2, one launch (start us, length us, event | category | flops | bytes accessed | tf_op | source)
XLA Modules:
  0.0 131.8 jit_solution(1745570272185023314)
XLA Ops:
  0.6 1.6 %edge_rows.1 = (f32[3,16,128]{2,1,0:T(8,128)}, f32[3,16,128]{2,1,0:T(8,128)}) custom-call(s32[1]{0:T(128)} %bitcast.core, f32[16,256,128]{2,1,0:T(8,128)} %state_next.1, f32[16,256,128]{2,1,0:T(8,128)} %state_next.1, f32[16,256,128]{2,1,0:T(8,128)} %cot_next.3, f32[16,256,128]{2,1,0:T(8,128)} %cot_next.3, bf16[16,256,128]{2,1,0:T(8,128)(2,1)} %east_prev.3), custom_call_target="tpu_custom_call" | custom-call | tf_op jit(solution)/shard_map/edge_rows/pallas_call | solution.py:198
  2.3 8.2 %collective-permute-start = (f32[3,16,128]{2,1,0:T(8,128)}, f32[3,16,128]{2,1,0:T(8,128)S(1)}, u32[]{:S(2)}, u32[]{:S(2)}) collective-permute-start(f32[3,16,128]{2,1,0:T(8,128)} %get-tuple-element.41), channel_id=1, source_target_pairs={{0,248},{8,16},{16,8},{24,32},{32,24},{40,48},{48,40},{56,64},{64,... | collective-permute-start | bytes 73736 | tf_op jit(solution)/shard_map/ppermute | solution.py:421
  10.5 0.0 collective-permute-start.1
  10.5 1.7 %collective-permute-done = f32[3,16,128]{2,1,0:T(8,128)S(1)} collective-permute-done((f32[3,16,128]{2,1,0:T(8,128)}, f32[3,16,128]{2,1,0:T(8,128)S(1)}, u32[]{:S(2)}, u32[]{:S(2)}) %collective-permute-start) | collective-permute-done | bytes 24608 | tf_op jit(solution)/shard_map/ppermute | solution.py:421
  12.2 0.0 collective-permute-done.1
  12.2 6.0 %transport_one.2 = (f32[256,16,128]{2,1,0:T(8,128)}, f32[256,16,128]{2,1,0:T(8,128)}, bf16[256,2,16,128]{3,2,1,0:T(8,128)(2,1)}, bf16[128,2,16,128]{3,2,1,0:T(8,128)(2,1)}) custom-call(f32[16,256,128]{2,1,0:T(8,128)} %state_next.1, f32[16,256,128]{2,1,0:T(8,128)} %state_next.1, f32[16,256,128]{2,1,0:T(8,128)} %state_next.1, f32[16,256,128]{2,1,0:T(8,128)} %cot_next.3, ...), custom_call_target="tpu_custom_call" | custom-call | flops 10485760 | bytes 7340032 | tf_op jit(solution)/shard_map/transport_one/pallas_call | solution.py:147
  18.2 5.3 %all-to-all-start = ((bf16[8,16,2,16,128]{4,3,2,1,0:T(8,128)(2,1)}), bf16[8,16,2,16,128]{4,3,2,1,0:T(8,128)(2,1)S(1)}, u32[]{:S(2)}, u32[]{:S(2)}) async-start(bf16[8,16,2,16,128]{4,3,2,1,0:T(8,128)(2,1)} %bitcast.30), calls=%async_computation | async-start | bytes 2097152 | tf_op jit(solution)/shard_map/all_to_all | solution.py:434
  23.5 6.0 %transport_one.3 = (f32[256,16,128]{2,1,0:T(8,128)}, f32[256,16,128]{2,1,0:T(8,128)}, bf16[256,2,16,128]{3,2,1,0:T(8,128)(2,1)}, bf16[128,2,16,128]{3,2,1,0:T(8,128)(2,1)}) custom-call(f32[16,256,128]{2,1,0:T(8,128)} %state_next.1, f32[16,256,128]{2,1,0:T(8,128)} %state_next.1, ...), custom_call_target="tpu_custom_call", output_to_operand_aliasing={{0}: (11, {}), {1}: (12, {}), {2}: (13, {})} | custom-call | flops 10485760 | bytes 7340032 | tf_op jit(solution)/shard_map/transport_one/pallas_call | solution.py:147
  29.5 0.0 copy-start
  29.5 0.0 copy-start.1
  29.5 7.6 %all-to-all-done.cols = bf16[8,16,2,16,128]{4,3,2,1,0:T(8,128)(2,1)S(1)} async-done(((bf16[8,16,2,16,128]{4,3,2,1,0:T(8,128)(2,1)}), bf16[8,16,2,16,128]{4,3,2,1,0:T(8,128)(2,1)S(1)}, u32[]{:S(2)}, u32[]{:S(2)}) %all-to-all-start) | async-done | bytes 1048608 | tf_op jit(solution)/shard_map/all_to_all | solution.py:434
  37.1 4.8 %all-to-all-start.1 = ((bf16[8,16,2,16,128]{4,3,2,1,0:T(8,128)(2,1)}), bf16[8,16,2,16,128]{4,3,2,1,0:T(8,128)(2,1)S(1)}, u32[]{:S(2)}, u32[]{:S(2)}) async-start(bf16[8,16,2,16,128]{4,3,2,1,0:T(8,128)(2,1)} %bitcast.29), calls=%async_computation.1 | async-start | bytes 2097152 | tf_op jit(solution)/shard_map/all_to_all | solution.py:434
  41.9 0.0 copy-done
  41.9 0.8 copy.13
  42.8 0.0 copy-done.1
  42.8 0.8 copy.14
  43.6 10.2 %column_network.2 = (bf16[8,16,2,16,128]{4,3,2,1,0:T(8,128)(2,1)}, f32[2,1024,128]{2,1,0:T(8,128)S(1)}) custom-call(bf16[8,16,2,16,128]{4,3,2,1,0:T(8,128)(2,1)S(1)} %all-to-all-done.cols, bf16[1024,128]{1,0:T(8,128)(2,1)} %bitcast.31, bf16[1024,128]{1,0:T(8,128)(2,1)} %bitcast.33, bf16[128,1024]{1,0:T(8,128)(2,1)} %w_in.3, bf16[128,1024]{1,0:T(8,128)(2,1)} %w_out.3), custom_call_target="tpu_custom_call" | custom-call | flops 3221225472 | bytes 2097152 | tf_op jit(solution)/shard_map/column_network/pallas_call | solution.py:260
  53.8 2.0 %all-to-all-done.1.cols = bf16[8,16,2,16,128]{4,3,2,1,0:T(8,128)(2,1)S(1)} async-done(((bf16[8,16,2,16,128]{4,3,2,1,0:T(8,128)(2,1)}), bf16[8,16,2,16,128]{4,3,2,1,0:T(8,128)(2,1)S(1)}, u32[]{:S(2)}, u32[]{:S(2)}) %all-to-all-start.1) | async-done | bytes 1048608 | tf_op jit(solution)/shard_map/all_to_all | solution.py:434
  55.7 4.8 %all-to-all-start.2 = ((bf16[8,16,2,16,128]{4,3,2,1,0:T(8,128)(2,1)}), bf16[8,16,2,16,128]{4,3,2,1,0:T(8,128)(2,1)S(1)}, u32[]{:S(2)}, u32[]{:S(2)}) async-start(bf16[8,16,2,16,128]{4,3,2,1,0:T(8,128)(2,1)} %get-tuple-element.50), calls=%async_computation.2 | async-start | bytes 2097152 | tf_op jit(solution)/shard_map/all_to_all | solution.py:434
  60.5 10.1 %column_network.3 = (bf16[8,16,2,16,128]{4,3,2,1,0:T(8,128)(2,1)}, f32[2,1024,128]{2,1,0:T(8,128)S(1)}) custom-call(bf16[8,16,2,16,128]{4,3,2,1,0:T(8,128)(2,1)S(1)} %all-to-all-done.1.cols, bf16[1024,128]{1,0:T(8,128)(2,1)} %bitcast.32, bf16[1024,128]{1,0:T(8,128)(2,1)} %bitcast.34, bf16[128,1024]{1,0:T(8,128)(2,1)} %w_in.3, bf16[128,1024]{1,0:T(8,128)(2,1)} %w_out.3), custom_call_target="tpu_custom_call" | custom-call | flops 3221225472 | bytes 2097152 | tf_op jit(solution)/shard_map/column_network/pallas_call | solution.py:260
  70.7 0.1 add.29
  70.8 0.1 collective-permute-start.2
  70.9 1.9 %collective-permute-done.2 = f32[1024,128]{1,0:T(8,128)S(1)} collective-permute-done((f32[1024,128]{1,0:T(8,128)S(1)}, f32[1024,128]{1,0:T(8,128)S(1)}, u32[]{:S(2)}, u32[]{:S(2)}) %collective-permute-start.2) | collective-permute-done | bytes 524320 | tf_op jit(solution)/shard_map/ppermute | solution.py:438
  72.8 0.8 bitcast_add_fusion
  73.7 0.7 all-to-all-done.2
  74.4 5.5 %all-to-all-start.3 = ((f32[32,32,128]{2,1,0:T(8,128)}), f32[32,32,128]{2,1,0:T(8,128)S(1)}, u32[]{:S(2)}, u32[]{:S(2)}) async-start(f32[32,32,128]{2,1,0:T(8,128)} %bitcast.7), calls=%async_computation.3 | async-start | bytes 1048576 | tf_op jit(solution)/shard_map/all_to_all | solution.py:453
  79.9 0.8 fusion
  80.7 10.3 %all-to-all-done.3 = f32[32,32,128]{2,1,0:T(8,128)S(1)} async-done(((f32[32,32,128]{2,1,0:T(8,128)}), f32[32,32,128]{2,1,0:T(8,128)S(1)}, u32[]{:S(2)}, u32[]{:S(2)}) %all-to-all-start.3) | async-done | bytes 524320 | tf_op jit(solution)/shard_map/all_to_all | solution.py:453
  91.1 4.3 %all-to-all-start.4 = ((bf16[8,16,2,16,128]{4,3,2,1,0:T(8,128)(2,1)}), bf16[8,16,2,16,128]{4,3,2,1,0:T(8,128)(2,1)S(1)}, u32[]{:S(2)}, u32[]{:S(2)}) async-start(bf16[8,16,2,16,128]{4,3,2,1,0:T(8,128)(2,1)} %get-tuple-element.57), calls=%async_computation.4 | async-start | bytes 2097152 | tf_op jit(solution)/shard_map/all_to_all | solution.py:434
  95.4 0.0 collective-permute-start.3
  95.4 5.3 %collective-permute-start.7 = (f32[2,16,128]{2,1,0:T(8,128)S(1)}, f32[2,16,128]{2,1,0:T(8,128)S(1)}, u32[]{:S(2)}, u32[]{:S(2)}) collective-permute-start(f32[2,16,128]{2,1,0:T(8,128)S(1)} %get-tuple-element.83), channel_id=1, source_target_pairs={{0,248},{8,16},{16,8},{24,32},{32,24},{40,48},{48,40},{56,64},{64,... | collective-permute-start | bytes 49160 | tf_op jit(solution)/shard_map/ppermute | solution.py:421
  100.8 0.0 collective-permute-start.8
  100.8 0.0 collective-permute-done.3
  100.8 0.1 collective-permute-start.4
  100.9 2.7 %collective-permute-start.5 = (f32[2,32,128]{2,1,0:T(8,128)S(1)}, f32[2,32,128]{2,1,0:T(8,128)S(1)}, u32[]{:S(2)}, u32[]{:S(2)}) collective-permute-start(f32[2,32,128]{2,1,0:T(8,128)S(1)} %pad_maximum_fusion), channel_id=1, source_target_pairs={{0,32},{8,40},{16,48},{24,56},{32,0},{40,8},{48,16},{56,24},{64,96... | collective-permute-start | bytes 98312 | tf_op jit(solution)/shard_map/ppermute | solution.py:438
  103.6 3.7 %collective-permute-start.6 = (f32[2,32,128]{2,1,0:T(8,128)S(1)}, f32[2,32,128]{2,1,0:T(8,128)S(1)}, u32[]{:S(2)}, u32[]{:S(2)}) collective-permute-start(f32[2,32,128]{2,1,0:T(8,128)S(1)} %pad_maximum_fusion), channel_id=1, source_target_pairs={{0,48},{8,56},{16,32},{24,40},{32,16},{40,24},{48,0},{56,8},{64,11... | collective-permute-start | bytes 98312 | tf_op jit(solution)/shard_map/ppermute | solution.py:438
  107.3 4.0 %collective-permute-done.7 = f32[2,16,128]{2,1,0:T(8,128)S(1)} collective-permute-done((f32[2,16,128]{2,1,0:T(8,128)S(1)}, f32[2,16,128]{2,1,0:T(8,128)S(1)}, u32[]{:S(2)}, u32[]{:S(2)}) %collective-permute-start.7) | collective-permute-done | bytes 16416 | tf_op jit(solution)/shard_map/ppermute | solution.py:421
  111.4 0.0 collective-permute-done.8
  111.4 0.0 collective-permute-done.4
  111.4 1.8 %collective-permute-done.5 = f32[2,32,128]{2,1,0:T(8,128)S(1)} collective-permute-done((f32[2,32,128]{2,1,0:T(8,128)S(1)}, f32[2,32,128]{2,1,0:T(8,128)S(1)}, u32[]{:S(2)}, u32[]{:S(2)}) %collective-permute-start.5) | collective-permute-done | bytes 32800 | tf_op jit(solution)/shard_map/ppermute | solution.py:438
  113.3 0.8 collective-permute-done.6
  114.1 0.0 all-to-all-done.4
  114.1 0.9 broadcast_in_dim.10
  115.0 6.2 %all-to-all-start.5 = ((bf16[32,2,32,128]{3,2,1,0:T(8,128)(2,1)}), bf16[32,2,32,128]{3,2,1,0:T(8,128)(2,1)S(1)}, u32[]{:S(2)}, u32[]{:S(2)}) async-start(bf16[32,2,32,128]{3,2,1,0:T(8,128)(2,1)} %broadcast_in_dim.10), calls=%async_computation.5 | async-start | bytes 1048576 | tf_op jit(solution)/shard_map/all_to_all | solution.py:453
  121.2 8.6 %transport_two.1 = (f32[16,256,128]{2,1,0:T(8,128)}, f32[16,256,128]{2,1,0:T(8,128)}) custom-call(f32[256,16,128]{2,1,0:T(8,128)} %get-tuple-element.53.first.first_next, f32[256,16,128]{2,1,0:T(8,128)} %get-tuple-element.53.first.first_next, f32[256,16,128]{2,1,0:T(8,128)} %get-tuple-element.54.back.back_next, ...), custom_call_target="tpu_custom_call" | custom-call | flops 20971520 | bytes 12582912 | tf_op jit(solution)/shard_map/transport_two/pallas_call | solution.py:393
  129.9 0.8 all-to-all-done.5.sums
  130.7 1.2 weight_totals.1
  (11 shorter events, 0.1 us)
Async XLA Ops:
  2.3 9.9 %collective-permute-start = (f32[3,16,128]{2,1,0:T(8,128)}, f32[3,16,128]{2,1,0:T(8,128)S(1)}, u32[]{:S(2)}, u32[]{:S(2)}) collective-permute-start(f32[3,16,128]{2,1,0:T(8,128)} %get-tuple-element.41), channel_id=1, source_target_pairs={{0,248},{8,16},{16,8},{24,32},{32,24},{40,48},{48,40},{56,64},{64,... | collective-permute-start | bytes 73736 | tf_op jit(solution)/shard_map/ppermute | solution.py:421
  10.5 1.7 %collective-permute-start.1 = (f32[3,16,128]{2,1,0:T(8,128)}, f32[3,16,128]{2,1,0:T(8,128)S(1)}, u32[]{:S(2)}, u32[]{:S(2)}) collective-permute-start(f32[3,16,128]{2,1,0:T(8,128)} %get-tuple-element.42), channel_id=1, source_target_pairs={{0,8},{8,0},{16,24},{24,16},{32,40},{40,32},{48,56},{56,48},{64,72... | collective-permute-start | bytes 73736 | tf_op jit(solution)/shard_map/ppermute | solution.py:438
  18.2 18.9 %all-to-all-start = ((bf16[8,16,2,16,128]{4,3,2,1,0:T(8,128)(2,1)}), bf16[8,16,2,16,128]{4,3,2,1,0:T(8,128)(2,1)S(1)}, u32[]{:S(2)}, u32[]{:S(2)}) async-start(bf16[8,16,2,16,128]{4,3,2,1,0:T(8,128)(2,1)} %bitcast.30), calls=%async_computation | async-start | bytes 2097152 | tf_op jit(solution)/shard_map/all_to_all | solution.py:434
  29.5 12.4 %copy-start = (bf16[128,1024]{1,0:T(8,128)(2,1)S(1)}, bf16[128,1024]{1,0:T(8,128)(2,1)}, u32[]{:S(2)}) copy-start(bf16[128,1024]{1,0:T(8,128)(2,1)} %w_in.3) | copy-start | bytes 786436
  29.5 13.3 %copy-start.1 = (bf16[128,1024]{1,0:T(8,128)(2,1)S(1)}, bf16[128,1024]{1,0:T(8,128)(2,1)}, u32[]{:S(2)}) copy-start(bf16[128,1024]{1,0:T(8,128)(2,1)} %w_out.3) | copy-start | bytes 786436
  37.1 18.6 %all-to-all-start.1 = ((bf16[8,16,2,16,128]{4,3,2,1,0:T(8,128)(2,1)}), bf16[8,16,2,16,128]{4,3,2,1,0:T(8,128)(2,1)S(1)}, u32[]{:S(2)}, u32[]{:S(2)}) async-start(bf16[8,16,2,16,128]{4,3,2,1,0:T(8,128)(2,1)} %bitcast.29), calls=%async_computation.1 | async-start | bytes 2097152 | tf_op jit(solution)/shard_map/all_to_all | solution.py:434
  55.7 18.6 %all-to-all-start.2 = ((bf16[8,16,2,16,128]{4,3,2,1,0:T(8,128)(2,1)}), bf16[8,16,2,16,128]{4,3,2,1,0:T(8,128)(2,1)S(1)}, u32[]{:S(2)}, u32[]{:S(2)}) async-start(bf16[8,16,2,16,128]{4,3,2,1,0:T(8,128)(2,1)} %get-tuple-element.50), calls=%async_computation.2 | async-start | bytes 2097152 | tf_op jit(solution)/shard_map/all_to_all | solution.py:434
  70.8 2.0 %collective-permute-start.2 = (f32[1024,128]{1,0:T(8,128)S(1)}, f32[1024,128]{1,0:T(8,128)S(1)}, u32[]{:S(2)}, u32[]{:S(2)}) collective-permute-start(f32[1024,128]{1,0:T(8,128)S(1)} %dynamic-slice_bitcast_fusion), channel_id=1, source_target_pairs={{0,8},{8,0},{16,24},{24,16},{32,40},{40,32},{48,56},{56,48},{64,72... | collective-permute-start | bytes 1572872 | tf_op jit(solution)/shard_map/ppermute | solution.py:438
  74.4 16.7 %all-to-all-start.3 = ((f32[32,32,128]{2,1,0:T(8,128)}), f32[32,32,128]{2,1,0:T(8,128)S(1)}, u32[]{:S(2)}, u32[]{:S(2)}) async-start(f32[32,32,128]{2,1,0:T(8,128)} %bitcast.7), calls=%async_computation.3 | async-start | bytes 1048576 | tf_op jit(solution)/shard_map/all_to_all | solution.py:453
  91.1 23.0 %all-to-all-start.4 = ((bf16[8,16,2,16,128]{4,3,2,1,0:T(8,128)(2,1)}), bf16[8,16,2,16,128]{4,3,2,1,0:T(8,128)(2,1)S(1)}, u32[]{:S(2)}, u32[]{:S(2)}) async-start(bf16[8,16,2,16,128]{4,3,2,1,0:T(8,128)(2,1)} %get-tuple-element.57), calls=%async_computation.4 | async-start | bytes 2097152 | tf_op jit(solution)/shard_map/all_to_all | solution.py:434
  95.4 5.4 %collective-permute-start.3 = (f32[32,128]{1,0:T(8,128)S(1)}, f32[32,128]{1,0:T(8,128)S(1)}, u32[]{:S(2)}, u32[]{:S(2)}) collective-permute-start(f32[32,128]{1,0:T(8,128)S(1)} %reduce_sum.9), channel_id=1, source_target_pairs={{0,8},{8,0},{16,24},{24,16},{32,40},{40,32},{48,56},{56,48},{64,72... | collective-permute-start | bytes 49160 | tf_op jit(solution)/shard_map/ppermute | solution.py:438
  95.4 16.0 %collective-permute-start.7 = (f32[2,16,128]{2,1,0:T(8,128)S(1)}, f32[2,16,128]{2,1,0:T(8,128)S(1)}, u32[]{:S(2)}, u32[]{:S(2)}) collective-permute-start(f32[2,16,128]{2,1,0:T(8,128)S(1)} %get-tuple-element.83), channel_id=1, source_target_pairs={{0,248},{8,16},{16,8},{24,32},{32,24},{40,48},{48,40},{56,64},{64,... | collective-permute-start | bytes 49160 | tf_op jit(solution)/shard_map/ppermute | solution.py:421
  100.8 10.6 %collective-permute-start.8 = (f32[2,16,128]{2,1,0:T(8,128)S(1)}, f32[2,16,128]{2,1,0:T(8,128)S(1)}, u32[]{:S(2)}, u32[]{:S(2)}) collective-permute-start(f32[2,16,128]{2,1,0:T(8,128)S(1)} %get-tuple-element.82), channel_id=1, source_target_pairs={{0,8},{8,0},{16,24},{24,16},{32,40},{40,32},{48,56},{56,48},{64,72... | collective-permute-start | bytes 49160 | tf_op jit(solution)/shard_map/ppermute | solution.py:438
  100.8 10.6 %collective-permute-start.4 = (f32[2,32,128]{2,1,0:T(8,128)S(1)}, f32[2,32,128]{2,1,0:T(8,128)S(1)}, u32[]{:S(2)}, u32[]{:S(2)}) collective-permute-start(f32[2,32,128]{2,1,0:T(8,128)S(1)} %pad_maximum_fusion), channel_id=1, source_target_pairs={{0,16},{8,24},{16,0},{24,8},{32,48},{40,56},{48,32},{56,40},{64,80... | collective-permute-start | bytes 98312 | tf_op jit(solution)/shard_map/ppermute | solution.py:438
  100.9 12.4 %collective-permute-start.5 = (f32[2,32,128]{2,1,0:T(8,128)S(1)}, f32[2,32,128]{2,1,0:T(8,128)S(1)}, u32[]{:S(2)}, u32[]{:S(2)}) collective-permute-start(f32[2,32,128]{2,1,0:T(8,128)S(1)} %pad_maximum_fusion), channel_id=1, source_target_pairs={{0,32},{8,40},{16,48},{24,56},{32,0},{40,8},{48,16},{56,24},{64,96... | collective-permute-start | bytes 98312 | tf_op jit(solution)/shard_map/ppermute | solution.py:438
  103.6 10.5 %collective-permute-start.6 = (f32[2,32,128]{2,1,0:T(8,128)S(1)}, f32[2,32,128]{2,1,0:T(8,128)S(1)}, u32[]{:S(2)}, u32[]{:S(2)}) collective-permute-start(f32[2,32,128]{2,1,0:T(8,128)S(1)} %pad_maximum_fusion), channel_id=1, source_target_pairs={{0,48},{8,56},{16,32},{24,40},{32,16},{40,24},{48,0},{56,8},{64,11... | collective-permute-start | bytes 98312 | tf_op jit(solution)/shard_map/ppermute | solution.py:438
  115.0 15.6 %all-to-all-start.5 = ((bf16[32,2,32,128]{3,2,1,0:T(8,128)(2,1)}), bf16[32,2,32,128]{3,2,1,0:T(8,128)(2,1)S(1)}, u32[]{:S(2)}, u32[]{:S(2)}) async-start(bf16[32,2,32,128]{3,2,1,0:T(8,128)(2,1)} %broadcast_in_dim.10), calls=%async_computation.5 | async-start | bytes 1048576 | tf_op jit(solution)/shard_map/all_to_all | solution.py:453
